TPU v7x, 256 devices: a whole 4x4x8 slice. The times are simulated.
256 devices in a mesh: region: 4 (over z_lo), dev: 64 (over y, z_hi, x, core).
Axes of the slice: x: 4, y: 4, z: 8 (z_hi: 2, z_lo: 4; z = z_hi * 4 + z_lo), core: 2. Of those that a mesh axis runs over, the one named last changes fastest.
Arguments:
- disp_start: float32 [3, 5242880], P(None, ('region', 'dev')), may hold values from -6 to 6
- veloc_start: float32 [3, 5242880], P(None, ('region', 'dev')), may hold values from -6 to 6
- jacobian: float32 [3, 125, 81920], P(None, None, ('region', 'dev')), may hold values from 0.5 to 2
- lame_lambda: float32 [125, 81920], P(None, ('region', 'dev')), may hold values from 0.01 to 0.08
- lame_mu: float32 [125, 81920], P(None, ('region', 'dev')), may hold values from 0.01 to 0.08
- density: float32 [125, 81920], P(None, ('region', 'dev')), may hold values from 0.5 to 2
- connect: int32 [125, 81920], P(None, ('region', 'dev')), may hold values from 0 to 20479, as said below
- fine_slots: int32 [20480], P(('region', 'dev')), may hold values from 0 to 320, as said below
- peer_nodes: int32 [4, 655360], P(None, ('region', 'dev')), may hold values from 0 to 2559, as said below
Outputs:
- disp_final: float32 [3, 5242880], P(None, ('region', 'dev'))
- veloc_final: float32 [3, 5242880], P(None, ('region', 'dev'))
Inputs may be any that keep to these rules, and one draw needn't show every extreme that they name: `connect`: entry (k, e) is the device-local index of node k of that device's element e; it lies in the window 64 * e to 64 * e + 127 taken modulo 20480; an element's 125 nodes are distinct, and nodes 64 * e to 64 * e + 63 all belong to element e. `fine_slots`: each device's 80 slots first name distinct elements of that device and then hold 320; the two devices whose dev indices differ only in the lowest bit hold 80 fine elements together, and in every draw some device has all 80 slots filled. `peer_nodes`: each row of a device is a permutation of 0 to 2559 that moves an entry only within its aligned group of 128 slots; nodes below 10240 are shared with no other device.
All inputs are finite; a program needn't handle non-finite values.
Results may differ from a plain program's by a relative error of at most 0.0003.
Values sent between devices are 32-bit elements; how exact they have to be, the bound alone decides.
No kernel may reach another device: no remote copies, remote signals or barrier semaphores. Data moves between devices by JAX's collectives and lax.ppermute only.
A program may use at most 128 MiB of HBM per device.

v0:
```python
import math

import jax
import jax.numpy as jnp
import ml_dtypes
import numpy as np
from jax import lax
from jax.experimental import pallas as pl
from jax.experimental.pallas import tpu as pltpu
from jax.sharding import PartitionSpec as P

NODES = 125
ELEM = 320
NLOC = 20480
FCAP = 80
LANES = 128
ROWS = NLOC // LANES
FIRST = ROWS // 2
GROUPS = 20
SHARED = 4 * GROUPS
SUBSTEPS = 4
GLL_POINTS = (-1.0, -math.sqrt(3.0 / 7.0), 0.0, math.sqrt(3.0 / 7.0), 1.0)
TIME_STEP = 0.2
STEP = TIME_STEP / SUBSTEPS
PAD_ROWS = 168
PAD_ELEM = 384


def slope_rows():
    points = GLL_POINTS
    rows = []
    for row_at in range(5):
        entries = []
        for col_at in range(5):
            if row_at == col_at:
                summed = 0.0
                for other_at in range(5):
                    if other_at != row_at:
                        summed += 1.0 / (points[row_at] - points[other_at])
                entries.append(summed)
            else:
                top_prod = 1.0
                low_prod = 1.0
                for other_at in range(5):
                    if other_at != row_at:
                        top_prod *= points[row_at] - points[other_at]
                    if other_at != col_at:
                        low_prod *= points[col_at] - points[other_at]
                entries.append(top_prod / low_prod / (points[row_at] - points[col_at]))
        rows.append(entries)
    return rows


def slope_operands():
    slopes = np.array(slope_rows(), dtype=np.float32)
    eye = np.eye(5, dtype=np.float32)
    along = [
        np.kron(np.kron(slopes, eye), eye),
        np.kron(np.kron(eye, slopes), eye),
        np.kron(np.kron(eye, eye), slopes),
    ]
    grad = np.zeros((LANES, 3 * LANES), np.float32)
    back = np.zeros((3 * LANES, LANES), np.float32)
    for i, matrix in enumerate(along):
        grad[:NODES, i * LANES : i * LANES + NODES] = matrix.T
        back[i * LANES : i * LANES + NODES, :NODES] = matrix

    def terms(whole):
        high = whole.astype(ml_dtypes.bfloat16)
        low = (whole - high.astype(np.float32)).astype(ml_dtypes.bfloat16)
        return np.concatenate([high, high, low], axis=0)

    return terms(grad), terms(back)


def split_terms(whole):
    high = whole.astype(jnp.bfloat16)
    low = (whole - high.astype(jnp.float32)).astype(jnp.bfloat16)
    return high, low


def lane_pick(values, index):
    return jnp.take_along_axis(values, index, axis=1, mode="promise_in_bounds")


def forces(shifted, jac, lam, mu, grad, back):
    count = shifted[0].shape[0]
    high, low = split_terms(jnp.concatenate(shifted, axis=0))
    slope = jnp.dot(
        jnp.concatenate([high, low, high], axis=1), grad, preferred_element_type=jnp.float32
    )
    strain = [
        [
            jac[i] * slope[c * count : (c + 1) * count, i * LANES : (i + 1) * LANES]
            for i in range(3)
        ]
        for c in range(3)
    ]
    traced = lam * (strain[0][0] + strain[1][1] + strain[2][2])
    rows = []
    for c in range(3):
        fluxes = []
        for i in range(3):
            stress = mu * (strain[c][i] + strain[i][c])
            if c == i:
                stress = stress + traced
            fluxes.append(jac[i] * stress)
        rows.append(jnp.concatenate(fluxes, axis=1))
    high, low = split_terms(jnp.concatenate(rows, axis=0))
    out = jnp.dot(
        jnp.concatenate([high, low, high], axis=1), back, preferred_element_type=jnp.float32
    )
    return [out[c * count : (c + 1) * count] for c in range(3)]


def inverse_block(rows_ref, count, missing):
    target = lax.broadcasted_iota(jnp.int32, (LANES, LANES), 0)

    def step(k, found):
        row = rows_ref[pl.ds(k, 1), :]
        return jnp.where(row == target, k, found)

    return lax.fori_loop(
        0, count, step, jnp.full((LANES, LANES), missing, jnp.int32), unroll=4 if count % 4 == 0 else 5
    )


def high_half(shape):
    return lax.broadcasted_iota(jnp.int32, shape, 1) >= LANES // 2


def fine_local(disp_ref, slots_ref, window_ref, statics, spread, grad, back):
    jac0, jac1, jac2, lam, mu, index, place = statics
    upper = high_half((1, LANES))
    for s in range(FCAP):
        e = slots_ref[s]
        first = lax.shift_right_logical(e, 1)
        second = lax.shift_right_logical(e + 1, 1)
        for c in range(3):
            window_ref[c, pl.ds(s, 1), :] = jnp.where(
                upper, disp_ref[c, pl.ds(first, 1), :], disp_ref[c, pl.ds(second, 1), :]
            )
    shifted = [lane_pick(window_ref[c], index) for c in range(3)]
    out = forces(shifted, (jac0, jac1, jac2), lam, mu, grad, back)
    slotted = jnp.concatenate([lane_pick(o, place) for o in out], axis=1)
    upper = lax.broadcasted_iota(jnp.int32, slotted.shape, 1) % LANES >= LANES // 2
    blank = jnp.zeros((LANES - FCAP, slotted.shape[1]), jnp.float32)
    both = jnp.concatenate(
        [jnp.where(upper, slotted, 0.0), blank, jnp.where(upper, 0.0, slotted), blank], axis=0
    )
    high, low = split_terms(both)
    return jnp.dot(spread, high, preferred_element_type=jnp.float32) + jnp.dot(
        spread, low, preferred_element_type=jnp.float32
    )


def send_rows(shared, picks, parities, staged_ref, outs):
    dev_odd, region_odd = parities
    for c, values in enumerate(shared):
        staged_ref[c] = lane_pick(values, picks)
    for c in range(len(shared)):
        part = [staged_ref[c, GROUPS * p : GROUPS * (p + 1), :] for p in range(4)]
        put = pl.ds(c * GROUPS, GROUPS)
        outs[0][put, :] = jnp.where(dev_odd, part[0], part[1])
        outs[1][put, :] = jnp.where(dev_odd, part[1], part[0])
        outs[2][put, :] = jnp.where(region_odd, part[2], part[3])
        outs[3][put, :] = jnp.where(region_odd, part[3], part[2])


def received_rows(arrived, channels, places, parities, staged_ref):
    dev_odd, region_odd = parities
    for c in range(channels):
        got = [a[c * GROUPS : (c + 1) * GROUPS, :] for a in arrived]
        staged_ref[c, 0:GROUPS, :] = jnp.where(dev_odd, got[0], got[1])
        staged_ref[c, GROUPS : 2 * GROUPS, :] = jnp.where(dev_odd, got[1], got[0])
        staged_ref[c, 2 * GROUPS : 3 * GROUPS, :] = jnp.where(region_odd, got[2], got[3])
        staged_ref[c, 3 * GROUPS : 4 * GROUPS, :] = jnp.where(region_odd, got[3], got[2])
    return [lane_pick(staged_ref[c], places) for c in range(channels)]


def own_parities():
    return (
        jnp.bitwise_and(lax.axis_index("dev"), 1) == 1,
        jnp.bitwise_and(lax.axis_index("region"), 1) == 1,
    )


def first_kernel(
    slots_ref,
    slot_row_ref,
    disp_in,
    veloc_in,
    jac_ref,
    lam_ref,
    mu_ref,
    dens_ref,
    conn_ref,
    peer_ref,
    grad_ref,
    back_ref,
    disp_ref,
    veloc_ref,
    coarse_ref,
    summed_ref,
    fixed_ref,
    index_ref,
    spread_ref,
    peer_index_ref,
    sends0,
    sends1,
    sends2,
    sends3,
    turned_ref,
    turned_index_ref,
    pad_ref,
    conn_pad_ref,
    peer_rows_ref,
    peer_cols_ref,
    window_ref,
    staged_ref,
    total_ref,
    spread_wide_ref,
):
    grad, back = grad_ref[...], back_ref[...]
    parities = own_parities()
    for j in range(ROWS):
        cols = slice(j * LANES, (j + 1) * LANES)
        for c in range(3):
            disp_ref[c, j : j + 1, :] = disp_in[c : c + 1, cols]
            veloc_ref[c, j : j + 1, :] = veloc_in[c : c + 1, cols]
    for c in range(3):
        disp_ref[c, ROWS:PAD_ROWS, :] = jnp.broadcast_to(
            disp_in[c : c + 1, 0:LANES], (PAD_ROWS - ROWS, LANES)
        )
    for p in range(4):
        for j in range(GROUPS):
            at = p * GROUPS + j
            peer_rows_ref[at : at + 1, :] = peer_ref[
                p : p + 1, j * LANES : (j + 1) * LANES
            ] & (LANES - 1)
    peer_rows_ref[SHARED:, :] = jnp.zeros((LANES - SHARED, LANES), jnp.int32)
    pad_ref[...] = jnp.zeros_like(pad_ref)
    sources = [jac_ref.at[0], jac_ref.at[1], jac_ref.at[2], lam_ref, mu_ref, dens_ref]
    for a, source in enumerate(sources):
        pad_ref[0:NODES, 0:ELEM] = source[...]
        for b in range(3):
            block = slice(b * LANES, (b + 1) * LANES)
            turned_ref[a, block, :] = pad_ref[:, block].T
    conn_pad_ref[...] = jnp.zeros_like(conn_pad_ref)
    for b in range(3):
        block = slice(b * LANES, (b + 1) * LANES)
        width = min(LANES, ELEM - b * LANES)
        conn_pad_ref[b, 0:NODES, 0:width] = conn_ref[
            :, b * LANES : b * LANES + width
        ] & (LANES - 1)
        turned_index_ref[0, block, :] = conn_pad_ref[b].T
        turned_index_ref[1, block, :] = inverse_block(
            conn_pad_ref.at[b], NODES, LANES - 1
        ).T
    peer_index_ref[0] = peer_rows_ref[0:SHARED, :]
    peer_cols_ref[...] = peer_rows_ref[...].T
    peer_index_ref[1] = inverse_block(peer_cols_ref, LANES, 0).T[0:SHARED, :]
    for s in range(FCAP):
        e = slots_ref[s]
        for a in range(5):
            fixed_ref[a, s : s + 1, :] = turned_ref[a, pl.ds(e, 1), :]
        for a in range(2):
            index_ref[a, s : s + 1, :] = turned_index_ref[a, pl.ds(e, 1), :]
        for a in range(3):
            turned_ref[a, pl.ds(e, 1), :] = jnp.zeros((1, LANES), jnp.float32)
    rows = lax.broadcasted_iota(jnp.int32, (ROWS, FCAP), 0)
    slot_row = slot_row_ref[...]
    second = lax.shift_right_logical(slot_row + 1, 1)
    second = jnp.where(second == ROWS, 0, second)
    spread_wide_ref[...] = jnp.zeros_like(spread_wide_ref)
    spread_wide_ref[:, 0:FCAP] = jnp.where(
        lax.shift_right_logical(slot_row, 1) == rows, 1.0, 0.0
    )
    spread_wide_ref[:, LANES : LANES + FCAP] = jnp.where(second == rows, 1.0, 0.0)
    spread_ref[...] = spread_wide_ref[...].astype(jnp.bfloat16)
    total_ref[...] = jnp.zeros_like(total_ref)
    part = 40
    upper = high_half((1, LANES))
    for r0 in range(0, ROWS, part):

        def paired(ref, a):
            return jnp.concatenate(
                [ref[a, pl.ds(2 * r0 + odd, part, stride=2), :] for odd in range(2)], axis=0
            )

        index, place = paired(turned_index_ref, 0), paired(turned_index_ref, 1)
        shifted = []
        for c in range(3):
            here = disp_ref[c, r0 : r0 + part, :]
            after = disp_ref[c, r0 + 1 : r0 + part + 1, :]
            shifted.append(
                lane_pick(jnp.concatenate([here, jnp.where(upper, here, after)], axis=0), index)
            )
        nodal = forces(
            shifted,
            [paired(turned_ref, a) for a in range(3)],
            paired(turned_ref, 3),
            paired(turned_ref, 4),
            grad,
            back,
        )
        nodal.append(paired(turned_ref, 5))
        for c in range(4):
            spot = lane_pick(nodal[c], place)
            even, odd = spot[:part], spot[part:]
            total_ref[c, r0 : r0 + part, :] += even + jnp.where(upper, odd, 0.0)
            total_ref[c, r0 + 1 : r0 + part + 1, :] += jnp.where(upper, 0.0, odd)
    for c in range(4):
        total_ref[c, 0:1, :] += total_ref[c, ROWS : ROWS + 1, :]
        coarse_ref[c] = total_ref[c, 0:ROWS, :]
    fine = fine_local(
        disp_ref,
        slots_ref,
        window_ref,
        [fixed_ref[a] for a in range(5)] + [index_ref[a] for a in range(2)],
        spread_ref[...],
        grad,
        back,
    )
    for c in range(3):
        summed_ref[c] = coarse_ref[c] + fine[:, c * LANES : (c + 1) * LANES]
    send_rows(
        [summed_ref[c, FIRST:, :] for c in range(3)] + [coarse_ref[3, FIRST:, :]],
        peer_index_ref[0],
        parities,
        staged_ref,
        (sends0, sends1, sends2, sends3),
    )


def advance(disp, veloc, summed_ref, inverse_mass, placed):
    moved = []
    for c in range(3):
        force = jnp.concatenate(
            [summed_ref[c, :FIRST, :], summed_ref[c, FIRST:, :] + placed[c]], axis=0
        )
        v = veloc[c] - STEP * (inverse_mass * force)
        moved.append((disp[c] + STEP * v, v))
    return moved


def middle_kernel(
    opening,
    slots_ref,
    disp_ref,
    veloc_ref,
    coarse_ref,
    summed_ref,
    inverse_ref,
    fixed_ref,
    index_ref,
    spread_ref,
    peer_index_ref,
    got0,
    got1,
    got2,
    got3,
    grad_ref,
    back_ref,
    disp_out,
    veloc_out,
    summed_out,
    *rest,
):
    if opening:
        inverse_out, sends0, sends1, sends2, sends3, window_ref, staged_ref = rest
    else:
        sends0, sends1, sends2, sends3, window_ref, staged_ref = rest
    parities = own_parities()
    placed = received_rows(
        (got0, got1, got2, got3), 4 if opening else 3, peer_index_ref[1], parities, staged_ref
    )
    if opening:
        inverse_out[0:FIRST, :] = 1.0 / coarse_ref[3, 0:FIRST, :]
        inverse_out[FIRST:, :] = 1.0 / (coarse_ref[3, FIRST:, :] + placed[3])
        inverse_mass = inverse_out[...]
    else:
        inverse_mass = inverse_ref[...]
    moved = advance(
        [disp_ref[c, 0:ROWS, :] for c in range(3)],
        [veloc_ref[c] for c in range(3)],
        summed_ref,
        inverse_mass,
        placed,
    )
    for c in range(3):
        disp_out[c, 0:ROWS, :] = moved[c][0]
        disp_out[c, ROWS:PAD_ROWS, :] = jnp.broadcast_to(
            moved[c][0][0:1], (PAD_ROWS - ROWS, LANES)
        )
        veloc_out[c] = moved[c][1]
    fine = fine_local(
        disp_out,
        slots_ref,
        window_ref,
        [fixed_ref[a] for a in range(5)] + [index_ref[a] for a in range(2)],
        spread_ref[...],
        grad_ref[...],
        back_ref[...],
    )
    for c in range(3):
        summed_out[c] = coarse_ref[c] + fine[:, c * LANES : (c + 1) * LANES]
    send_rows(
        [summed_out[c, FIRST:, :] for c in range(3)],
        peer_index_ref[0],
        parities,
        staged_ref,
        (sends0, sends1, sends2, sends3),
    )


def last_kernel(
    disp_ref,
    veloc_ref,
    summed_ref,
    inverse_ref,
    peer_index_ref,
    got0,
    got1,
    got2,
    got3,
    disp_out,
    veloc_out,
    staged_ref,
    rows_ref,
):
    placed = received_rows(
        (got0, got1, got2, got3), 3, peer_index_ref[1], own_parities(), staged_ref
    )
    moved = advance(
        [disp_ref[c, 0:ROWS, :] for c in range(3)],
        [veloc_ref[c] for c in range(3)],
        summed_ref,
        inverse_ref[...],
        placed,
    )
    for which, out in ((0, disp_out), (1, veloc_out)):
        for c in range(3):
            rows_ref[which, c] = moved[c][which]
    for j in range(ROWS):
        cols = slice(j * LANES, (j + 1) * LANES)
        for which, out in ((0, disp_out), (1, veloc_out)):
            for c in range(3):
                out[c : c + 1, cols] = rows_ref[which, c, j : j + 1, :]


def swap_pairs(count, colour):
    pairs = []
    for low in range(colour, count, 2):
        high = (low + 1) % count
        pairs += [(low, high), (high, low)]
    return pairs


def swap_all(sends):
    plan = (("dev", 0), ("dev", 1), ("region", 0), ("region", 1))
    return [
        lax.ppermute(sent, axis, swap_pairs(lax.axis_size(axis), colour))
        for sent, (axis, colour) in zip(sends, plan)
    ]


def shape(dims, kind=jnp.float32):
    return jax.ShapeDtypeStruct(dims, kind)


PARAMS = pltpu.CompilerParams(vmem_limit_bytes=48 * 1024 * 1024)


def body(
    disp_start,
    veloc_start,
    jacobian,
    lame_lambda,
    lame_mu,
    density,
    connect,
    fine_slots,
    peer_nodes,
):
    grad_np, back_np = slope_operands()
    grad, back = jnp.asarray(grad_np), jnp.asarray(back_np)
    scalar = pl.BlockSpec(memory_space=pltpu.SMEM)
    vector = pl.BlockSpec(memory_space=pltpu.VMEM)
    field = shape((3, ROWS, LANES))
    padded = shape((3, PAD_ROWS, LANES))

    def sends(channels):
        return [shape((channels * GROUPS, LANES))] * 4

    outs = pl.pallas_call(
        first_kernel,
        in_specs=[scalar] + [vector] * 11,
        out_shape=[
            padded,
            field,
            shape((4, ROWS, LANES)),
            field,
            shape((5, FCAP, LANES)),
            shape((2, FCAP, LANES), jnp.int32),
            shape((ROWS, 2 * LANES), jnp.bfloat16),
            shape((2, SHARED, LANES), jnp.int32),
        ]
        + sends(4),
        out_specs=[vector] * 12,
        scratch_shapes=[
            pltpu.VMEM((6, PAD_ELEM, LANES), jnp.float32),
            pltpu.VMEM((2, PAD_ELEM, LANES), jnp.int32),
            pltpu.VMEM((LANES, PAD_ELEM), jnp.float32),
            pltpu.VMEM((3, LANES, LANES), jnp.int32),
            pltpu.VMEM((LANES, LANES), jnp.int32),
            pltpu.VMEM((LANES, LANES), jnp.int32),
            pltpu.VMEM((3, FCAP, LANES), jnp.float32),
            pltpu.VMEM((4, SHARED, LANES), jnp.float32),
            pltpu.VMEM((4, PAD_ROWS, LANES), jnp.float32),
            pltpu.VMEM((ROWS, 2 * LANES), jnp.float32),
        ],
        compiler_params=PARAMS,
        name="first",
    )(
        fine_slots,
        fine_slots.reshape(1, FCAP),
        disp_start,
        veloc_start,
        jacobian,
        lame_lambda,
        lame_mu,
        density,
        connect,
        peer_nodes,
        grad,
        back,
    )
    disp, veloc, coarse, summed, fixed, index, spread, peer_index = outs[:8]
    got = swap_all(outs[8:])
    inverse_mass = None
    for substep in range(SUBSTEPS - 1):
        opening = substep == 0
        extra = [shape((ROWS, LANES))] if opening else []
        outs = pl.pallas_call(
            lambda *refs, opening=opening: middle_kernel(opening, *refs),
            in_specs=[scalar] + [vector] * 15,
            out_shape=[padded, field, field] + extra + sends(3),
            out_specs=[vector] * (7 + len(extra)),
            scratch_shapes=[
                pltpu.VMEM((3, FCAP, LANES), jnp.float32),
                pltpu.VMEM((4, SHARED, LANES), jnp.float32),
            ],
            compiler_params=PARAMS,
            name="middle",
        )(
            fine_slots,
            disp,
            veloc,
            coarse,
            summed,
            coarse if opening else inverse_mass,
            fixed,
            index,
            spread,
            peer_index,
            *got,
            grad,
            back,
        )
        disp, veloc, summed = outs[:3]
        if opening:
            inverse_mass = outs[3]
        got = swap_all(outs[-4:])
    return pl.pallas_call(
        last_kernel,
        in_specs=[vector] * 9,
        out_shape=[shape((3, NLOC)), shape((3, NLOC))],
        out_specs=[vector] * 2,
        scratch_shapes=[
            pltpu.VMEM((4, SHARED, LANES), jnp.float32),
            pltpu.VMEM((2, 3, ROWS, LANES), jnp.float32),
        ],
        compiler_params=PARAMS,
        name="last",
    )(disp, veloc, summed, inverse_mass, peer_index, *got)


def solution(mesh):
    in_specs = (
        P(None, ("region", "dev")),
        P(None, ("region", "dev")),
        P(None, None, ("region", "dev")),
        P(None, ("region", "dev")),
        P(None, ("region", "dev")),
        P(None, ("region", "dev")),
        P(None, ("region", "dev")),
        P(("region", "dev")),
        P(None, ("region", "dev")),
    )
    out_specs = (P(None, ("region", "dev")), P(None, ("region", "dev")))
    return jax.shard_map(body, mesh=mesh, in_specs=in_specs, out_specs=out_specs, check_vma=False)
```

profile of v0, /device:TPU:0, one launch (start us, length us, event | category | flops | bytes accessed | tf_op | source)
XLA Modules:
  0.0 73.3 jit_solution(1848840109526866864)
XLA Ops:
  0.7 1.1 %copy.14.lam_ref = f32[125,320]{1,0:T(8,128)S(1)} copy(f32[125,320]{0,1:T(8,128)} %param.14) | data formatting | bytes 320000 | tf_op args[3]
  1.8 0.1 copy.15.mu_ref
  1.9 0.1 copy.16.dens_ref
  2.1 0.8 %copy-done.9 = s32[125,320]{0,1:T(8,128)S(1)} copy-done((s32[125,320]{0,1:T(8,128)S(1)}, s32[125,320]{0,1:T(8,128)}, u32[]{:S(2)}) %copy-start.9) | copy-done | bytes 160024
  2.8 0.1 copy.17.conn_ref
  3.0 0.3 copy.13.jac_ref
  3.3 0.5 copy-done.3
  3.8 0.2 copy-done
  4.1 0.1 copy-done.2
  4.2 9.0 %first.1 = (f32[3,168,128]{2,1,0:T(8,128)S(1)}, f32[3,160,128]{2,1,0:T(8,128)S(1)}, f32[4,160,128]{2,1,0:T(8,128)S(1)}, f32[3,160,128]{2,1,0:T(8,128)S(1)}, f32[...) custom-call(s32[80]{0:T(128)S(1)} %copy-done.5, ...), custom_call_target="tpu_custom_call" | custom-call | tf_op jit(solution)/shard_map/first/pallas_call | solution.py:496
  13.2 0.1 collective-permute-start
  13.3 10.2 %collective-permute-start.1 = (f32[80,128]{1,0:T(8,128)S(1)}, f32[80,128]{1,0:T(8,128)S(1)}, u32[]{:S(2)}, u32[]{:S(2)}) collective-permute-start(f32[80,128]{1,0:T(8,128)S(1)} %get-tuple-element.45), channel_id=1, source_target_pairs={{1,2},{2,1},{3,4},{4,3},{5,6},{6,5},{7,8},{8,7},{9,10},{10,9},{11,... | collective-permute-start | bytes 122888 | tf_op jit(solution)/shard_map/ppermute | solution.py:463
  23.5 1.0 %collective-permute-start.2 = (f32[80,128]{1,0:T(8,128)S(1)}, f32[80,128]{1,0:T(8,128)S(1)}, u32[]{:S(2)}, u32[]{:S(2)}) collective-permute-start(f32[80,128]{1,0:T(8,128)S(1)} %get-tuple-element.46), channel_id=1, source_target_pairs={{0,64},{64,0},{128,192},{192,128},{1,65},{65,1},{129,193},{193,129... | collective-permute-start | bytes 122888 | tf_op jit(solution)/shard_map/ppermute | solution.py:463
  24.6 1.9 %collective-permute-start.3 = (f32[80,128]{1,0:T(8,128)S(1)}, f32[80,128]{1,0:T(8,128)S(1)}, u32[]{:S(2)}, u32[]{:S(2)}) collective-permute-start(f32[80,128]{1,0:T(8,128)S(1)} %get-tuple-element.47), channel_id=1, source_target_pairs={{64,128},{128,64},{192,0},{0,192},{65,129},{129,65},{193,1},{1,193... | collective-permute-start | bytes 122888 | tf_op jit(solution)/shard_map/ppermute | solution.py:463
  26.5 1.4 %collective-permute-done.2.refs_12_ = f32[80,128]{1,0:T(8,128)S(1)} collective-permute-done((f32[80,128]{1,0:T(8,128)S(1)}, f32[80,128]{1,0:T(8,128)S(1)}, u32[]{:S(2)}, u32[]{:S(2)}) %collective-permute-start.2) | collective-permute-done | bytes 40992 | tf_op jit(solution)/shard_map/ppermute | solution.py:463
  27.9 2.5 %collective-permute-done.3.refs_13_ = f32[80,128]{1,0:T(8,128)S(1)} collective-permute-done((f32[80,128]{1,0:T(8,128)S(1)}, f32[80,128]{1,0:T(8,128)S(1)}, u32[]{:S(2)}, u32[]{:S(2)}) %collective-permute-start.3) | collective-permute-done | bytes 40992 | tf_op jit(solution)/shard_map/ppermute | solution.py:463
  30.4 2.1 %middle.3 = (f32[3,168,128]{2,1,0:T(8,128)S(1)}, f32[3,160,128]{2,1,0:T(8,128)S(1)}, f32[3,160,128]{2,1,0:T(8,128)S(1)}, f32[160,128]{1,0:T(8,128)S(1)}, f32[60,...) custom-call(s32[80]{0:T(128)S(1)} %copy-done.5, ...), custom_call_target="tpu_custom_call" | custom-call | tf_op jit(solution)/shard_map/middle/pallas_call | solution.py:545
  32.5 4.8 %collective-permute-start.5 = (f32[60,128]{1,0:T(8,128)S(1)}, f32[60,128]{1,0:T(8,128)S(1)}, u32[]{:S(2)}, u32[]{:S(2)}) collective-permute-start(f32[60,128]{1,0:T(8,128)S(1)} %get-tuple-element.53), channel_id=1, source_target_pairs={{1,2},{2,1},{3,4},{4,3},{5,6},{6,5},{7,8},{8,7},{9,10},{10,9},{11,... | collective-permute-start | bytes 92168 | tf_op jit(solution)/shard_map/ppermute | solution.py:463
  37.4 1.0 %collective-permute-start.6 = (f32[60,128]{1,0:T(8,128)S(1)}, f32[60,128]{1,0:T(8,128)S(1)}, u32[]{:S(2)}, u32[]{:S(2)}) collective-permute-start(f32[60,128]{1,0:T(8,128)S(1)} %get-tuple-element.54), channel_id=1, source_target_pairs={{0,64},{64,0},{128,192},{192,128},{1,65},{65,1},{129,193},{193,129... | collective-permute-start | bytes 92168 | tf_op jit(solution)/shard_map/ppermute | solution.py:463
  38.4 1.9 %collective-permute-start.7 = (f32[60,128]{1,0:T(8,128)S(1)}, f32[60,128]{1,0:T(8,128)S(1)}, u32[]{:S(2)}, u32[]{:S(2)}) collective-permute-start(f32[60,128]{1,0:T(8,128)S(1)} %get-tuple-element.55), channel_id=1, source_target_pairs={{64,128},{128,64},{192,0},{0,192},{65,129},{129,65},{193,1},{1,193... | collective-permute-start | bytes 92168 | tf_op jit(solution)/shard_map/ppermute | solution.py:463
  40.3 3.9 %collective-permute-done.5.refs_11_ = f32[60,128]{1,0:T(8,128)S(1)} collective-permute-done((f32[60,128]{1,0:T(8,128)S(1)}, f32[60,128]{1,0:T(8,128)S(1)}, u32[]{:S(2)}, u32[]{:S(2)}) %collective-permute-start.5) | collective-permute-done | bytes 30752 | tf_op jit(solution)/shard_map/ppermute | solution.py:463
  44.2 2.0 %middle.4 = (f32[3,168,128]{2,1,0:T(8,128)S(1)}, f32[3,160,128]{2,1,0:T(8,128)S(1)}, f32[3,160,128]{2,1,0:T(8,128)S(1)}, f32[60,128]{1,0:T(8,128)S(1)}, f32[60,1...) custom-call(s32[80]{0:T(128)S(1)} %copy-done.5, f32[3,168,128]{2,1,0:T(8,128)S(1)} %get-tuple-element.48.refs_1_, ...), custom_call_target="tpu_custom_call" | custom-call | tf_op jit(solution)/shard_map/middle/pallas_call | solution.py:545
  46.3 4.9 %collective-permute-start.9 = (f32[60,128]{1,0:T(8,128)S(1)}, f32[60,128]{1,0:T(8,128)S(1)}, u32[]{:S(2)}, u32[]{:S(2)}) collective-permute-start(f32[60,128]{1,0:T(8,128)S(1)} %get-tuple-element.60), channel_id=1, source_target_pairs={{1,2},{2,1},{3,4},{4,3},{5,6},{6,5},{7,8},{8,7},{9,10},{10,9},{11,... | collective-permute-start | bytes 92168 | tf_op jit(solution)/shard_map/ppermute | solution.py:463
  51.3 1.0 %collective-permute-start.10 = (f32[60,128]{1,0:T(8,128)S(1)}, f32[60,128]{1,0:T(8,128)S(1)}, u32[]{:S(2)}, u32[]{:S(2)}) collective-permute-start(f32[60,128]{1,0:T(8,128)S(1)} %get-tuple-element.61), channel_id=1, source_target_pairs={{0,64},{64,0},{128,192},{192,128},{1,65},{65,1},{129,193},{193,129... | collective-permute-start | bytes 92168 | tf_op jit(solution)/shard_map/ppermute | solution.py:463
  52.3 1.9 %collective-permute-start.11 = (f32[60,128]{1,0:T(8,128)S(1)}, f32[60,128]{1,0:T(8,128)S(1)}, u32[]{:S(2)}, u32[]{:S(2)}) collective-permute-start(f32[60,128]{1,0:T(8,128)S(1)} %get-tuple-element.62), channel_id=1, source_target_pairs={{64,128},{128,64},{192,0},{0,192},{65,129},{129,65},{193,1},{1,193... | collective-permute-start | bytes 92168 | tf_op jit(solution)/shard_map/ppermute | solution.py:463
  54.1 4.0 %collective-permute-done.9.refs_11_ = f32[60,128]{1,0:T(8,128)S(1)} collective-permute-done((f32[60,128]{1,0:T(8,128)S(1)}, f32[60,128]{1,0:T(8,128)S(1)}, u32[]{:S(2)}, u32[]{:S(2)}) %collective-permute-start.9) | collective-permute-done | bytes 30752 | tf_op jit(solution)/shard_map/ppermute | solution.py:463
  58.2 2.0 %middle.5 = (f32[3,168,128]{2,1,0:T(8,128)S(1)}, f32[3,160,128]{2,1,0:T(8,128)S(1)}, f32[3,160,128]{2,1,0:T(8,128)S(1)}, f32[60,128]{1,0:T(8,128)S(1)}, f32[60,1...) custom-call(s32[80]{0:T(128)S(1)} %copy-done.5, f32[3,168,128]{2,1,0:T(8,128)S(1)} %get-tuple-element.56.refs_1_, ...), custom_call_target="tpu_custom_call" | custom-call | tf_op jit(solution)/shard_map/middle/pallas_call | solution.py:545
  60.3 4.7 %collective-permute-start.13 = (f32[60,128]{1,0:T(8,128)S(1)}, f32[60,128]{1,0:T(8,128)S(1)}, u32[]{:S(2)}, u32[]{:S(2)}) collective-permute-start(f32[60,128]{1,0:T(8,128)S(1)} %get-tuple-element.67), channel_id=1, source_target_pairs={{1,2},{2,1},{3,4},{4,3},{5,6},{6,5},{7,8},{8,7},{9,10},{10,9},{11,... | collective-permute-start | bytes 92168 | tf_op jit(solution)/shard_map/ppermute | solution.py:463
  65.0 1.0 %collective-permute-start.14 = (f32[60,128]{1,0:T(8,128)S(1)}, f32[60,128]{1,0:T(8,128)S(1)}, u32[]{:S(2)}, u32[]{:S(2)}) collective-permute-start(f32[60,128]{1,0:T(8,128)S(1)} %get-tuple-element.68), channel_id=1, source_target_pairs={{0,64},{64,0},{128,192},{192,128},{1,65},{65,1},{129,193},{193,129... | collective-permute-start | bytes 92168 | tf_op jit(solution)/shard_map/ppermute | solution.py:463
  65.9 1.9 %collective-permute-start.15 = (f32[60,128]{1,0:T(8,128)S(1)}, f32[60,128]{1,0:T(8,128)S(1)}, u32[]{:S(2)}, u32[]{:S(2)}) collective-permute-start(f32[60,128]{1,0:T(8,128)S(1)} %get-tuple-element.69), channel_id=1, source_target_pairs={{64,128},{128,64},{192,0},{0,192},{65,129},{129,65},{193,1},{1,193... | collective-permute-start | bytes 92168 | tf_op jit(solution)/shard_map/ppermute | solution.py:463
  67.8 4.1 %collective-permute-done.13.got1 = f32[60,128]{1,0:T(8,128)S(1)} collective-permute-done((f32[60,128]{1,0:T(8,128)S(1)}, f32[60,128]{1,0:T(8,128)S(1)}, u32[]{:S(2)}, u32[]{:S(2)}) %collective-permute-start.13) | collective-permute-done | bytes 30752 | tf_op jit(solution)/shard_map/ppermute | solution.py:463
  72.0 1.3 %last.1 = (f32[3,20480]{1,0:T(4,128)}, f32[3,20480]{1,0:T(4,128)}) custom-call(f32[3,168,128]{2,1,0:T(8,128)S(1)} %get-tuple-element.63.disp_ref, f32[3,160,128]{2,1,0:T(8,128)S(1)} %get-tuple-element.64.veloc_ref, f32[3,160,128]{2,1,0:T(8,128)S(1)} %get-tuple-element.65.summed_ref, f32[160,128]{1,0:T(8,128)S(1)} %get-tuple-element.51.refs_5_.inverse_ref, ...), custom_call_target="tpu_custom_call" | custom-call | tf_op jit(solution)/shard_map/last/pallas_call | solution.py:575
  (30 shorter events, 0.4 us)
Async XLA Ops:
  0.6 1.1 %copy-start.7 = (f32[125,320]{0,1:T(8,128)S(1)}, f32[125,320]{0,1:T(8,128)}, u32[]{:S(2)}) copy-start(f32[125,320]{0,1:T(8,128)} %param.15) | copy-start | bytes 480004
  0.6 1.3 %copy-start.8 = (f32[125,320]{0,1:T(8,128)S(1)}, f32[125,320]{0,1:T(8,128)}, u32[]{:S(2)}) copy-start(f32[125,320]{0,1:T(8,128)} %param.16) | copy-start | bytes 480004
  1.8 1.2 %copy-start.6 = (f32[3,125,320]{1,2,0:T(8,128)S(1)}, f32[3,125,320]{1,2,0:T(8,128)}, u32[]{:S(2)}) copy-start(f32[3,125,320]{1,2,0:T(8,128)} %param.13) | copy-start | bytes 1440004
  1.9 0.9 %copy-start.9 = (s32[125,320]{0,1:T(8,128)S(1)}, s32[125,320]{0,1:T(8,128)}, u32[]{:S(2)}) copy-start(s32[125,320]{0,1:T(8,128)} %param.17) | copy-start | bytes 480004
  2.8 1.0 %copy-start.3 = (f32[3,20480]{1,0:T(4,128)S(1)}, f32[3,20480]{1,0:T(4,128)}, u32[]{:S(2)}) copy-start(f32[3,20480]{1,0:T(4,128)} %veloc_in.1) | copy-start | bytes 737284
  3.0 1.0 %copy-start = (bf16[1152,128]{1,0:T(8,128)(2,1)S(1)}, bf16[1152,128]{1,0:T(8,128)(2,1)}, u32[]{:S(2)}) copy-start(bf16[1152,128]{1,0:T(8,128)(2,1)} %constant.5.clone.back_ref.refs_15_) | copy-start | bytes 884740
  3.0 1.1 %copy-start.1 = (bf16[384,384]{1,0:T(8,128)(2,1)S(1)}, bf16[384,384]{1,0:T(8,128)(2,1)}, u32[]{:S(2)}) copy-start(bf16[384,384]{1,0:T(8,128)(2,1)} %constant.4.clone.grad_ref.refs_14_) | copy-start | bytes 884740
  3.0 1.2 %copy-start.2 = (f32[3,20480]{1,0:T(4,128)S(1)}, f32[3,20480]{1,0:T(4,128)}, u32[]{:S(2)}) copy-start(f32[3,20480]{1,0:T(4,128)} %disp_in.1) | copy-start | bytes 737284
  3.0 1.1 %copy-start.4 = (s32[4,2560]{1,0:T(4,128)S(1)}, s32[4,2560]{1,0:T(4,128)}, u32[]{:S(2)}) copy-start(s32[4,2560]{1,0:T(4,128)} %peer_ref.1) | copy-start | bytes 122884
  3.3 0.9 %copy-start.5 = (s32[80]{0:T(128)S(1)}, s32[80]{0:T(128)}, u32[]{:S(2)}) copy-start(s32[80]{0:T(128)} %refs_0_.5) | copy-start | bytes 964
  13.2 13.2 %collective-permute-start = (f32[80,128]{1,0:T(8,128)S(1)}, f32[80,128]{1,0:T(8,128)S(1)}, u32[]{:S(2)}, u32[]{:S(2)}) collective-permute-start(f32[80,128]{1,0:T(8,128)S(1)} %get-tuple-element.44), channel_id=1, source_target_pairs={{0,1},{1,0},{2,3},{3,2},{4,5},{5,4},{6,7},{7,6},{8,9},{9,8},{10,11... | collective-permute-start | bytes 122888 | tf_op jit(solution)/shard_map/ppermute | solution.py:463
  13.3 13.1 %collective-permute-start.1 = (f32[80,128]{1,0:T(8,128)S(1)}, f32[80,128]{1,0:T(8,128)S(1)}, u32[]{:S(2)}, u32[]{:S(2)}) collective-permute-start(f32[80,128]{1,0:T(8,128)S(1)} %get-tuple-element.45), channel_id=1, source_target_pairs={{1,2},{2,1},{3,4},{4,3},{5,6},{6,5},{7,8},{8,7},{9,10},{10,9},{11,... | collective-permute-start | bytes 122888 | tf_op jit(solution)/shard_map/ppermute | solution.py:463
  23.5 4.4 %collective-permute-start.2 = (f32[80,128]{1,0:T(8,128)S(1)}, f32[80,128]{1,0:T(8,128)S(1)}, u32[]{:S(2)}, u32[]{:S(2)}) collective-permute-start(f32[80,128]{1,0:T(8,128)S(1)} %get-tuple-element.46), channel_id=1, source_target_pairs={{0,64},{64,0},{128,192},{192,128},{1,65},{65,1},{129,193},{193,129... | collective-permute-start | bytes 122888 | tf_op jit(solution)/shard_map/ppermute | solution.py:463
  24.6 5.8 %collective-permute-start.3 = (f32[80,128]{1,0:T(8,128)S(1)}, f32[80,128]{1,0:T(8,128)S(1)}, u32[]{:S(2)}, u32[]{:S(2)}) collective-permute-start(f32[80,128]{1,0:T(8,128)S(1)} %get-tuple-element.47), channel_id=1, source_target_pairs={{64,128},{128,64},{192,0},{0,192},{65,129},{129,65},{193,1},{1,193... | collective-permute-start | bytes 122888 | tf_op jit(solution)/shard_map/ppermute | solution.py:463
  32.4 7.8 %collective-permute-start.4 = (f32[60,128]{1,0:T(8,128)S(1)}, f32[60,128]{1,0:T(8,128)S(1)}, u32[]{:S(2)}, u32[]{:S(2)}) collective-permute-start(f32[60,128]{1,0:T(8,128)S(1)} %get-tuple-element.52), channel_id=1, source_target_pairs={{0,1},{1,0},{2,3},{3,2},{4,5},{5,4},{6,7},{7,6},{8,9},{9,8},{10,11... | collective-permute-start | bytes 92168 | tf_op jit(solution)/shard_map/ppermute | solution.py:463
  32.5 11.7 %collective-permute-start.5 = (f32[60,128]{1,0:T(8,128)S(1)}, f32[60,128]{1,0:T(8,128)S(1)}, u32[]{:S(2)}, u32[]{:S(2)}) collective-permute-start(f32[60,128]{1,0:T(8,128)S(1)} %get-tuple-element.53), channel_id=1, source_target_pairs={{1,2},{2,1},{3,4},{4,3},{5,6},{6,5},{7,8},{8,7},{9,10},{10,9},{11,... | collective-permute-start | bytes 92168 | tf_op jit(solution)/shard_map/ppermute | solution.py:463
  37.4 6.8 %collective-permute-start.6 = (f32[60,128]{1,0:T(8,128)S(1)}, f32[60,128]{1,0:T(8,128)S(1)}, u32[]{:S(2)}, u32[]{:S(2)}) collective-permute-start(f32[60,128]{1,0:T(8,128)S(1)} %get-tuple-element.54), channel_id=1, source_target_pairs={{0,64},{64,0},{128,192},{192,128},{1,65},{65,1},{129,193},{193,129... | collective-permute-start | bytes 92168 | tf_op jit(solution)/shard_map/ppermute | solution.py:463
  38.4 5.8 %collective-permute-start.7 = (f32[60,128]{1,0:T(8,128)S(1)}, f32[60,128]{1,0:T(8,128)S(1)}, u32[]{:S(2)}, u32[]{:S(2)}) collective-permute-start(f32[60,128]{1,0:T(8,128)S(1)} %get-tuple-element.55), channel_id=1, source_target_pairs={{64,128},{128,64},{192,0},{0,192},{65,129},{129,65},{193,1},{1,193... | collective-permute-start | bytes 92168 | tf_op jit(solution)/shard_map/ppermute | solution.py:463
  46.2 7.9 %collective-permute-start.8 = (f32[60,128]{1,0:T(8,128)S(1)}, f32[60,128]{1,0:T(8,128)S(1)}, u32[]{:S(2)}, u32[]{:S(2)}) collective-permute-start(f32[60,128]{1,0:T(8,128)S(1)} %get-tuple-element.59), channel_id=1, source_target_pairs={{0,1},{1,0},{2,3},{3,2},{4,5},{5,4},{6,7},{7,6},{8,9},{9,8},{10,11... | collective-permute-start | bytes 92168 | tf_op jit(solution)/shard_map/ppermute | solution.py:463
  46.3 11.8 %collective-permute-start.9 = (f32[60,128]{1,0:T(8,128)S(1)}, f32[60,128]{1,0:T(8,128)S(1)}, u32[]{:S(2)}, u32[]{:S(2)}) collective-permute-start(f32[60,128]{1,0:T(8,128)S(1)} %get-tuple-element.60), channel_id=1, source_target_pairs={{1,2},{2,1},{3,4},{4,3},{5,6},{6,5},{7,8},{8,7},{9,10},{10,9},{11,... | collective-permute-start | bytes 92168 | tf_op jit(solution)/shard_map/ppermute | solution.py:463
  51.3 6.9 %collective-permute-start.10 = (f32[60,128]{1,0:T(8,128)S(1)}, f32[60,128]{1,0:T(8,128)S(1)}, u32[]{:S(2)}, u32[]{:S(2)}) collective-permute-start(f32[60,128]{1,0:T(8,128)S(1)} %get-tuple-element.61), channel_id=1, source_target_pairs={{0,64},{64,0},{128,192},{192,128},{1,65},{65,1},{129,193},{193,129... | collective-permute-start | bytes 92168 | tf_op jit(solution)/shard_map/ppermute | solution.py:463
  52.3 5.9 %collective-permute-start.11 = (f32[60,128]{1,0:T(8,128)S(1)}, f32[60,128]{1,0:T(8,128)S(1)}, u32[]{:S(2)}, u32[]{:S(2)}) collective-permute-start(f32[60,128]{1,0:T(8,128)S(1)} %get-tuple-element.62), channel_id=1, source_target_pairs={{64,128},{128,64},{192,0},{0,192},{65,129},{129,65},{193,1},{1,193... | collective-permute-start | bytes 92168 | tf_op jit(solution)/shard_map/ppermute | solution.py:463
  60.2 7.6 %collective-permute-start.12 = (f32[60,128]{1,0:T(8,128)S(1)}, f32[60,128]{1,0:T(8,128)S(1)}, u32[]{:S(2)}, u32[]{:S(2)}) collective-permute-start(f32[60,128]{1,0:T(8,128)S(1)} %get-tuple-element.66), channel_id=1, source_target_pairs={{0,1},{1,0},{2,3},{3,2},{4,5},{5,4},{6,7},{7,6},{8,9},{9,8},{10,11... | collective-permute-start | bytes 92168 | tf_op jit(solution)/shard_map/ppermute | solution.py:463
  60.3 11.7 %collective-permute-start.13 = (f32[60,128]{1,0:T(8,128)S(1)}, f32[60,128]{1,0:T(8,128)S(1)}, u32[]{:S(2)}, u32[]{:S(2)}) collective-permute-start(f32[60,128]{1,0:T(8,128)S(1)} %get-tuple-element.67), channel_id=1, source_target_pairs={{1,2},{2,1},{3,4},{4,3},{5,6},{6,5},{7,8},{8,7},{9,10},{10,9},{11,... | collective-permute-start | bytes 92168 | tf_op jit(solution)/shard_map/ppermute | solution.py:463
  65.0 7.0 %collective-permute-start.14 = (f32[60,128]{1,0:T(8,128)S(1)}, f32[60,128]{1,0:T(8,128)S(1)}, u32[]{:S(2)}, u32[]{:S(2)}) collective-permute-start(f32[60,128]{1,0:T(8,128)S(1)} %get-tuple-element.68), channel_id=1, source_target_pairs={{0,64},{64,0},{128,192},{192,128},{1,65},{65,1},{129,193},{193,129... | collective-permute-start | bytes 92168 | tf_op jit(solution)/shard_map/ppermute | solution.py:463
  65.9 6.0 %collective-permute-start.15 = (f32[60,128]{1,0:T(8,128)S(1)}, f32[60,128]{1,0:T(8,128)S(1)}, u32[]{:S(2)}, u32[]{:S(2)}) collective-permute-start(f32[60,128]{1,0:T(8,128)S(1)} %get-tuple-element.69), channel_id=1, source_target_pairs={{64,128},{128,64},{192,0},{0,192},{65,129},{129,65},{193,1},{1,193... | collective-permute-start | bytes 92168 | tf_op jit(solution)/shard_map/ppermute | solution.py:463
where the time goes:
time: 73.4 us; the launch traced here: 73.3 us
  starting transfers between devices  36.6 us (50%)
  Pallas kernels  16.5 us (22%)
  waiting for transfers between devices  16 us (22%)
  local copies, waits for them, and re-layouts  3.47 us (5%)
  between operations  0.78 us (1%)
    ppermute x16, starting transfers between devices, swap_all(): lax.ppermute(sent, axis, swap_pairs(lax.axis_size(axis), colour))  36.6 us
    ppermute x16, waiting for transfers between devices, swap_all(): lax.ppermute(sent, axis, swap_pairs(lax.axis_size(axis), colour))  16 us
    pallas_call x1, Pallas kernels, body(): pl.pallas_call(first_kernel, in_specs=[scalar] + [vector] * 11, out_shape...  9.04 us
    pallas_call x3, Pallas kernels, body(): pl.pallas_call(lambda *refs, opening=opening: middle_kernel(opening, *ref...  6.12 us
    unnamed x25, local copies, waits for them, and re-layouts  3.47 us
  transfers between devices with their start and end apart: 16, of which 5 were waited for; matrix products, arithmetic and copies ran while one was open for 0% of the time, Pallas kernels for 0%

commit v1 on v0

v1 whole, which is shorter than its diff:
```python
import functools
import math

import jax
import jax.numpy as jnp
import ml_dtypes
import numpy as np
from jax import lax
from jax.experimental import pallas as pl
from jax.experimental.pallas import tpu as pltpu
from jax.sharding import PartitionSpec as P

NODES = 125
ELEM = 320
NLOC = 20480
FCAP = 80
LANES = 128
ROWS = NLOC // LANES
FIRST = ROWS // 2
GROUPS = 20
SHARED = 4 * GROUPS
SUBSTEPS = 4
GLL_POINTS = (-1.0, -math.sqrt(3.0 / 7.0), 0.0, math.sqrt(3.0 / 7.0), 1.0)
TIME_STEP = 0.2
STEP = TIME_STEP / SUBSTEPS
PAD_ROWS = 168


def slope_rows():
    points = GLL_POINTS
    rows = []
    for row_at in range(5):
        entries = []
        for col_at in range(5):
            if row_at == col_at:
                summed = 0.0
                for other_at in range(5):
                    if other_at != row_at:
                        summed += 1.0 / (points[row_at] - points[other_at])
                entries.append(summed)
            else:
                top_prod = 1.0
                low_prod = 1.0
                for other_at in range(5):
                    if other_at != row_at:
                        top_prod *= points[row_at] - points[other_at]
                    if other_at != col_at:
                        low_prod *= points[col_at] - points[other_at]
                entries.append(top_prod / low_prod / (points[row_at] - points[col_at]))
        rows.append(entries)
    return rows


def slope_operands():
    slopes = np.array(slope_rows(), dtype=np.float32)
    eye = np.eye(5, dtype=np.float32)
    along = [
        np.kron(np.kron(slopes, eye), eye),
        np.kron(np.kron(eye, slopes), eye),
        np.kron(np.kron(eye, eye), slopes),
    ]
    grad = np.zeros((LANES, 3 * LANES), np.float32)
    back = np.zeros((3 * LANES, LANES), np.float32)
    for i, matrix in enumerate(along):
        grad[:NODES, i * LANES : i * LANES + NODES] = matrix.T
        back[i * LANES : i * LANES + NODES, :NODES] = matrix

    def terms(whole):
        high = whole.astype(ml_dtypes.bfloat16)
        low = (whole - high.astype(np.float32)).astype(ml_dtypes.bfloat16)
        return np.concatenate([high, high, low], axis=0)

    return terms(grad), terms(back)


def split_terms(whole):
    high = whole.astype(jnp.bfloat16)
    low = (whole - high.astype(jnp.float32)).astype(jnp.bfloat16)
    return high, low


def lane_pick(values, index):
    return jnp.take_along_axis(values, index, axis=1, mode="promise_in_bounds")


def forces(shifted, jac, lam, mu, grad, back):
    count = shifted[0].shape[0]
    high, low = split_terms(jnp.concatenate(shifted, axis=0))
    slope = jnp.dot(
        jnp.concatenate([high, low, high], axis=1), grad, preferred_element_type=jnp.float32
    )
    strain = [
        [
            jac[i] * slope[c * count : (c + 1) * count, i * LANES : (i + 1) * LANES]
            for i in range(3)
        ]
        for c in range(3)
    ]
    traced = lam * (strain[0][0] + strain[1][1] + strain[2][2])
    rows = []
    for c in range(3):
        fluxes = []
        for i in range(3):
            stress = mu * (strain[c][i] + strain[i][c])
            if c == i:
                stress = stress + traced
            fluxes.append(jac[i] * stress)
        rows.append(jnp.concatenate(fluxes, axis=1))
    high, low = split_terms(jnp.concatenate(rows, axis=0))
    out = jnp.dot(
        jnp.concatenate([high, low, high], axis=1), back, preferred_element_type=jnp.float32
    )
    return [out[c * count : (c + 1) * count] for c in range(3)]


def inverse_rows(index, turned_ref, count, missing):
    turned_ref[...] = index.astype(jnp.float32).T
    target = lax.broadcasted_iota(jnp.int32, (LANES, LANES), 0).astype(jnp.float32)
    target = target.astype(jnp.bfloat16)
    found = jnp.full((LANES, LANES), missing, jnp.bfloat16)
    for k in range(count):
        row = jnp.broadcast_to(turned_ref[k : k + 1, :], (16, LANES)).astype(jnp.bfloat16)
        row = jnp.concatenate([row] * (LANES // 16), axis=0)
        found = jnp.where(row == target, jnp.full((LANES, LANES), k, jnp.bfloat16), found)
    return found.astype(jnp.float32).T.astype(jnp.int32)


def high_half(shape):
    return lax.broadcasted_iota(jnp.int32, shape, 1) >= LANES // 2


def fine_local(disp_ref, slots_ref, window_ref, statics, spread, grad, back):
    jac0, jac1, jac2, lam, mu, index, place = statics
    upper = high_half((1, LANES))
    for s in range(FCAP):
        e = slots_ref[s]
        first = lax.shift_right_logical(e, 1)
        second = lax.shift_right_logical(e + 1, 1)
        for c in range(3):
            window_ref[c, pl.ds(s, 1), :] = jnp.where(
                upper, disp_ref[c, pl.ds(first, 1), :], disp_ref[c, pl.ds(second, 1), :]
            )
    shifted = [lane_pick(window_ref[c], index) for c in range(3)]
    out = forces(shifted, (jac0, jac1, jac2), lam, mu, grad, back)
    slotted = jnp.concatenate([lane_pick(o, place) for o in out], axis=1)
    upper = lax.broadcasted_iota(jnp.int32, slotted.shape, 1) % LANES >= LANES // 2
    blank = jnp.zeros((LANES - FCAP, slotted.shape[1]), jnp.float32)
    both = jnp.concatenate(
        [jnp.where(upper, slotted, 0.0), blank, jnp.where(upper, 0.0, slotted), blank], axis=0
    )
    high, low = split_terms(both)
    return jnp.dot(spread, high, preferred_element_type=jnp.float32) + jnp.dot(
        spread, low, preferred_element_type=jnp.float32
    )


def send_pair(shared, picks, odd, staged_ref, outs):
    for c, values in enumerate(shared):
        staged_ref[c] = lane_pick(values, picks)
    for c in range(len(shared)):
        part = [staged_ref[c, GROUPS * p : GROUPS * (p + 1), :] for p in range(2)]
        put = pl.ds(c * GROUPS, GROUPS)
        outs[0][put, :] = jnp.where(odd, part[0], part[1])
        outs[1][put, :] = jnp.where(odd, part[1], part[0])


def received_pair(arrived, channels, places, odd, staged_ref):
    for c in range(channels):
        got = [a[c * GROUPS : (c + 1) * GROUPS, :] for a in arrived]
        staged_ref[c, 0:GROUPS, :] = jnp.where(odd, got[0][...], got[1][...])
        staged_ref[c, GROUPS : 2 * GROUPS, :] = jnp.where(odd, got[1][...], got[0][...])
    return [lane_pick(staged_ref[c], places) for c in range(channels)]


def odd_place(axis):
    return jnp.bitwise_and(lax.axis_index(axis), 1) == 1


def peer_maps(peer_ref, first, rows_ref):
    for p in range(2):
        for j in range(GROUPS):
            at = p * GROUPS + j
            rows_ref[at : at + 1, :] = peer_ref[
                first + p : first + p + 1, j * LANES : (j + 1) * LANES
            ] & (LANES - 1)


def element_rows(refs, low, count, pads, clear):
    jac_ref, lam_ref, mu_ref, dens_ref, conn_ref = refs
    value_ref, index_ref = pads
    if clear:
        value_ref[:, :, LANES - 8 :] = jnp.zeros_like(value_ref[:, :, LANES - 8 :])
        index_ref[:, LANES - 8 :] = jnp.zeros_like(index_ref[:, LANES - 8 :])
    sources = [jac_ref.at[0], jac_ref.at[1], jac_ref.at[2], lam_ref, mu_ref, dens_ref]
    for a, source in enumerate(sources):
        value_ref[a, 0:count, 0:NODES] = source[low : low + count, :]
    index_ref[0:count, 0:NODES] = conn_ref[low : low + count, :] & (LANES - 1)


def row_forces(low_row, part, disp_ref, disp_low, value_ref, index_ref, place_ref, first, grad, back, total_ref, total_low):
    upper = high_half((1, LANES))

    def paired(ref, *at):
        start = 2 * low_row - first
        return jnp.concatenate(
            [ref[(*at, pl.ds(start + odd, part, stride=2), slice(None))] for odd in range(2)],
            axis=0,
        )

    index, place = paired(index_ref), paired(place_ref)
    shifted = []
    at = low_row - disp_low
    for c in range(3):
        here = disp_ref[c, at : at + part, :]
        after = disp_ref[c, at + 1 : at + part + 1, :]
        shifted.append(
            lane_pick(jnp.concatenate([here, jnp.where(upper, here, after)], axis=0), index)
        )
    nodal = forces(
        shifted,
        [paired(value_ref, a) for a in range(3)],
        paired(value_ref, 3),
        paired(value_ref, 4),
        grad,
        back,
    )
    nodal.append(paired(value_ref, 5))
    at = low_row - total_low
    for c in range(4):
        spot = lane_pick(nodal[c], place)
        even, odd = spot[:part], spot[part:]
        total_ref[c, at : at + part, :] += even + jnp.where(upper, odd, 0.0)
        total_ref[c, at + 1 : at + part + 1, :] += jnp.where(upper, 0.0, odd)


def field_rows(source, low, count, out_ref):
    for j in range(count):
        row = (low + j) % ROWS
        for c in range(3):
            out_ref[c, j : j + 1, :] = source[
                c : c + 1, row * LANES : (row + 1) * LANES
            ]


EDGE = 8
HALF = 2 * GROUPS
WIDE = HALF + EDGE


def edge_kernel(
    axis,
    disp_in,
    jac_in,
    lam_in,
    mu_in,
    dens_in,
    conn_in,
    peer_in,
    grad_in,
    back_in,
    order_in,
    base_ref,
    spill_ref,
    sends0,
    sends1,
    value_ref,
    index_ref,
    place_ref,
    turned_ref,
    disp_ref,
    peer_rows_ref,
    staged_ref,
    total_ref,
    jac_ref,
    lam_ref,
    mu_ref,
    dens_ref,
    conn_ref,
    strip_ref,
    peer_ref,
    grad_ref,
    back_ref,
    sems,
):
    first = FIRST if axis == "dev" else FIRST + HALF
    low_row = first - EDGE
    count = 2 * WIDE
    part = pl.ds(2 * low_row, count)
    pairs = [
        (conn_in.at[part, :], conn_ref),
        (disp_in.at[:, pl.ds(low_row * LANES, WIDE * LANES)], strip_ref.at[:, 0 : WIDE * LANES]),
        (
            disp_in.at[:, pl.ds((low_row + WIDE) % ROWS * LANES, LANES)],
            strip_ref.at[:, WIDE * LANES : (WIDE + 1) * LANES],
        ),
        (grad_in, grad_ref),
        (jac_in.at[:, part, :], jac_ref),
        (lam_in.at[part, :], lam_ref),
        (mu_in.at[part, :], mu_ref),
        (dens_in.at[part, :], dens_ref),
        (back_in, back_ref),
        (peer_in, peer_ref),
    ]
    copies = [
        pltpu.make_async_copy(source, target, sems.at[i])
        for i, (source, target) in enumerate(pairs)
    ]
    for copy in copies:
        copy.start()
    index_ref[...] = jnp.zeros_like(index_ref)
    total_ref[...] = jnp.zeros_like(total_ref)
    for copy in copies:
        copy.wait()
    for j in range(WIDE + 1):
        for c in range(3):
            disp_ref[c, j : j + 1, :] = strip_ref[c : c + 1, j * LANES : (j + 1) * LANES]
    peer_maps(peer_ref, 0 if axis == "dev" else 2, peer_rows_ref)
    element_rows(
        (jac_ref, lam_ref, mu_ref, dens_ref, conn_ref), 0, count, (value_ref, index_ref), True
    )
    place_ref[...] = inverse_rows(index_ref[...], turned_ref, NODES, LANES - 1)
    row_forces(
        low_row,
        WIDE,
        disp_ref,
        low_row,
        value_ref,
        index_ref,
        place_ref,
        2 * low_row,
        grad_ref[...],
        back_ref[...],
        total_ref,
        low_row,
    )
    for c in range(4):
        base_ref[c] = total_ref[c, EDGE:WIDE, :]
        spill_ref[c] = total_ref[c, WIDE : WIDE + 8, :]
    send_pair(
        [base_ref[c] for c in range(4)],
        peer_rows_ref[...],
        odd_place(axis),
        staged_ref,
        (sends0, sends1),
    )


def inner_kernel(
    slots_ref,
    slot_row_ref,
    disp_in,
    veloc_in,
    jac_ref,
    lam_ref,
    mu_ref,
    dens_ref,
    conn_ref,
    peer_ref,
    spill_in,
    grad_ref,
    back_ref,
    veloc_ref,
    base_ref,
    fixed_ref,
    index_out,
    spread_ref,
    peer_index_ref,
    value_ref,
    index_ref,
    place_ref,
    turned_ref,
    disp_ref,
    peer_rows_ref,
    total_ref,
    spread_wide_ref,
):
    field_rows(disp_in, 0, FIRST + 1, disp_ref)
    field_rows(veloc_in, 0, ROWS, veloc_ref)
    index_ref[...] = jnp.zeros_like(index_ref)
    element_rows(
        (jac_ref, lam_ref, mu_ref, dens_ref, conn_ref), 0, ELEM, (value_ref, index_ref), True
    )
    value_ref[:, ELEM:, :] = jnp.zeros_like(value_ref[:, ELEM:, :])
    for s in range(FCAP):
        e = slots_ref[s]
        for a in range(5):
            fixed_ref[a, s : s + 1, :] = value_ref[a, pl.ds(e, 1), :]
        index_out[0, s : s + 1, :] = index_ref[pl.ds(e, 1), :]
    tail = ELEM // 2 - LANES
    place_ref[0:LANES, :] = inverse_rows(index_ref[0:LANES, :], turned_ref, NODES, LANES - 1)
    both = jnp.concatenate(
        [
            index_ref[LANES : LANES + tail, :],
            index_out[0],
            jnp.zeros((LANES - tail - FCAP, LANES), jnp.int32),
        ],
        axis=0,
    )
    found = inverse_rows(both, turned_ref, NODES, LANES - 1)
    place_ref[LANES : LANES + tail, :] = found[0:tail]
    index_out[1] = found[tail : tail + FCAP]
    for half in range(2):
        peer_maps(peer_ref, 2 * half, peer_rows_ref.at[pl.ds(half * HALF, HALF), :])
    peer_rows_ref[SHARED:, :] = jnp.zeros((LANES - SHARED, LANES), jnp.int32)
    peer_index_ref[0] = peer_rows_ref[0:SHARED, :]
    peer_index_ref[1] = inverse_rows(peer_rows_ref[...], turned_ref, LANES, 0)[0:SHARED]
    rows = lax.broadcasted_iota(jnp.int32, (ROWS, FCAP), 0)
    slot_row = slot_row_ref[...]
    second = lax.shift_right_logical(slot_row + 1, 1)
    second = jnp.where(second == ROWS, 0, second)
    spread_wide_ref[...] = jnp.zeros_like(spread_wide_ref)
    spread_wide_ref[:, 0:FCAP] = jnp.where(
        lax.shift_right_logical(slot_row, 1) == rows, 1.0, 0.0
    )
    spread_wide_ref[:, LANES : LANES + FCAP] = jnp.where(second == rows, 1.0, 0.0)
    spread_ref[...] = spread_wide_ref[...].astype(jnp.bfloat16)
    total_ref[...] = jnp.zeros_like(total_ref)
    for c in range(4):
        total_ref[c, 0:1, :] = spill_in[c, 0:1, :]
    for low_row in (0, HALF):
        row_forces(
            low_row,
            HALF,
            disp_ref,
            0,
            value_ref,
            index_ref,
            place_ref,
            0,
            grad_ref[...],
            back_ref[...],
            total_ref,
            0,
        )
    for c in range(4):
        base_ref[c] = total_ref[c, 0:FIRST, :]


def received_rows(arrived, channels, peer_index_ref, staged_ref):
    dev = received_pair(
        arrived[:2], channels, peer_index_ref[1, 0:HALF, :], odd_place("dev"), staged_ref
    )
    region = received_pair(
        arrived[2:], channels, peer_index_ref[1, HALF:, :], odd_place("region"), staged_ref
    )
    return [jnp.concatenate([d, r], axis=0) for d, r in zip(dev, region)]


def whole_base(c, inner_ref, dev_ref, region_ref):
    return jnp.concatenate([inner_ref[c], dev_ref[c], region_ref[c]], axis=0)


def middle_kernel(
    opening,
    slots_ref,
    moved_ref,
    veloc_ref,
    inner_ref,
    dev_ref,
    region_ref,
    summed_ref,
    inverse_ref,
    fixed_ref,
    index_ref,
    spread_ref,
    peer_index_ref,
    got0,
    got1,
    got2,
    got3,
    grad_ref,
    back_ref,
    moved_out,
    veloc_out,
    summed_out,
    *rest,
):
    if opening:
        inverse_out, sends0, sends1, sends2, sends3, window_ref, staged_ref = rest
    else:
        sends0, sends1, sends2, sends3, window_ref, staged_ref = rest
    placed = received_rows(
        (got0, got1, got2, got3), 4 if opening else 3, peer_index_ref, staged_ref
    )
    if opening:
        mass = whole_base(3, inner_ref, dev_ref, region_ref)
        inverse_out[0:FIRST, :] = 1.0 / mass[:FIRST]
        inverse_out[FIRST:, :] = 1.0 / (mass[FIRST:] + placed[3])
        inverse_mass = inverse_out[...]
    else:
        inverse_mass = inverse_ref[...]
    base = [whole_base(c, inner_ref, dev_ref, region_ref) for c in range(3)]
    for c in range(3):
        local = base[c] if opening else summed_ref[c]
        force = jnp.concatenate([local[:FIRST], local[FIRST:] + placed[c]], axis=0)
        v = veloc_ref[c] - STEP * (inverse_mass * force)
        moved = STEP * v if opening else moved_ref[c, 0:ROWS, :] + STEP * v
        moved_out[c, 0:ROWS, :] = moved
        moved_out[c, ROWS:PAD_ROWS, :] = jnp.broadcast_to(moved[0:1], (PAD_ROWS - ROWS, LANES))
        veloc_out[c] = v
    fine = fine_local(
        moved_out,
        slots_ref,
        window_ref,
        [fixed_ref[a] for a in range(5)] + [index_ref[a] for a in range(2)],
        spread_ref[...],
        grad_ref[...],
        back_ref[...],
    )
    for c in range(3):
        summed_out[c] = base[c] + fine[:, c * LANES : (c + 1) * LANES]
    for axis, at, outs in (("dev", 0, (sends0, sends1)), ("region", HALF, (sends2, sends3))):
        send_pair(
            [summed_out[c, FIRST + at : FIRST + at + HALF, :] for c in range(3)],
            peer_index_ref[0, at : at + HALF, :],
            odd_place(axis),
            staged_ref,
            outs,
        )


def last_kernel(
    disp_in,
    moved_ref,
    veloc_ref,
    summed_ref,
    inverse_ref,
    peer_index_ref,
    got0,
    got1,
    got2,
    got3,
    disp_out,
    veloc_out,
    staged_ref,
    rows_ref,
):
    placed = received_rows((got0, got1, got2, got3), 3, peer_index_ref, staged_ref)
    for c in range(3):
        force = jnp.concatenate(
            [summed_ref[c, :FIRST, :], summed_ref[c, FIRST:, :] + placed[c]], axis=0
        )
        v = veloc_ref[c] - STEP * (inverse_ref[...] * force)
        rows_ref[0, c] = moved_ref[c, 0:ROWS, :] + STEP * v
        rows_ref[1, c] = v
    for j in range(ROWS):
        cols = slice(j * LANES, (j + 1) * LANES)
        for c in range(3):
            disp_out[c : c + 1, cols] = disp_in[c : c + 1, cols] + rows_ref[0, c, j : j + 1, :]
            veloc_out[c : c + 1, cols] = rows_ref[1, c, j : j + 1, :]


def swap_pairs(count, colour):
    pairs = []
    for low in range(colour, count, 2):
        high = (low + 1) % count
        pairs += [(low, high), (high, low)]
    return pairs


def swap_all(sends, axis):
    return [
        lax.ppermute(sent, axis, swap_pairs(lax.axis_size(axis), colour))
        for colour, sent in enumerate(sends)
    ]


def shape(dims, kind=jnp.float32):
    return jax.ShapeDtypeStruct(dims, kind)


def scratch(*dims, kind=jnp.float32):
    return pltpu.VMEM(dims, kind)


PARAMS = pltpu.CompilerParams(vmem_limit_bytes=48 * 1024 * 1024)
ALONE = pltpu.CompilerParams(vmem_limit_bytes=62 * 1024 * 1024)


def body(
    disp_start,
    veloc_start,
    jacobian,
    lame_lambda,
    lame_mu,
    density,
    connect,
    fine_slots,
    peer_nodes,
):
    grad_np, back_np = slope_operands()
    grad, back = jnp.asarray(grad_np), jnp.asarray(back_np)
    scalar = pl.BlockSpec(memory_space=pltpu.SMEM)
    vector = pl.BlockSpec(memory_space=pltpu.VMEM)
    field = shape((3, ROWS, LANES))
    padded = shape((3, PAD_ROWS, LANES))
    elements = (
        jnp.transpose(jacobian, (0, 2, 1)),
        lame_lambda.T,
        lame_mu.T,
        density.T,
        connect.T,
    )

    def sends(channels, count):
        return [shape((channels * GROUPS, LANES))] * count

    got, bases = [], []
    raw = pl.BlockSpec(memory_space=pltpu.HBM)
    order = peer_nodes
    count = 2 * WIDE
    for axis in ("dev", "region"):
        base, spill, send0, send1 = pl.pallas_call(
            functools.partial(edge_kernel, axis),
            in_specs=[raw] * 9 + [pl.BlockSpec(memory_space=pl.ANY)],
            out_shape=[shape((4, HALF, LANES)), shape((4, 8, LANES))] + sends(4, 2),
            out_specs=[vector] * 4,
            scratch_shapes=[
                scratch(6, LANES, LANES),
                scratch(LANES, LANES, kind=jnp.int32),
                scratch(LANES, LANES, kind=jnp.int32),
                scratch(LANES, LANES),
                scratch(3, WIDE + 8, LANES),
                scratch(HALF, LANES, kind=jnp.int32),
                scratch(4, HALF, LANES),
                scratch(4, WIDE + 8, LANES),
                scratch(3, count, NODES),
                scratch(count, NODES),
                scratch(count, NODES),
                scratch(count, NODES),
                scratch(count, NODES, kind=jnp.int32),
                scratch(3, (WIDE + 1) * LANES),
                scratch(4, GROUPS * LANES, kind=jnp.int32),
                scratch(*grad_np.shape, kind=jnp.bfloat16),
                scratch(*back_np.shape, kind=jnp.bfloat16),
                pltpu.SemaphoreType.DMA((10,)),
            ],
            compiler_params=PARAMS,
            name="edge_" + axis,
        )(*[pltpu.with_memory_space_constraint(x, pltpu.HBM) for x in (disp_start, *elements, peer_nodes, grad, back)], order)
        order = spill
        got += swap_all((send0, send1), axis)
        bases.append(base)
    veloc, inner, fixed, index, spread, peer_index = pl.pallas_call(
        inner_kernel,
        in_specs=[scalar] + [vector] * 12,
        out_shape=[
            field,
            shape((4, FIRST, LANES)),
            shape((5, FCAP, LANES)),
            shape((2, FCAP, LANES), jnp.int32),
            shape((ROWS, 2 * LANES), jnp.bfloat16),
            shape((2, SHARED, LANES), jnp.int32),
        ],
        out_specs=[vector] * 6,
        scratch_shapes=[
            scratch(6, ELEM + 8, LANES),
            scratch(ELEM + 8, LANES, kind=jnp.int32),
            scratch(ELEM // 2, LANES, kind=jnp.int32),
            scratch(LANES, LANES),
            scratch(3, FIRST + 8, LANES),
            scratch(LANES, LANES, kind=jnp.int32),
            scratch(4, FIRST + 8, LANES),
            scratch(ROWS, 2 * LANES),
        ],
        compiler_params=PARAMS,
        name="inner",
    )(
        fine_slots,
        fine_slots.reshape(1, FCAP),
        disp_start,
        veloc_start,
        *elements,
        peer_nodes,
        spill,
        grad,
        back,
    )
    inverse_mass, moved, summed = peer_index, peer_index, peer_index
    for substep in range(SUBSTEPS - 1):
        opening = substep == 0
        extra = [shape((ROWS, LANES))] if opening else []
        outs = pl.pallas_call(
            functools.partial(middle_kernel, opening),
            in_specs=[scalar] + [vector] * 17,
            out_shape=[padded, field, field] + extra + sends(3, 4),
            out_specs=[vector] * (7 + len(extra)),
            scratch_shapes=[
                scratch(3, FCAP, LANES),
                scratch(4, HALF, LANES),
            ],
            compiler_params=PARAMS,
            name="middle",
        )(
            fine_slots,
            moved,
            veloc,
            inner,
            *bases,
            summed,
            inverse_mass,
            fixed,
            index,
            spread,
            peer_index,
            *got,
            grad,
            back,
        )
        moved, veloc, summed = outs[:3]
        if opening:
            inverse_mass = outs[3]
        got = swap_all(outs[-4:-2], "dev") + swap_all(outs[-2:], "region")
    return pl.pallas_call(
        last_kernel,
        in_specs=[vector] * 10,
        out_shape=[shape((3, NLOC)), shape((3, NLOC))],
        out_specs=[vector] * 2,
        scratch_shapes=[
            scratch(4, HALF, LANES),
            scratch(2, 3, ROWS, LANES),
        ],
        compiler_params=PARAMS,
        name="last",
    )(disp_start, moved, veloc, summed, inverse_mass, peer_index, *got)


def solution(mesh):
    in_specs = (
        P(None, ("region", "dev")),
        P(None, ("region", "dev")),
        P(None, None, ("region", "dev")),
        P(None, ("region", "dev")),
        P(None, ("region", "dev")),
        P(None, ("region", "dev")),
        P(None, ("region", "dev")),
        P(("region", "dev")),
        P(None, ("region", "dev")),
    )
    out_specs = (P(None, ("region", "dev")), P(None, ("region", "dev")))
    return jax.shard_map(body, mesh=mesh, in_specs=in_specs, out_specs=out_specs, check_vma=False)
```

time: 73.4 us -> 66.5 us (0.906)
  starting transfers between devices: 36.6 us -> 28.4 us
  waiting for transfers between devices: 16 us -> 20.4 us
  local copies, waits for them, and re-layouts: 3.47 us -> 0.62 us
    ppermute x16, starting transfers between devices: 36.6 us -> 28.4 us  [swap_all(): lax.ppermute(sent, axis, swap_pairs(lax.axis_size(axis), colour))]
    ppermute x16, waiting for transfers between devices: 16 us -> 20.4 us  [swap_all(): lax.ppermute(sent, axis, swap_pairs(lax.axis_size(axis), colour))]
    unnamed x25 -> x22, local copies, waits for them, and re-layouts: 3.47 us -> 0.62 us
    pallas_call x5 -> x7, Pallas kernels: 16.5 us -> 16.1 us  [the longest x3 6.12 us: body(): pl.pallas_call(functools.partial(middle_kernel, opening), in_specs=[scala...]
  transfers between devices with their start and end apart: 16 -> 16, of which waited for: 5 -> 3; matrix products, arithmetic and copies ran while one was open for 0% -> 0% of each run, Pallas kernels for 0% -> 9%
where the time goes in v1:
time: 66.5 us; the launch traced here: 66.4 us
  starting transfers between devices  28.4 us (43%)
  waiting for transfers between devices  20.4 us (31%)
  Pallas kernels  16.1 us (24%)
  between operations  0.85 us (1%)
    ppermute x16, starting transfers between devices, swap_all(): lax.ppermute(sent, axis, swap_pairs(lax.axis_size(axis), colour))  28.4 us
    ppermute x16, waiting for transfers between devices, swap_all(): lax.ppermute(sent, axis, swap_pairs(lax.axis_size(axis), colour))  20.4 us
    pallas_call x3, Pallas kernels, body(): pl.pallas_call(functools.partial(middle_kernel, opening), in_specs=[scala...  6.12 us
    pallas_call x2, Pallas kernels, body(): pl.pallas_call(functools.partial(edge_kernel, axis), in_specs=[raw] * 9 +...  5.4 us
    pallas_call x1, Pallas kernels, body(): pl.pallas_call(inner_kernel, in_specs=[scalar] + [vector] * 12, out_shape...  3.17 us
    pallas_call x1, Pallas kernels, body(): pl.pallas_call(last_kernel, in_specs=[vector] * 10, out_shape=[shape((3,...  1.42 us
  transfers between devices with their start and end apart: 16, of which 3 were waited for; matrix products, arithmetic and copies ran while one was open for 0% of the time, Pallas kernels for 9%

profile of v1, /device:TPU:0, one launch (start us, length us, event | category | flops | bytes accessed | tf_op | source)
XLA Modules:
  0.0 66.4 jit_solution(15190311134313891429)
XLA Ops:
  0.6 2.7 %edge_dev.1 = (f32[4,40,128]{2,1,0:T(8,128)S(1)}, f32[4,8,128]{2,1,0:T(8,128)S(1)}, f32[80,128]{1,0:T(8,128)S(1)}, f32[80,128]{1,0:T(8,128)S(1)}) custom-call(f32[3,20480]{1,0:T(4,128)} %disp_in.7, f32[3,320,125]{2,1,0:T(8,128)} %bitcast.6, f32[320,125]{1,0:T(8,128)} %bitcast.9, f32[320,125]{1,0:T(8,128)} %bitcast.12, f32[320,125]{1,0:T(8,128)} %bitcast.15, ...), custom_call_target="tpu_custom_call" | custom-call | tf_op jit(solution)/shard_map/edge_dev/pallas_call | solution.py:613
  3.3 0.1 collective-permute-start
  3.4 10.2 %collective-permute-start.1 = (f32[80,128]{1,0:T(8,128)S(1)}, f32[80,128]{1,0:T(8,128)S(1)}, u32[]{:S(2)}, u32[]{:S(2)}) collective-permute-start(f32[80,128]{1,0:T(8,128)S(1)} %get-tuple-element.49), channel_id=1, source_target_pairs={{1,2},{2,1},{3,4},{4,3},{5,6},{6,5},{7,8},{8,7},{9,10},{10,9},{11,... | collective-permute-start | bytes 122888 | tf_op jit(solution)/shard_map/ppermute | solution.py:563
  13.6 0.0 copy-start.4
  13.6 0.0 copy-start.5
  13.7 0.0 copy-start.6
  13.7 0.0 copy-start.7
  13.7 0.0 copy-start.8
  13.7 2.7 %edge_region.1 = (f32[4,40,128]{2,1,0:T(8,128)S(1)}, f32[4,8,128]{2,1,0:T(8,128)S(1)}, f32[80,128]{1,0:T(8,128)S(1)}, f32[80,128]{1,0:T(8,128)S(1)}) custom-call(f32[3,20480]{1,0:T(4,128)} %disp_in.7, f32[3,320,125]{2,1,0:T(8,128)} %bitcast.7, f32[320,125]{1,0:T(8,128)} %bitcast.10, f32[320,125]{1,0:T(8,128)} %bitcast.13, f32[320,125]{1,0:T(8,128)} %bitcast.16, ...), custom_call_target="tpu_custom_call" | custom-call | tf_op jit(solution)/shard_map/edge_region/pallas_call | solution.py:613
  16.4 1.1 %collective-permute-start.2 = (f32[80,128]{1,0:T(8,128)S(1)}, f32[80,128]{1,0:T(8,128)S(1)}, u32[]{:S(2)}, u32[]{:S(2)}) collective-permute-start(f32[80,128]{1,0:T(8,128)S(1)} %get-tuple-element.50), channel_id=1, source_target_pairs={{0,64},{64,0},{128,192},{192,128},{1,65},{65,1},{129,193},{193,129... | collective-permute-start | bytes 122888 | tf_op jit(solution)/shard_map/ppermute | solution.py:563
  17.5 1.9 %collective-permute-start.3 = (f32[80,128]{1,0:T(8,128)S(1)}, f32[80,128]{1,0:T(8,128)S(1)}, u32[]{:S(2)}, u32[]{:S(2)}) collective-permute-start(f32[80,128]{1,0:T(8,128)S(1)} %get-tuple-element.51), channel_id=1, source_target_pairs={{64,128},{128,64},{192,0},{0,192},{65,129},{129,65},{193,1},{1,193... | collective-permute-start | bytes 122888 | tf_op jit(solution)/shard_map/ppermute | solution.py:563
  19.5 0.6 copy-done.10
  20.1 3.2 %inner.1 = (f32[3,160,128]{2,1,0:T(8,128)S(1)}, f32[4,80,128]{2,1,0:T(8,128)S(1)}, f32[5,80,128]{2,1,0:T(8,128)S(1)}, s32[2,80,128]{2,1,0:T(8,128)S(1)}, bf16[16...) custom-call(s32[80]{0:T(128)S(1)} %copy-done.10, s32[1,80]{1,0:T(1,128)S(1)} %bitcast.21, f32[3,20480]{1,0:T(4,128)S(1)} %copy-done.2, ...), custom_call_target="tpu_custom_call" | custom-call | tf_op jit(solution)/shard_map/inner/pallas_call | solution.py:644
  23.3 0.0 collective-permute-done.got0
  23.3 0.0 collective-permute-done.3.got3
  23.3 2.1 %middle.3 = (f32[3,168,128]{2,1,0:T(8,128)S(1)}, f32[3,160,128]{2,1,0:T(8,128)S(1)}, f32[3,160,128]{2,1,0:T(8,128)S(1)}, f32[160,128]{1,0:T(8,128)S(1)}, f32[60,...) custom-call(s32[80]{0:T(128)S(1)} %copy-done.10, ...), custom_call_target="tpu_custom_call" | custom-call | tf_op jit(solution)/shard_map/middle/pallas_call | solution.py:683
  25.4 0.1 collective-permute-start.4
  25.5 1.9 %collective-permute-start.5 = (f32[60,128]{1,0:T(8,128)S(1)}, f32[60,128]{1,0:T(8,128)S(1)}, u32[]{:S(2)}, u32[]{:S(2)}) collective-permute-start(f32[60,128]{1,0:T(8,128)S(1)} %get-tuple-element.57), channel_id=1, source_target_pairs={{1,2},{2,1},{3,4},{4,3},{5,6},{6,5},{7,8},{8,7},{9,10},{10,9},{11,... | collective-permute-start | bytes 92168 | tf_op jit(solution)/shard_map/ppermute | solution.py:563
  27.4 1.0 %collective-permute-start.6 = (f32[60,128]{1,0:T(8,128)S(1)}, f32[60,128]{1,0:T(8,128)S(1)}, u32[]{:S(2)}, u32[]{:S(2)}) collective-permute-start(f32[60,128]{1,0:T(8,128)S(1)} %get-tuple-element.58), channel_id=1, source_target_pairs={{0,64},{64,0},{128,192},{192,128},{1,65},{65,1},{129,193},{193,129... | collective-permute-start | bytes 92168 | tf_op jit(solution)/shard_map/ppermute | solution.py:563
  28.4 1.9 %collective-permute-start.7 = (f32[60,128]{1,0:T(8,128)S(1)}, f32[60,128]{1,0:T(8,128)S(1)}, u32[]{:S(2)}, u32[]{:S(2)}) collective-permute-start(f32[60,128]{1,0:T(8,128)S(1)} %get-tuple-element.59), channel_id=1, source_target_pairs={{64,128},{128,64},{192,0},{0,192},{65,129},{129,65},{193,1},{1,193... | collective-permute-start | bytes 92168 | tf_op jit(solution)/shard_map/ppermute | solution.py:563
  30.4 6.8 %collective-permute-done.5.got1 = f32[60,128]{1,0:T(8,128)S(1)} collective-permute-done((f32[60,128]{1,0:T(8,128)S(1)}, f32[60,128]{1,0:T(8,128)S(1)}, u32[]{:S(2)}, u32[]{:S(2)}) %collective-permute-start.5) | collective-permute-done | bytes 30752 | tf_op jit(solution)/shard_map/ppermute | solution.py:563
  37.2 2.0 %middle.4 = (f32[3,168,128]{2,1,0:T(8,128)S(1)}, f32[3,160,128]{2,1,0:T(8,128)S(1)}, f32[3,160,128]{2,1,0:T(8,128)S(1)}, f32[60,128]{1,0:T(8,128)S(1)}, f32[60,1...) custom-call(s32[80]{0:T(128)S(1)} %copy-done.10, f32[3,168,128]{2,1,0:T(8,128)S(1)} %get-tuple-element.52.moved_ref, ...), custom_call_target="tpu_custom_call" | custom-call | tf_op jit(solution)/shard_map/middle/pallas_call | solution.py:683
  39.2 0.1 collective-permute-start.8
  39.3 3.1 %collective-permute-start.9 = (f32[60,128]{1,0:T(8,128)S(1)}, f32[60,128]{1,0:T(8,128)S(1)}, u32[]{:S(2)}, u32[]{:S(2)}) collective-permute-start(f32[60,128]{1,0:T(8,128)S(1)} %get-tuple-element.64), channel_id=1, source_target_pairs={{1,2},{2,1},{3,4},{4,3},{5,6},{6,5},{7,8},{8,7},{9,10},{10,9},{11,... | collective-permute-start | bytes 92168 | tf_op jit(solution)/shard_map/ppermute | solution.py:563
  42.4 1.9 %collective-permute-start.11 = (f32[60,128]{1,0:T(8,128)S(1)}, f32[60,128]{1,0:T(8,128)S(1)}, u32[]{:S(2)}, u32[]{:S(2)}) collective-permute-start(f32[60,128]{1,0:T(8,128)S(1)} %get-tuple-element.66), channel_id=1, source_target_pairs={{64,128},{128,64},{192,0},{0,192},{65,129},{129,65},{193,1},{1,193... | collective-permute-start | bytes 92168 | tf_op jit(solution)/shard_map/ppermute | solution.py:563
  44.4 6.8 %collective-permute-done.9.got1 = f32[60,128]{1,0:T(8,128)S(1)} collective-permute-done((f32[60,128]{1,0:T(8,128)S(1)}, f32[60,128]{1,0:T(8,128)S(1)}, u32[]{:S(2)}, u32[]{:S(2)}) %collective-permute-start.9) | collective-permute-done | bytes 30752 | tf_op jit(solution)/shard_map/ppermute | solution.py:563
  51.2 2.0 %middle.5 = (f32[3,168,128]{2,1,0:T(8,128)S(1)}, f32[3,160,128]{2,1,0:T(8,128)S(1)}, f32[3,160,128]{2,1,0:T(8,128)S(1)}, f32[60,128]{1,0:T(8,128)S(1)}, f32[60,1...) custom-call(s32[80]{0:T(128)S(1)} %copy-done.10, f32[3,168,128]{2,1,0:T(8,128)S(1)} %get-tuple-element.60.moved_ref, ...), custom_call_target="tpu_custom_call" | custom-call | tf_op jit(solution)/shard_map/middle/pallas_call | solution.py:683
  53.2 0.1 collective-permute-start.12
  53.3 3.0 %collective-permute-start.13 = (f32[60,128]{1,0:T(8,128)S(1)}, f32[60,128]{1,0:T(8,128)S(1)}, u32[]{:S(2)}, u32[]{:S(2)}) collective-permute-start(f32[60,128]{1,0:T(8,128)S(1)} %get-tuple-element.71), channel_id=1, source_target_pairs={{1,2},{2,1},{3,4},{4,3},{5,6},{6,5},{7,8},{8,7},{9,10},{10,9},{11,... | collective-permute-start | bytes 92168 | tf_op jit(solution)/shard_map/ppermute | solution.py:563
  56.3 1.9 %collective-permute-start.15 = (f32[60,128]{1,0:T(8,128)S(1)}, f32[60,128]{1,0:T(8,128)S(1)}, u32[]{:S(2)}, u32[]{:S(2)}) collective-permute-start(f32[60,128]{1,0:T(8,128)S(1)} %get-tuple-element.73), channel_id=1, source_target_pairs={{64,128},{128,64},{192,0},{0,192},{65,129},{129,65},{193,1},{1,193... | collective-permute-start | bytes 92168 | tf_op jit(solution)/shard_map/ppermute | solution.py:563
  58.2 6.8 %collective-permute-done.13.got1 = f32[60,128]{1,0:T(8,128)S(1)} collective-permute-done((f32[60,128]{1,0:T(8,128)S(1)}, f32[60,128]{1,0:T(8,128)S(1)}, u32[]{:S(2)}, u32[]{:S(2)}) %collective-permute-start.13) | collective-permute-done | bytes 30752 | tf_op jit(solution)/shard_map/ppermute | solution.py:563
  65.0 1.4 %last.1 = (f32[3,20480]{1,0:T(4,128)}, f32[3,20480]{1,0:T(4,128)}) custom-call(f32[3,20480]{1,0:T(4,128)S(1)} %copy-done.2, f32[3,168,128]{2,1,0:T(8,128)S(1)} %get-tuple-element.67.moved_ref, f32[3,160,128]{2,1,0:T(8,128)S(1)} %get-tuple-element.68.veloc_ref, f32[3,160,128]{2,1,0:T(8,128)S(1)} %get-tuple-element.69.summed_ref, ...), custom_call_target="tpu_custom_call" | custom-call | tf_op jit(solution)/shard_map/last/pallas_call | solution.py:714
  (29 shorter events, 0.1 us)
Async XLA Ops:
  0.6 18.8 %copy-start.9 = (f32[3,20480]{1,0:T(4,128)S(1)}, f32[3,20480]{1,0:T(4,128)}, u32[]{:S(2)}) copy-start(f32[3,20480]{1,0:T(4,128)} %veloc_in.1) | copy-start | bytes 737284
  3.3 20.0 %collective-permute-start = (f32[80,128]{1,0:T(8,128)S(1)}, f32[80,128]{1,0:T(8,128)S(1)}, u32[]{:S(2)}, u32[]{:S(2)}) collective-permute-start(f32[80,128]{1,0:T(8,128)S(1)} %get-tuple-element.48), channel_id=1, source_target_pairs={{0,1},{1,0},{2,3},{3,2},{4,5},{5,4},{6,7},{7,6},{8,9},{9,8},{10,11... | collective-permute-start | bytes 122888 | tf_op jit(solution)/shard_map/ppermute | solution.py:563
  3.4 19.9 %collective-permute-start.1 = (f32[80,128]{1,0:T(8,128)S(1)}, f32[80,128]{1,0:T(8,128)S(1)}, u32[]{:S(2)}, u32[]{:S(2)}) collective-permute-start(f32[80,128]{1,0:T(8,128)S(1)} %get-tuple-element.49), channel_id=1, source_target_pairs={{1,2},{2,1},{3,4},{4,3},{5,6},{6,5},{7,8},{8,7},{9,10},{10,9},{11,... | collective-permute-start | bytes 122888 | tf_op jit(solution)/shard_map/ppermute | solution.py:563
  13.6 5.8 %copy-start = (bf16[1152,128]{1,0:T(8,128)(2,1)S(1)}, bf16[1152,128]{1,0:T(8,128)(2,1)}, u32[]{:S(2)}) copy-start(bf16[1152,128]{1,0:T(8,128)(2,1)} %constant.5.clone.back_in.back_ref) | copy-start | bytes 884740
  13.6 5.8 %copy-start.1 = (bf16[384,384]{1,0:T(8,128)(2,1)S(1)}, bf16[384,384]{1,0:T(8,128)(2,1)}, u32[]{:S(2)}) copy-start(bf16[384,384]{1,0:T(8,128)(2,1)} %constant.4.clone.grad_in.grad_ref) | copy-start | bytes 884740
  13.6 5.8 %copy-start.2 = (f32[3,20480]{1,0:T(4,128)S(1)}, f32[3,20480]{1,0:T(4,128)}, u32[]{:S(2)}) copy-start(f32[3,20480]{1,0:T(4,128)} %disp_in.7) | copy-start | bytes 737284
  13.6 5.9 %copy-start.3 = (f32[3,125,320]{1,2,0:T(8,128)S(1)}, f32[3,125,320]{1,2,0:T(8,128)}, u32[]{:S(2)}) copy-start(f32[3,125,320]{1,2,0:T(8,128)} %param.13) | copy-start | bytes 1440004
  13.6 5.9 %copy-start.4 = (f32[125,320]{0,1:T(8,128)S(1)}, f32[125,320]{0,1:T(8,128)}, u32[]{:S(2)}) copy-start(f32[125,320]{0,1:T(8,128)} %param.14) | copy-start | bytes 480004
  13.6 5.9 %copy-start.5 = (f32[125,320]{0,1:T(8,128)S(1)}, f32[125,320]{0,1:T(8,128)}, u32[]{:S(2)}) copy-start(f32[125,320]{0,1:T(8,128)} %param.15) | copy-start | bytes 480004
  13.7 5.9 %copy-start.6 = (f32[125,320]{0,1:T(8,128)S(1)}, f32[125,320]{0,1:T(8,128)}, u32[]{:S(2)}) copy-start(f32[125,320]{0,1:T(8,128)} %param.16) | copy-start | bytes 480004
  13.7 5.9 %copy-start.7 = (s32[125,320]{0,1:T(8,128)S(1)}, s32[125,320]{0,1:T(8,128)}, u32[]{:S(2)}) copy-start(s32[125,320]{0,1:T(8,128)} %param.17) | copy-start | bytes 480004
  13.7 5.8 %copy-start.8 = (s32[4,2560]{1,0:T(4,128)S(1)}, s32[4,2560]{1,0:T(4,128)}, u32[]{:S(2)}) copy-start(s32[4,2560]{1,0:T(4,128)} %peer_ref.1) | copy-start | bytes 122884
  16.4 6.9 %collective-permute-start.2 = (f32[80,128]{1,0:T(8,128)S(1)}, f32[80,128]{1,0:T(8,128)S(1)}, u32[]{:S(2)}, u32[]{:S(2)}) collective-permute-start(f32[80,128]{1,0:T(8,128)S(1)} %get-tuple-element.50), channel_id=1, source_target_pairs={{0,64},{64,0},{128,192},{192,128},{1,65},{65,1},{129,193},{193,129... | collective-permute-start | bytes 122888 | tf_op jit(solution)/shard_map/ppermute | solution.py:563
  17.5 5.8 %collective-permute-start.3 = (f32[80,128]{1,0:T(8,128)S(1)}, f32[80,128]{1,0:T(8,128)S(1)}, u32[]{:S(2)}, u32[]{:S(2)}) collective-permute-start(f32[80,128]{1,0:T(8,128)S(1)} %get-tuple-element.51), channel_id=1, source_target_pairs={{64,128},{128,64},{192,0},{0,192},{65,129},{129,65},{193,1},{1,193... | collective-permute-start | bytes 122888 | tf_op jit(solution)/shard_map/ppermute | solution.py:563
  19.5 0.7 copy-start.10
  25.4 5.0 %collective-permute-start.4 = (f32[60,128]{1,0:T(8,128)S(1)}, f32[60,128]{1,0:T(8,128)S(1)}, u32[]{:S(2)}, u32[]{:S(2)}) collective-permute-start(f32[60,128]{1,0:T(8,128)S(1)} %get-tuple-element.56), channel_id=1, source_target_pairs={{0,1},{1,0},{2,3},{3,2},{4,5},{5,4},{6,7},{7,6},{8,9},{9,8},{10,11... | collective-permute-start | bytes 92168 | tf_op jit(solution)/shard_map/ppermute | solution.py:563
  25.5 11.7 %collective-permute-start.5 = (f32[60,128]{1,0:T(8,128)S(1)}, f32[60,128]{1,0:T(8,128)S(1)}, u32[]{:S(2)}, u32[]{:S(2)}) collective-permute-start(f32[60,128]{1,0:T(8,128)S(1)} %get-tuple-element.57), channel_id=1, source_target_pairs={{1,2},{2,1},{3,4},{4,3},{5,6},{6,5},{7,8},{8,7},{9,10},{10,9},{11,... | collective-permute-start | bytes 92168 | tf_op jit(solution)/shard_map/ppermute | solution.py:563
  27.4 9.7 %collective-permute-start.6 = (f32[60,128]{1,0:T(8,128)S(1)}, f32[60,128]{1,0:T(8,128)S(1)}, u32[]{:S(2)}, u32[]{:S(2)}) collective-permute-start(f32[60,128]{1,0:T(8,128)S(1)} %get-tuple-element.58), channel_id=1, source_target_pairs={{0,64},{64,0},{128,192},{192,128},{1,65},{65,1},{129,193},{193,129... | collective-permute-start | bytes 92168 | tf_op jit(solution)/shard_map/ppermute | solution.py:563
  28.4 8.7 %collective-permute-start.7 = (f32[60,128]{1,0:T(8,128)S(1)}, f32[60,128]{1,0:T(8,128)S(1)}, u32[]{:S(2)}, u32[]{:S(2)}) collective-permute-start(f32[60,128]{1,0:T(8,128)S(1)} %get-tuple-element.59), channel_id=1, source_target_pairs={{64,128},{128,64},{192,0},{0,192},{65,129},{129,65},{193,1},{1,193... | collective-permute-start | bytes 92168 | tf_op jit(solution)/shard_map/ppermute | solution.py:563
  39.2 5.1 %collective-permute-start.8 = (f32[60,128]{1,0:T(8,128)S(1)}, f32[60,128]{1,0:T(8,128)S(1)}, u32[]{:S(2)}, u32[]{:S(2)}) collective-permute-start(f32[60,128]{1,0:T(8,128)S(1)} %get-tuple-element.63), channel_id=1, source_target_pairs={{0,1},{1,0},{2,3},{3,2},{4,5},{5,4},{6,7},{7,6},{8,9},{9,8},{10,11... | collective-permute-start | bytes 92168 | tf_op jit(solution)/shard_map/ppermute | solution.py:563
  39.3 11.8 %collective-permute-start.9 = (f32[60,128]{1,0:T(8,128)S(1)}, f32[60,128]{1,0:T(8,128)S(1)}, u32[]{:S(2)}, u32[]{:S(2)}) collective-permute-start(f32[60,128]{1,0:T(8,128)S(1)} %get-tuple-element.64), channel_id=1, source_target_pairs={{1,2},{2,1},{3,4},{4,3},{5,6},{6,5},{7,8},{8,7},{9,10},{10,9},{11,... | collective-permute-start | bytes 92168 | tf_op jit(solution)/shard_map/ppermute | solution.py:563
  42.4 8.7 %collective-permute-start.10 = (f32[60,128]{1,0:T(8,128)S(1)}, f32[60,128]{1,0:T(8,128)S(1)}, u32[]{:S(2)}, u32[]{:S(2)}) collective-permute-start(f32[60,128]{1,0:T(8,128)S(1)} %get-tuple-element.65), channel_id=1, source_target_pairs={{0,64},{64,0},{128,192},{192,128},{1,65},{65,1},{129,193},{193,129... | collective-permute-start | bytes 92168 | tf_op jit(solution)/shard_map/ppermute | solution.py:563
  42.4 8.7 %collective-permute-start.11 = (f32[60,128]{1,0:T(8,128)S(1)}, f32[60,128]{1,0:T(8,128)S(1)}, u32[]{:S(2)}, u32[]{:S(2)}) collective-permute-start(f32[60,128]{1,0:T(8,128)S(1)} %get-tuple-element.66), channel_id=1, source_target_pairs={{64,128},{128,64},{192,0},{0,192},{65,129},{129,65},{193,1},{1,193... | collective-permute-start | bytes 92168 | tf_op jit(solution)/shard_map/ppermute | solution.py:563
  53.2 5.0 %collective-permute-start.12 = (f32[60,128]{1,0:T(8,128)S(1)}, f32[60,128]{1,0:T(8,128)S(1)}, u32[]{:S(2)}, u32[]{:S(2)}) collective-permute-start(f32[60,128]{1,0:T(8,128)S(1)} %get-tuple-element.70), channel_id=1, source_target_pairs={{0,1},{1,0},{2,3},{3,2},{4,5},{5,4},{6,7},{7,6},{8,9},{9,8},{10,11... | collective-permute-start | bytes 92168 | tf_op jit(solution)/shard_map/ppermute | solution.py:563
  53.3 11.7 %collective-permute-start.13 = (f32[60,128]{1,0:T(8,128)S(1)}, f32[60,128]{1,0:T(8,128)S(1)}, u32[]{:S(2)}, u32[]{:S(2)}) collective-permute-start(f32[60,128]{1,0:T(8,128)S(1)} %get-tuple-element.71), channel_id=1, source_target_pairs={{1,2},{2,1},{3,4},{4,3},{5,6},{6,5},{7,8},{8,7},{9,10},{10,9},{11,... | collective-permute-start | bytes 92168 | tf_op jit(solution)/shard_map/ppermute | solution.py:563
  56.2 8.7 %collective-permute-start.14 = (f32[60,128]{1,0:T(8,128)S(1)}, f32[60,128]{1,0:T(8,128)S(1)}, u32[]{:S(2)}, u32[]{:S(2)}) collective-permute-start(f32[60,128]{1,0:T(8,128)S(1)} %get-tuple-element.72), channel_id=1, source_target_pairs={{0,64},{64,0},{128,192},{192,128},{1,65},{65,1},{129,193},{193,129... | collective-permute-start | bytes 92168 | tf_op jit(solution)/shard_map/ppermute | solution.py:563
  56.3 8.7 %collective-permute-start.15 = (f32[60,128]{1,0:T(8,128)S(1)}, f32[60,128]{1,0:T(8,128)S(1)}, u32[]{:S(2)}, u32[]{:S(2)}) collective-permute-start(f32[60,128]{1,0:T(8,128)S(1)} %get-tuple-element.73), channel_id=1, source_target_pairs={{64,128},{128,64},{192,0},{0,192},{65,129},{129,65},{193,1},{1,193... | collective-permute-start | bytes 92168 | tf_op jit(solution)/shard_map/ppermute | solution.py:563

commit v2 on v1

--- a/solution.py
+++ b/solution.py
@@ -185,16 +185,17 @@
             ] & (LANES - 1)
 
 
-def element_rows(refs, low, count, pads, clear):
-    jac_ref, lam_ref, mu_ref, dens_ref, conn_ref = refs
-    value_ref, index_ref = pads
-    if clear:
-        value_ref[:, :, LANES - 8 :] = jnp.zeros_like(value_ref[:, :, LANES - 8 :])
-        index_ref[:, LANES - 8 :] = jnp.zeros_like(index_ref[:, LANES - 8 :])
+def index_rows(conn_ref, low, count, index_ref):
+    index_ref[...] = jnp.zeros_like(index_ref)
+    index_ref[0:count, 0:NODES] = conn_ref[low : low + count, :] & (LANES - 1)
+
+
+def value_rows(refs, low, count, value_ref):
+    jac_ref, lam_ref, mu_ref, dens_ref = refs
+    value_ref[:, :, LANES - 8 :] = jnp.zeros_like(value_ref[:, :, LANES - 8 :])
     sources = [jac_ref.at[0], jac_ref.at[1], jac_ref.at[2], lam_ref, mu_ref, dens_ref]
     for a, source in enumerate(sources):
         value_ref[a, 0:count, 0:NODES] = source[low : low + count, :]
-    index_ref[0:count, 0:NODES] = conn_ref[low : low + count, :] & (LANES - 1)
 
 
 def row_forces(low_row, part, disp_ref, disp_low, value_ref, index_ref, place_ref, first, grad, back, total_ref, total_low):
@@ -247,78 +248,30 @@
 WIDE = HALF + EDGE
 
 
-def edge_kernel(
-    axis,
-    disp_in,
-    jac_in,
-    lam_in,
-    mu_in,
-    dens_in,
-    conn_in,
-    peer_in,
-    grad_in,
-    back_in,
-    order_in,
-    base_ref,
-    spill_ref,
-    sends0,
-    sends1,
-    value_ref,
-    index_ref,
-    place_ref,
-    turned_ref,
-    disp_ref,
-    peer_rows_ref,
-    staged_ref,
-    total_ref,
-    jac_ref,
-    lam_ref,
-    mu_ref,
-    dens_ref,
-    conn_ref,
-    strip_ref,
-    peer_ref,
-    grad_ref,
-    back_ref,
-    sems,
-):
+def edge_part(axis, ready, sources, outs, scratches):
+    disp_in, jac_ref, lam_ref, mu_ref, dens_ref, conn_ref, peer_ref, grad_ref, back_ref = sources
+    base_ref, spill_ref, sends0, sends1 = outs
+    (
+        value_ref,
+        index_ref,
+        place_ref,
+        turned_ref,
+        disp_ref,
+        peer_rows_ref,
+        staged_ref,
+        total_ref,
+    ) = scratches
     first = FIRST if axis == "dev" else FIRST + HALF
     low_row = first - EDGE
-    count = 2 * WIDE
-    part = pl.ds(2 * low_row, count)
-    pairs = [
-        (conn_in.at[part, :], conn_ref),
-        (disp_in.at[:, pl.ds(low_row * LANES, WIDE * LANES)], strip_ref.at[:, 0 : WIDE * LANES]),
-        (
-            disp_in.at[:, pl.ds((low_row + WIDE) % ROWS * LANES, LANES)],
-            strip_ref.at[:, WIDE * LANES : (WIDE + 1) * LANES],
-        ),
-        (grad_in, grad_ref),
-        (jac_in.at[:, part, :], jac_ref),
-        (lam_in.at[part, :], lam_ref),
-        (mu_in.at[part, :], mu_ref),
-        (dens_in.at[part, :], dens_ref),
-        (back_in, back_ref),
-        (peer_in, peer_ref),
-    ]
-    copies = [
-        pltpu.make_async_copy(source, target, sems.at[i])
-        for i, (source, target) in enumerate(pairs)
-    ]
-    for copy in copies:
-        copy.start()
-    index_ref[...] = jnp.zeros_like(index_ref)
     total_ref[...] = jnp.zeros_like(total_ref)
-    for copy in copies:
-        copy.wait()
-    for j in range(WIDE + 1):
-        for c in range(3):
-            disp_ref[c, j : j + 1, :] = strip_ref[c : c + 1, j * LANES : (j + 1) * LANES]
+    ready(0)
+    index_rows(conn_ref, 2 * low_row, 2 * WIDE, index_ref)
+    place_ref[...] = inverse_rows(index_ref[...], turned_ref, NODES, LANES - 1)
+    ready(1)
+    field_rows(disp_in, low_row, WIDE + 1, disp_ref)
     peer_maps(peer_ref, 0 if axis == "dev" else 2, peer_rows_ref)
-    element_rows(
-        (jac_ref, lam_ref, mu_ref, dens_ref, conn_ref), 0, count, (value_ref, index_ref), True
-    )
-    place_ref[...] = inverse_rows(index_ref[...], turned_ref, NODES, LANES - 1)
+    ready(2)
+    value_rows((jac_ref, lam_ref, mu_ref, dens_ref), 2 * low_row, 2 * WIDE, value_ref)
     row_forces(
         low_row,
         WIDE,
@@ -343,6 +296,50 @@
         staged_ref,
         (sends0, sends1),
     )
+
+
+def dev_edge_kernel(*refs):
+    raw, kept, outs, scratches = refs[:10], refs[10:20], refs[20:24], refs[24:32]
+    sems = refs[32]
+    disp_in, veloc_in, jac_in, lam_in, mu_in, dens_in, conn_in, peer_in, grad_in, back_in = raw
+    disp, veloc, jac, lam, mu, dens, conn, peer, grad, back = kept
+    low = 2 * (FIRST - EDGE)
+    mine, lower, upper = pl.ds(low, 2 * WIDE), pl.ds(0, low), pl.ds(low + 2 * WIDE, ELEM - low - 2 * WIDE)
+    steps = [
+        [(conn_in.at[mine, :], conn.at[mine, :])],
+        [(disp_in, disp), (peer_in, peer)],
+        [(jac_in.at[:, mine, :], jac.at[:, mine, :]), (grad_in, grad)]
+        + [(x.at[mine, :], y.at[mine, :]) for x, y in ((lam_in, lam), (mu_in, mu), (dens_in, dens))]
+        + [(back_in, back)],
+        [(veloc_in, veloc)]
+        + [(jac_in.at[:, part, :], jac.at[:, part, :]) for part in (upper, lower)]
+        + [
+            (x.at[part, :], y.at[part, :])
+            for part in (upper, lower)
+            for x, y in ((lam_in, lam), (mu_in, mu), (dens_in, dens), (conn_in, conn))
+        ],
+    ]
+    copies, count = [], 0
+    for step in steps:
+        group = []
+        for source, target in step:
+            group.append(pltpu.make_async_copy(source, target, sems.at[count]))
+            count += 1
+        copies.append(group)
+    for group in copies:
+        for copy in group:
+            copy.start()
+
+    def ready(step):
+        for copy in copies[step]:
+            copy.wait()
+
+    edge_part("dev", ready, (disp,) + tuple(kept[2:]), outs, scratches)
+    ready(3)
+
+
+def region_edge_kernel(*refs):
+    edge_part("region", lambda step: None, refs[:9], refs[10:14], refs[14:22])
 
 
 def inner_kernel(
@@ -376,10 +373,8 @@
 ):
     field_rows(disp_in, 0, FIRST + 1, disp_ref)
     field_rows(veloc_in, 0, ROWS, veloc_ref)
-    index_ref[...] = jnp.zeros_like(index_ref)
-    element_rows(
-        (jac_ref, lam_ref, mu_ref, dens_ref, conn_ref), 0, ELEM, (value_ref, index_ref), True
-    )
+    index_rows(conn_ref, 0, ELEM, index_ref)
+    value_rows((jac_ref, lam_ref, mu_ref, dens_ref), 0, ELEM, value_ref)
     value_ref[:, ELEM:, :] = jnp.zeros_like(value_ref[:, ELEM:, :])
     for s in range(FCAP):
         e = slots_ref[s]
@@ -519,7 +514,49 @@
         )
 
 
-def last_kernel(
+def last_rows(low, count, force, refs, outs, scratches):
+    disp_in, moved_ref, veloc_ref, inverse_ref = refs
+    rows_ref, lines_ref, sems = scratches
+    part = pl.ds(low, count)
+    for c in range(3):
+        v = veloc_ref[c, part, :] - STEP * (inverse_ref[part, :] * force[c])
+        rows_ref[0, c] = moved_ref[c, part, :] + STEP * v
+        rows_ref[1, c] = v
+    copies = []
+    for which in (1, 0):
+        for j in range(count):
+            cols = slice(j * LANES, (j + 1) * LANES)
+            whole = slice((low + j) * LANES, (low + j + 1) * LANES)
+            for c in range(3):
+                row = rows_ref[which, c, j : j + 1, :]
+                if which == 0:
+                    row = disp_in[c : c + 1, whole] + row
+                lines_ref[which, c : c + 1, cols] = row
+        copy = pltpu.make_async_copy(
+            lines_ref.at[which],
+            outs[which].at[:, pl.ds(low * LANES, count * LANES)],
+            sems.at[which],
+        )
+        copy.start()
+        copies.append(copy)
+    for copy in copies:
+        copy.wait()
+
+
+def inner_last_kernel(
+    disp_in, moved_ref, veloc_ref, summed_ref, inverse_ref, disp_out, veloc_out, *scratches
+):
+    last_rows(
+        0,
+        FIRST,
+        [summed_ref[c, :FIRST, :] for c in range(3)],
+        (disp_in, moved_ref, veloc_ref, inverse_ref),
+        (disp_out, veloc_out),
+        scratches,
+    )
+
+
+def edge_last_kernel(
     disp_in,
     moved_ref,
     veloc_ref,
@@ -530,24 +567,22 @@
     got1,
     got2,
     got3,
+    disp_half,
+    veloc_half,
     disp_out,
     veloc_out,
     staged_ref,
-    rows_ref,
+    *scratches,
 ):
     placed = received_rows((got0, got1, got2, got3), 3, peer_index_ref, staged_ref)
-    for c in range(3):
-        force = jnp.concatenate(
-            [summed_ref[c, :FIRST, :], summed_ref[c, FIRST:, :] + placed[c]], axis=0
-        )
-        v = veloc_ref[c] - STEP * (inverse_ref[...] * force)
-        rows_ref[0, c] = moved_ref[c, 0:ROWS, :] + STEP * v
-        rows_ref[1, c] = v
-    for j in range(ROWS):
-        cols = slice(j * LANES, (j + 1) * LANES)
-        for c in range(3):
-            disp_out[c : c + 1, cols] = disp_in[c : c + 1, cols] + rows_ref[0, c, j : j + 1, :]
-            veloc_out[c : c + 1, cols] = rows_ref[1, c, j : j + 1, :]
+    last_rows(
+        FIRST,
+        FIRST,
+        [summed_ref[c, FIRST:, :] + placed[c] for c in range(3)],
+        (disp_in, moved_ref, veloc_ref, inverse_ref),
+        (disp_out, veloc_out),
+        scratches,
+    )
 
 
 def swap_pairs(count, colour):
@@ -574,7 +609,6 @@
 
 
 PARAMS = pltpu.CompilerParams(vmem_limit_bytes=48 * 1024 * 1024)
-ALONE = pltpu.CompilerParams(vmem_limit_bytes=62 * 1024 * 1024)
 
 
 def body(
@@ -607,40 +641,42 @@
 
     got, bases = [], []
     raw = pl.BlockSpec(memory_space=pltpu.HBM)
-    order = peer_nodes
-    count = 2 * WIDE
-    for axis in ("dev", "region"):
-        base, spill, send0, send1 = pl.pallas_call(
-            functools.partial(edge_kernel, axis),
-            in_specs=[raw] * 9 + [pl.BlockSpec(memory_space=pl.ANY)],
-            out_shape=[shape((4, HALF, LANES)), shape((4, 8, LANES))] + sends(4, 2),
-            out_specs=[vector] * 4,
-            scratch_shapes=[
-                scratch(6, LANES, LANES),
-                scratch(LANES, LANES, kind=jnp.int32),
-                scratch(LANES, LANES, kind=jnp.int32),
-                scratch(LANES, LANES),
-                scratch(3, WIDE + 8, LANES),
-                scratch(HALF, LANES, kind=jnp.int32),
-                scratch(4, HALF, LANES),
-                scratch(4, WIDE + 8, LANES),
-                scratch(3, count, NODES),
-                scratch(count, NODES),
-                scratch(count, NODES),
-                scratch(count, NODES),
-                scratch(count, NODES, kind=jnp.int32),
-                scratch(3, (WIDE + 1) * LANES),
-                scratch(4, GROUPS * LANES, kind=jnp.int32),
-                scratch(*grad_np.shape, kind=jnp.bfloat16),
-                scratch(*back_np.shape, kind=jnp.bfloat16),
-                pltpu.SemaphoreType.DMA((10,)),
-            ],
-            compiler_params=PARAMS,
-            name="edge_" + axis,
-        )(*[pltpu.with_memory_space_constraint(x, pltpu.HBM) for x in (disp_start, *elements, peer_nodes, grad, back)], order)
-        order = spill
-        got += swap_all((send0, send1), axis)
-        bases.append(base)
+    arguments = (disp_start, veloc_start, *elements, peer_nodes, grad, back)
+    edge_outs = [shape((4, HALF, LANES)), shape((4, 8, LANES))] + sends(4, 2)
+    edge_scratch = [
+        scratch(6, LANES, LANES),
+        scratch(LANES, LANES, kind=jnp.int32),
+        scratch(LANES, LANES, kind=jnp.int32),
+        scratch(LANES, LANES),
+        scratch(3, WIDE + 8, LANES),
+        scratch(HALF, LANES, kind=jnp.int32),
+        scratch(4, HALF, LANES),
+        scratch(4, WIDE + 8, LANES),
+    ]
+    outs = pl.pallas_call(
+        dev_edge_kernel,
+        in_specs=[raw] * 10,
+        out_shape=[shape(x.shape, x.dtype) for x in arguments] + edge_outs,
+        out_specs=[vector] * 14,
+        scratch_shapes=edge_scratch + [pltpu.SemaphoreType.DMA((20,))],
+        compiler_params=PARAMS,
+        name="edge_dev",
+    )(*[pltpu.with_memory_space_constraint(x, pltpu.HBM) for x in arguments])
+    disp_near, veloc_near, *near = outs[:10]
+    base, order, send0, send1 = outs[10:]
+    bases.append(base)
+    got += swap_all((send0, send1), "dev")
+    base, spill, send0, send1 = pl.pallas_call(
+        region_edge_kernel,
+        in_specs=[vector] * 10,
+        out_shape=edge_outs,
+        out_specs=[vector] * 4,
+        scratch_shapes=edge_scratch,
+        compiler_params=PARAMS,
+        name="edge_region",
+    )(disp_near, *near, order)
+    bases.append(base)
+    got += swap_all((send0, send1), "region")
     veloc, inner, fixed, index, spread, peer_index = pl.pallas_call(
         inner_kernel,
         in_specs=[scalar] + [vector] * 12,
@@ -668,13 +704,11 @@
     )(
         fine_slots,
         fine_slots.reshape(1, FCAP),
-        disp_start,
-        veloc_start,
-        *elements,
-        peer_nodes,
+        disp_near,
+        veloc_near,
+        *near[:6],
         spill,
-        grad,
-        back,
+        *near[6:],
     )
     inverse_mass, moved, summed = peer_index, peer_index, peer_index
     for substep in range(SUBSTEPS - 1):
@@ -711,18 +745,31 @@
         if opening:
             inverse_mass = outs[3]
         got = swap_all(outs[-4:-2], "dev") + swap_all(outs[-2:], "region")
+    state = (disp_near, moved, veloc, summed, inverse_mass)
+    last_scratch = [
+        scratch(2, 3, FIRST, LANES),
+        scratch(2, 3, FIRST * LANES),
+        pltpu.SemaphoreType.DMA((2,)),
+    ]
+    halves = pl.pallas_call(
+        inner_last_kernel,
+        in_specs=[vector] * 5,
+        out_shape=[shape((3, NLOC)), shape((3, NLOC))],
+        out_specs=[raw] * 2,
+        scratch_shapes=last_scratch,
+        compiler_params=PARAMS,
+        name="last_inner",
+    )(*state)
     return pl.pallas_call(
-        last_kernel,
-        in_specs=[vector] * 10,
+        edge_last_kernel,
+        in_specs=[vector] * 10 + [raw] * 2,
         out_shape=[shape((3, NLOC)), shape((3, NLOC))],
-        out_specs=[vector] * 2,
-        scratch_shapes=[
-            scratch(4, HALF, LANES),
-            scratch(2, 3, ROWS, LANES),
-        ],
+        out_specs=[raw] * 2,
+        scratch_shapes=[scratch(4, HALF, LANES)] + last_scratch,
+        input_output_aliases={10: 0, 11: 1},
         compiler_params=PARAMS,
-        name="last",
-    )(disp_start, moved, veloc, summed, inverse_mass, peer_index, *got)
+        name="last_edge",
+    )(*state, peer_index, *got, *halves)
 
 
 def solution(mesh):

time: 66.5 us -> 64.7 us (0.973)
  waiting for transfers between devices: 20.4 us -> 15 us
  starting transfers between devices: 28.4 us -> 32.8 us
  Pallas kernels: 16.1 us -> 15.1 us
    ppermute x16, waiting for transfers between devices: 20.4 us -> 15 us  [swap_all(): lax.ppermute(sent, axis, swap_pairs(lax.axis_size(axis), colour))]
    ppermute x16, starting transfers between devices: 28.4 us -> 32.8 us  [swap_all(): lax.ppermute(sent, axis, swap_pairs(lax.axis_size(axis), colour))]
    pallas_call x3 -> x4, Pallas kernels: 6.82 us -> 5.83 us  [the longest x1 2.61 us: body(): pl.pallas_call(dev_edge_kernel, in_specs=[raw] * 10, out_shape=[shape(x.s...]
  transfers between devices with their start and end apart: 16 -> 16, of which waited for: 3 -> 3; matrix products, arithmetic and copies ran while one was open for 0% -> 0% of each run, Pallas kernels for 9% -> 8%
where the time goes in v2:
time: 64.7 us; the launch traced here: 64.6 us
  starting transfers between devices  32.8 us (51%)
  Pallas kernels  15.1 us (23%)
  waiting for transfers between devices  15 us (23%)
  between operations  0.93 us (1%)
  local copies, waits for them, and re-layouts  0.66 us (1%)
    ppermute x16, starting transfers between devices, swap_all(): lax.ppermute(sent, axis, swap_pairs(lax.axis_size(axis), colour))  32.8 us
    ppermute x16, waiting for transfers between devices, swap_all(): lax.ppermute(sent, axis, swap_pairs(lax.axis_size(axis), colour))  15 us
    pallas_call x3, Pallas kernels, body(): pl.pallas_call(functools.partial(middle_kernel, opening), in_specs=[scala...  6.13 us
    pallas_call x1, Pallas kernels, body(): pl.pallas_call(inner_kernel, in_specs=[scalar] + [vector] * 12, out_shape...  3.17 us
    pallas_call x1, Pallas kernels, body(): pl.pallas_call(dev_edge_kernel, in_specs=[raw] * 10, out_shape=[shape(x.s...  2.61 us
  transfers between devices with their start and end apart: 16, of which 3 were waited for; matrix products, arithmetic and copies ran while one was open for 0% of the time, Pallas kernels for 8%

profile of v2, /device:TPU:0, one launch (start us, length us, event | category | flops | bytes accessed | tf_op | source)
XLA Modules:
  0.0 64.6 jit_solution(12239110811787991385)
XLA Ops:
  0.6 2.6 %edge_dev.1 = (f32[3,20480]{1,0:T(4,128)S(1)}, f32[3,20480]{1,0:T(4,128)S(1)}, f32[3,320,125]{2,1,0:T(8,128)S(1)}, f32[320,125]{1,0:T(8,128)S(1)}, f32[320,125]{...) custom-call(f32[3,20480]{1,0:T(4,128)} %refs_0_.1, ...), custom_call_target="tpu_custom_call" | custom-call | tf_op jit(solution)/shard_map/edge_dev/pallas_call | solution.py:656
  3.3 0.1 collective-permute-start
  3.4 10.2 %collective-permute-start.1 = (f32[80,128]{1,0:T(8,128)S(1)}, f32[80,128]{1,0:T(8,128)S(1)}, u32[]{:S(2)}, u32[]{:S(2)}) collective-permute-start(f32[80,128]{1,0:T(8,128)S(1)} %get-tuple-element.71), channel_id=1, source_target_pairs={{1,2},{2,1},{3,4},{4,3},{5,6},{6,5},{7,8},{8,7},{9,10},{10,9},{11,... | collective-permute-start | bytes 122888 | tf_op jit(solution)/shard_map/ppermute | solution.py:598
  13.6 1.2 %edge_region.1 = (f32[4,40,128]{2,1,0:T(8,128)S(1)}, f32[4,8,128]{2,1,0:T(8,128)S(1)}, f32[80,128]{1,0:T(8,128)S(1)}, f32[80,128]{1,0:T(8,128)S(1)}) custom-call(f32[3,20480]{1,0:T(4,128)S(1)} %get-tuple-element.50.refs_0_.disp_in, f32[3,320,125]{2,1,0:T(8,128)S(1)} %get-tuple-element.52.refs_1_.jac_ref, f32[320,125]{1,0:T(8,128)S(1)} %get-tuple-element.53.refs_2_.lam_ref, ...), custom_call_target="tpu_custom_call" | custom-call | tf_op jit(solution)/shard_map/edge_region/pallas_call | solution.py:669
  14.8 1.1 %collective-permute-start.2 = (f32[80,128]{1,0:T(8,128)S(1)}, f32[80,128]{1,0:T(8,128)S(1)}, u32[]{:S(2)}, u32[]{:S(2)}) collective-permute-start(f32[80,128]{1,0:T(8,128)S(1)} %get-tuple-element.72), channel_id=1, source_target_pairs={{0,64},{64,0},{128,192},{192,128},{1,65},{65,1},{129,193},{193,129... | collective-permute-start | bytes 122888 | tf_op jit(solution)/shard_map/ppermute | solution.py:598
  15.9 1.9 %collective-permute-start.3 = (f32[80,128]{1,0:T(8,128)S(1)}, f32[80,128]{1,0:T(8,128)S(1)}, u32[]{:S(2)}, u32[]{:S(2)}) collective-permute-start(f32[80,128]{1,0:T(8,128)S(1)} %get-tuple-element.73), channel_id=1, source_target_pairs={{64,128},{128,64},{192,0},{0,192},{65,129},{129,65},{193,1},{1,193... | collective-permute-start | bytes 122888 | tf_op jit(solution)/shard_map/ppermute | solution.py:598
  17.8 0.7 %copy-done.2 = s32[80]{0:T(128)S(1)} copy-done((s32[80]{0:T(128)S(1)}, s32[80]{0:T(128)}, u32[]{:S(2)}) %copy-start.2) | copy-done | bytes 344
  18.5 3.2 %inner.1 = (f32[3,160,128]{2,1,0:T(8,128)S(1)}, f32[4,80,128]{2,1,0:T(8,128)S(1)}, f32[5,80,128]{2,1,0:T(8,128)S(1)}, s32[2,80,128]{2,1,0:T(8,128)S(1)}, bf16[16...) custom-call(s32[80]{0:T(128)S(1)} %copy-done.2, s32[1,80]{1,0:T(1,128)S(1)} %bitcast.6, ...), custom_call_target="tpu_custom_call" | custom-call | tf_op jit(solution)/shard_map/inner/pallas_call | solution.py:680
  21.6 0.0 collective-permute-done.1.got1
  21.7 0.0 collective-permute-done.2.got2
  21.7 0.0 collective-permute-done.3.got3
  21.7 2.1 %middle.3 = (f32[3,168,128]{2,1,0:T(8,128)S(1)}, f32[3,160,128]{2,1,0:T(8,128)S(1)}, f32[3,160,128]{2,1,0:T(8,128)S(1)}, f32[160,128]{1,0:T(8,128)S(1)}, f32[60,...) custom-call(s32[80]{0:T(128)S(1)} %copy-done.2, ...), custom_call_target="tpu_custom_call" | custom-call | tf_op jit(solution)/shard_map/middle/pallas_call | solution.py:717
  23.8 0.1 collective-permute-start.4
  23.9 3.5 %collective-permute-start.5 = (f32[60,128]{1,0:T(8,128)S(1)}, f32[60,128]{1,0:T(8,128)S(1)}, u32[]{:S(2)}, u32[]{:S(2)}) collective-permute-start(f32[60,128]{1,0:T(8,128)S(1)} %get-tuple-element.79), channel_id=1, source_target_pairs={{1,2},{2,1},{3,4},{4,3},{5,6},{6,5},{7,8},{8,7},{9,10},{10,9},{11,... | collective-permute-start | bytes 92168 | tf_op jit(solution)/shard_map/ppermute | solution.py:598
  27.4 1.0 %collective-permute-start.6 = (f32[60,128]{1,0:T(8,128)S(1)}, f32[60,128]{1,0:T(8,128)S(1)}, u32[]{:S(2)}, u32[]{:S(2)}) collective-permute-start(f32[60,128]{1,0:T(8,128)S(1)} %get-tuple-element.80), channel_id=1, source_target_pairs={{0,64},{64,0},{128,192},{192,128},{1,65},{65,1},{129,193},{193,129... | collective-permute-start | bytes 92168 | tf_op jit(solution)/shard_map/ppermute | solution.py:598
  28.4 1.9 %collective-permute-start.7 = (f32[60,128]{1,0:T(8,128)S(1)}, f32[60,128]{1,0:T(8,128)S(1)}, u32[]{:S(2)}, u32[]{:S(2)}) collective-permute-start(f32[60,128]{1,0:T(8,128)S(1)} %get-tuple-element.81), channel_id=1, source_target_pairs={{64,128},{128,64},{192,0},{0,192},{65,129},{129,65},{193,1},{1,193... | collective-permute-start | bytes 92168 | tf_op jit(solution)/shard_map/ppermute | solution.py:598
  30.3 0.0 collective-permute-done.4.got0
  30.3 5.2 %collective-permute-done.5.got1 = f32[60,128]{1,0:T(8,128)S(1)} collective-permute-done((f32[60,128]{1,0:T(8,128)S(1)}, f32[60,128]{1,0:T(8,128)S(1)}, u32[]{:S(2)}, u32[]{:S(2)}) %collective-permute-start.5) | collective-permute-done | bytes 30752 | tf_op jit(solution)/shard_map/ppermute | solution.py:598
  35.5 2.0 %middle.4 = (f32[3,168,128]{2,1,0:T(8,128)S(1)}, f32[3,160,128]{2,1,0:T(8,128)S(1)}, f32[3,160,128]{2,1,0:T(8,128)S(1)}, f32[60,128]{1,0:T(8,128)S(1)}, f32[60,1...) custom-call(s32[80]{0:T(128)S(1)} %copy-done.2, f32[3,168,128]{2,1,0:T(8,128)S(1)} %get-tuple-element.74.moved_ref, ...), custom_call_target="tpu_custom_call" | custom-call | tf_op jit(solution)/shard_map/middle/pallas_call | solution.py:717
  37.6 0.1 collective-permute-start.8
  37.7 3.6 %collective-permute-start.9 = (f32[60,128]{1,0:T(8,128)S(1)}, f32[60,128]{1,0:T(8,128)S(1)}, u32[]{:S(2)}, u32[]{:S(2)}) collective-permute-start(f32[60,128]{1,0:T(8,128)S(1)} %get-tuple-element.86), channel_id=1, source_target_pairs={{1,2},{2,1},{3,4},{4,3},{5,6},{6,5},{7,8},{8,7},{9,10},{10,9},{11,... | collective-permute-start | bytes 92168 | tf_op jit(solution)/shard_map/ppermute | solution.py:598
  41.3 1.0 %collective-permute-start.10 = (f32[60,128]{1,0:T(8,128)S(1)}, f32[60,128]{1,0:T(8,128)S(1)}, u32[]{:S(2)}, u32[]{:S(2)}) collective-permute-start(f32[60,128]{1,0:T(8,128)S(1)} %get-tuple-element.87), channel_id=1, source_target_pairs={{0,64},{64,0},{128,192},{192,128},{1,65},{65,1},{129,193},{193,129... | collective-permute-start | bytes 92168 | tf_op jit(solution)/shard_map/ppermute | solution.py:598
  42.3 1.9 %collective-permute-start.11 = (f32[60,128]{1,0:T(8,128)S(1)}, f32[60,128]{1,0:T(8,128)S(1)}, u32[]{:S(2)}, u32[]{:S(2)}) collective-permute-start(f32[60,128]{1,0:T(8,128)S(1)} %get-tuple-element.88), channel_id=1, source_target_pairs={{64,128},{128,64},{192,0},{0,192},{65,129},{129,65},{193,1},{1,193... | collective-permute-start | bytes 92168 | tf_op jit(solution)/shard_map/ppermute | solution.py:598
  44.2 5.3 %collective-permute-done.9.got1 = f32[60,128]{1,0:T(8,128)S(1)} collective-permute-done((f32[60,128]{1,0:T(8,128)S(1)}, f32[60,128]{1,0:T(8,128)S(1)}, u32[]{:S(2)}, u32[]{:S(2)}) %collective-permute-start.9) | collective-permute-done | bytes 30752 | tf_op jit(solution)/shard_map/ppermute | solution.py:598
  49.5 2.0 %middle.5 = (f32[3,168,128]{2,1,0:T(8,128)S(1)}, f32[3,160,128]{2,1,0:T(8,128)S(1)}, f32[3,160,128]{2,1,0:T(8,128)S(1)}, f32[60,128]{1,0:T(8,128)S(1)}, f32[60,1...) custom-call(s32[80]{0:T(128)S(1)} %copy-done.2, f32[3,168,128]{2,1,0:T(8,128)S(1)} %get-tuple-element.82.moved_ref, ...), custom_call_target="tpu_custom_call" | custom-call | tf_op jit(solution)/shard_map/middle/pallas_call | solution.py:717
  51.6 0.1 collective-permute-start.12
  51.7 3.4 %collective-permute-start.13 = (f32[60,128]{1,0:T(8,128)S(1)}, f32[60,128]{1,0:T(8,128)S(1)}, u32[]{:S(2)}, u32[]{:S(2)}) collective-permute-start(f32[60,128]{1,0:T(8,128)S(1)} %get-tuple-element.93), channel_id=1, source_target_pairs={{1,2},{2,1},{3,4},{4,3},{5,6},{6,5},{7,8},{8,7},{9,10},{10,9},{11,... | collective-permute-start | bytes 92168 | tf_op jit(solution)/shard_map/ppermute | solution.py:598
  55.0 1.0 %collective-permute-start.14 = (f32[60,128]{1,0:T(8,128)S(1)}, f32[60,128]{1,0:T(8,128)S(1)}, u32[]{:S(2)}, u32[]{:S(2)}) collective-permute-start(f32[60,128]{1,0:T(8,128)S(1)} %get-tuple-element.94), channel_id=1, source_target_pairs={{0,64},{64,0},{128,192},{192,128},{1,65},{65,1},{129,193},{193,129... | collective-permute-start | bytes 92168 | tf_op jit(solution)/shard_map/ppermute | solution.py:598
  56.0 1.9 %collective-permute-start.15 = (f32[60,128]{1,0:T(8,128)S(1)}, f32[60,128]{1,0:T(8,128)S(1)}, u32[]{:S(2)}, u32[]{:S(2)}) collective-permute-start(f32[60,128]{1,0:T(8,128)S(1)} %get-tuple-element.95), channel_id=1, source_target_pairs={{64,128},{128,64},{192,0},{0,192},{65,129},{129,65},{193,1},{1,193... | collective-permute-start | bytes 92168 | tf_op jit(solution)/shard_map/ppermute | solution.py:598
  57.9 0.9 %last_inner.1 = (f32[3,20480]{1,0:T(4,128)}, f32[3,20480]{1,0:T(4,128)}) custom-call(f32[3,20480]{1,0:T(4,128)S(1)} %get-tuple-element.50.refs_0_.disp_in, f32[3,168,128]{2,1,0:T(8,128)S(1)} %get-tuple-element.89.moved_ref, f32[3,160,128]{2,1,0:T(8,128)S(1)} %get-tuple-element.90.veloc_ref, f32[3,160,128]{2,1,0:T(8,128)S(1)} %get-tuple-element.91.summed_ref, ...), custom_call_target="tpu_custom_call" | custom-call | tf_op jit(solution)/shard_map/last_inner/pallas_call | solution.py:754
  58.9 4.5 %collective-permute-done.13.got1 = f32[60,128]{1,0:T(8,128)S(1)} collective-permute-done((f32[60,128]{1,0:T(8,128)S(1)}, f32[60,128]{1,0:T(8,128)S(1)}, u32[]{:S(2)}, u32[]{:S(2)}) %collective-permute-start.13) | collective-permute-done | bytes 30752 | tf_op jit(solution)/shard_map/ppermute | solution.py:598
  63.3 1.1 %last_edge.1 = (f32[3,20480]{1,0:T(4,128)}, f32[3,20480]{1,0:T(4,128)}) custom-call(f32[3,20480]{1,0:T(4,128)S(1)} %get-tuple-element.50.refs_0_.disp_in, f32[3,168,128]{2,1,0:T(8,128)S(1)} %get-tuple-element.89.moved_ref, f32[3,160,128]{2,1,0:T(8,128)S(1)} %get-tuple-element.90.veloc_ref, ...), custom_call_target="tpu_custom_call", output_to_operand_aliasing={{0}: (10, {}), {1}: (11, {})} | custom-call | tf_op jit(solution)/shard_map/last_edge/pallas_call | solution.py:763
  (14 shorter events, 0.0 us)
Async XLA Ops:
  3.3 18.4 %collective-permute-start = (f32[80,128]{1,0:T(8,128)S(1)}, f32[80,128]{1,0:T(8,128)S(1)}, u32[]{:S(2)}, u32[]{:S(2)}) collective-permute-start(f32[80,128]{1,0:T(8,128)S(1)} %get-tuple-element.70), channel_id=1, source_target_pairs={{0,1},{1,0},{2,3},{3,2},{4,5},{5,4},{6,7},{7,6},{8,9},{9,8},{10,11... | collective-permute-start | bytes 122888 | tf_op jit(solution)/shard_map/ppermute | solution.py:598
  3.4 18.3 %collective-permute-start.1 = (f32[80,128]{1,0:T(8,128)S(1)}, f32[80,128]{1,0:T(8,128)S(1)}, u32[]{:S(2)}, u32[]{:S(2)}) collective-permute-start(f32[80,128]{1,0:T(8,128)S(1)} %get-tuple-element.71), channel_id=1, source_target_pairs={{1,2},{2,1},{3,4},{4,3},{5,6},{6,5},{7,8},{8,7},{9,10},{10,9},{11,... | collective-permute-start | bytes 122888 | tf_op jit(solution)/shard_map/ppermute | solution.py:598
  14.8 6.9 %collective-permute-start.2 = (f32[80,128]{1,0:T(8,128)S(1)}, f32[80,128]{1,0:T(8,128)S(1)}, u32[]{:S(2)}, u32[]{:S(2)}) collective-permute-start(f32[80,128]{1,0:T(8,128)S(1)} %get-tuple-element.72), channel_id=1, source_target_pairs={{0,64},{64,0},{128,192},{192,128},{1,65},{65,1},{129,193},{193,129... | collective-permute-start | bytes 122888 | tf_op jit(solution)/shard_map/ppermute | solution.py:598
  15.9 5.8 %collective-permute-start.3 = (f32[80,128]{1,0:T(8,128)S(1)}, f32[80,128]{1,0:T(8,128)S(1)}, u32[]{:S(2)}, u32[]{:S(2)}) collective-permute-start(f32[80,128]{1,0:T(8,128)S(1)} %get-tuple-element.73), channel_id=1, source_target_pairs={{64,128},{128,64},{192,0},{0,192},{65,129},{129,65},{193,1},{1,193... | collective-permute-start | bytes 122888 | tf_op jit(solution)/shard_map/ppermute | solution.py:598
  17.8 0.7 %copy-start.2 = (s32[80]{0:T(128)S(1)}, s32[80]{0:T(128)}, u32[]{:S(2)}) copy-start(s32[80]{0:T(128)} %slots_ref.7) | copy-start | bytes 964
  18.5 3.2 %copy-start = (bf16[1152,128]{1,0:T(8,128)(2,1)S(1)}, bf16[1152,128]{1,0:T(8,128)(2,1)}, u32[]{:S(2)}) copy-start(bf16[1152,128]{1,0:T(8,128)(2,1)} %constant.5.clone.refs_9_.back_ref) | copy-start | bytes 884740
  18.5 3.2 %copy-start.1 = (bf16[384,384]{1,0:T(8,128)(2,1)S(1)}, bf16[384,384]{1,0:T(8,128)(2,1)}, u32[]{:S(2)}) copy-start(bf16[384,384]{1,0:T(8,128)(2,1)} %constant.4.clone.refs_8_.grad_ref) | copy-start | bytes 884740
  23.8 6.6 %collective-permute-start.4 = (f32[60,128]{1,0:T(8,128)S(1)}, f32[60,128]{1,0:T(8,128)S(1)}, u32[]{:S(2)}, u32[]{:S(2)}) collective-permute-start(f32[60,128]{1,0:T(8,128)S(1)} %get-tuple-element.78), channel_id=1, source_target_pairs={{0,1},{1,0},{2,3},{3,2},{4,5},{5,4},{6,7},{7,6},{8,9},{9,8},{10,11... | collective-permute-start | bytes 92168 | tf_op jit(solution)/shard_map/ppermute | solution.py:598
  23.9 11.7 %collective-permute-start.5 = (f32[60,128]{1,0:T(8,128)S(1)}, f32[60,128]{1,0:T(8,128)S(1)}, u32[]{:S(2)}, u32[]{:S(2)}) collective-permute-start(f32[60,128]{1,0:T(8,128)S(1)} %get-tuple-element.79), channel_id=1, source_target_pairs={{1,2},{2,1},{3,4},{4,3},{5,6},{6,5},{7,8},{8,7},{9,10},{10,9},{11,... | collective-permute-start | bytes 92168 | tf_op jit(solution)/shard_map/ppermute | solution.py:598
  27.4 8.1 %collective-permute-start.6 = (f32[60,128]{1,0:T(8,128)S(1)}, f32[60,128]{1,0:T(8,128)S(1)}, u32[]{:S(2)}, u32[]{:S(2)}) collective-permute-start(f32[60,128]{1,0:T(8,128)S(1)} %get-tuple-element.80), channel_id=1, source_target_pairs={{0,64},{64,0},{128,192},{192,128},{1,65},{65,1},{129,193},{193,129... | collective-permute-start | bytes 92168 | tf_op jit(solution)/shard_map/ppermute | solution.py:598
  28.4 7.1 %collective-permute-start.7 = (f32[60,128]{1,0:T(8,128)S(1)}, f32[60,128]{1,0:T(8,128)S(1)}, u32[]{:S(2)}, u32[]{:S(2)}) collective-permute-start(f32[60,128]{1,0:T(8,128)S(1)} %get-tuple-element.81), channel_id=1, source_target_pairs={{64,128},{128,64},{192,0},{0,192},{65,129},{129,65},{193,1},{1,193... | collective-permute-start | bytes 92168 | tf_op jit(solution)/shard_map/ppermute | solution.py:598
  37.6 6.6 %collective-permute-start.8 = (f32[60,128]{1,0:T(8,128)S(1)}, f32[60,128]{1,0:T(8,128)S(1)}, u32[]{:S(2)}, u32[]{:S(2)}) collective-permute-start(f32[60,128]{1,0:T(8,128)S(1)} %get-tuple-element.85), channel_id=1, source_target_pairs={{0,1},{1,0},{2,3},{3,2},{4,5},{5,4},{6,7},{7,6},{8,9},{9,8},{10,11... | collective-permute-start | bytes 92168 | tf_op jit(solution)/shard_map/ppermute | solution.py:598
  37.7 11.8 %collective-permute-start.9 = (f32[60,128]{1,0:T(8,128)S(1)}, f32[60,128]{1,0:T(8,128)S(1)}, u32[]{:S(2)}, u32[]{:S(2)}) collective-permute-start(f32[60,128]{1,0:T(8,128)S(1)} %get-tuple-element.86), channel_id=1, source_target_pairs={{1,2},{2,1},{3,4},{4,3},{5,6},{6,5},{7,8},{8,7},{9,10},{10,9},{11,... | collective-permute-start | bytes 92168 | tf_op jit(solution)/shard_map/ppermute | solution.py:598
  41.3 8.2 %collective-permute-start.10 = (f32[60,128]{1,0:T(8,128)S(1)}, f32[60,128]{1,0:T(8,128)S(1)}, u32[]{:S(2)}, u32[]{:S(2)}) collective-permute-start(f32[60,128]{1,0:T(8,128)S(1)} %get-tuple-element.87), channel_id=1, source_target_pairs={{0,64},{64,0},{128,192},{192,128},{1,65},{65,1},{129,193},{193,129... | collective-permute-start | bytes 92168 | tf_op jit(solution)/shard_map/ppermute | solution.py:598
  42.3 7.2 %collective-permute-start.11 = (f32[60,128]{1,0:T(8,128)S(1)}, f32[60,128]{1,0:T(8,128)S(1)}, u32[]{:S(2)}, u32[]{:S(2)}) collective-permute-start(f32[60,128]{1,0:T(8,128)S(1)} %get-tuple-element.88), channel_id=1, source_target_pairs={{64,128},{128,64},{192,0},{0,192},{65,129},{129,65},{193,1},{1,193... | collective-permute-start | bytes 92168 | tf_op jit(solution)/shard_map/ppermute | solution.py:598
  51.6 7.3 %collective-permute-start.12 = (f32[60,128]{1,0:T(8,128)S(1)}, f32[60,128]{1,0:T(8,128)S(1)}, u32[]{:S(2)}, u32[]{:S(2)}) collective-permute-start(f32[60,128]{1,0:T(8,128)S(1)} %get-tuple-element.92), channel_id=1, source_target_pairs={{0,1},{1,0},{2,3},{3,2},{4,5},{5,4},{6,7},{7,6},{8,9},{9,8},{10,11... | collective-permute-start | bytes 92168 | tf_op jit(solution)/shard_map/ppermute | solution.py:598
  51.7 11.7 %collective-permute-start.13 = (f32[60,128]{1,0:T(8,128)S(1)}, f32[60,128]{1,0:T(8,128)S(1)}, u32[]{:S(2)}, u32[]{:S(2)}) collective-permute-start(f32[60,128]{1,0:T(8,128)S(1)} %get-tuple-element.93), channel_id=1, source_target_pairs={{1,2},{2,1},{3,4},{4,3},{5,6},{6,5},{7,8},{8,7},{9,10},{10,9},{11,... | collective-permute-start | bytes 92168 | tf_op jit(solution)/shard_map/ppermute | solution.py:598
  55.0 8.3 %collective-permute-start.14 = (f32[60,128]{1,0:T(8,128)S(1)}, f32[60,128]{1,0:T(8,128)S(1)}, u32[]{:S(2)}, u32[]{:S(2)}) collective-permute-start(f32[60,128]{1,0:T(8,128)S(1)} %get-tuple-element.94), channel_id=1, source_target_pairs={{0,64},{64,0},{128,192},{192,128},{1,65},{65,1},{129,193},{193,129... | collective-permute-start | bytes 92168 | tf_op jit(solution)/shard_map/ppermute | solution.py:598
  56.0 7.3 %collective-permute-start.15 = (f32[60,128]{1,0:T(8,128)S(1)}, f32[60,128]{1,0:T(8,128)S(1)}, u32[]{:S(2)}, u32[]{:S(2)}) collective-permute-start(f32[60,128]{1,0:T(8,128)S(1)} %get-tuple-element.95), channel_id=1, source_target_pairs={{64,128},{128,64},{192,0},{0,192},{65,129},{129,65},{193,1},{1,193... | collective-permute-start | bytes 92168 | tf_op jit(solution)/shard_map/ppermute | solution.py:598

commit v3 on v2

--- a/solution.py
+++ b/solution.py
@@ -23,7 +23,6 @@
 GLL_POINTS = (-1.0, -math.sqrt(3.0 / 7.0), 0.0, math.sqrt(3.0 / 7.0), 1.0)
 TIME_STEP = 0.2
 STEP = TIME_STEP / SUBSTEPS
-PAD_ROWS = 168
 
 
 def slope_rows():
@@ -67,10 +66,10 @@
 
     def terms(whole):
         high = whole.astype(ml_dtypes.bfloat16)
-        low = (whole - high.astype(np.float32)).astype(ml_dtypes.bfloat16)
-        return np.concatenate([high, high, low], axis=0)
-
-    return terms(grad), terms(back)
+        return high, (whole - high.astype(np.float32)).astype(ml_dtypes.bfloat16)
+
+    high, low = terms(grad)
+    return np.concatenate([high, high, low], axis=0), np.concatenate(terms(back), axis=1)
 
 
 def split_terms(whole):
@@ -81,6 +80,13 @@
 
 def lane_pick(values, index):
     return jnp.take_along_axis(values, index, axis=1, mode="promise_in_bounds")
+
+
+def one_hot_product(rows, high, low):
+    both = jnp.dot(
+        rows, jnp.concatenate([high, low], axis=1), preferred_element_type=jnp.float32
+    )
+    return both[:, : high.shape[1]] + both[:, high.shape[1] :]
 
 
 def forces(shifted, jac, lam, mu, grad, back):
@@ -107,8 +113,11 @@
             fluxes.append(jac[i] * stress)
         rows.append(jnp.concatenate(fluxes, axis=1))
     high, low = split_terms(jnp.concatenate(rows, axis=0))
-    out = jnp.dot(
-        jnp.concatenate([high, low, high], axis=1), back, preferred_element_type=jnp.float32
+    out = jnp.dot(high, back, preferred_element_type=jnp.float32)
+    out = (
+        out[:, :LANES]
+        + out[:, LANES:]
+        + jnp.dot(low, back[:, :LANES], preferred_element_type=jnp.float32)
     )
     return [out[c * count : (c + 1) * count] for c in range(3)]
 
@@ -129,18 +138,15 @@
     return lax.broadcasted_iota(jnp.int32, shape, 1) >= LANES // 2
 
 
-def fine_local(disp_ref, slots_ref, window_ref, statics, spread, grad, back):
+def fine_local(moved, statics, collect, spread, grad, back):
     jac0, jac1, jac2, lam, mu, index, place = statics
+    high, low = split_terms(jnp.concatenate(moved, axis=1))
+    rows = one_hot_product(collect, high, low)
     upper = high_half((1, LANES))
-    for s in range(FCAP):
-        e = slots_ref[s]
-        first = lax.shift_right_logical(e, 1)
-        second = lax.shift_right_logical(e + 1, 1)
-        for c in range(3):
-            window_ref[c, pl.ds(s, 1), :] = jnp.where(
-                upper, disp_ref[c, pl.ds(first, 1), :], disp_ref[c, pl.ds(second, 1), :]
-            )
-    shifted = [lane_pick(window_ref[c], index) for c in range(3)]
+    shifted = []
+    for c in range(3):
+        part = slice(c * LANES, (c + 1) * LANES)
+        shifted.append(lane_pick(jnp.where(upper, rows[:FCAP, part], rows[FCAP:, part]), index))
     out = forces(shifted, (jac0, jac1, jac2), lam, mu, grad, back)
     slotted = jnp.concatenate([lane_pick(o, place) for o in out], axis=1)
     upper = lax.broadcasted_iota(jnp.int32, slotted.shape, 1) % LANES >= LANES // 2
@@ -149,9 +155,7 @@
         [jnp.where(upper, slotted, 0.0), blank, jnp.where(upper, 0.0, slotted), blank], axis=0
     )
     high, low = split_terms(both)
-    return jnp.dot(spread, high, preferred_element_type=jnp.float32) + jnp.dot(
-        spread, low, preferred_element_type=jnp.float32
-    )
+    return one_hot_product(spread, high, low)
 
 
 def send_pair(shared, picks, odd, staged_ref, outs):
@@ -160,15 +164,15 @@
     for c in range(len(shared)):
         part = [staged_ref[c, GROUPS * p : GROUPS * (p + 1), :] for p in range(2)]
         put = pl.ds(c * GROUPS, GROUPS)
-        outs[0][put, :] = jnp.where(odd, part[0], part[1])
-        outs[1][put, :] = jnp.where(odd, part[1], part[0])
+        outs[0][put, :] = jnp.where(odd, part[1], part[0])
+        outs[1][put, :] = jnp.where(odd, part[0], part[1])
 
 
 def received_pair(arrived, channels, places, odd, staged_ref):
     for c in range(channels):
         got = [a[c * GROUPS : (c + 1) * GROUPS, :] for a in arrived]
-        staged_ref[c, 0:GROUPS, :] = jnp.where(odd, got[0][...], got[1][...])
-        staged_ref[c, GROUPS : 2 * GROUPS, :] = jnp.where(odd, got[1][...], got[0][...])
+        staged_ref[c, 0:GROUPS, :] = jnp.where(odd, got[1][...], got[0][...])
+        staged_ref[c, GROUPS : 2 * GROUPS, :] = jnp.where(odd, got[0][...], got[1][...])
     return [lane_pick(staged_ref[c], places) for c in range(channels)]
 
 
@@ -212,8 +216,8 @@
     shifted = []
     at = low_row - disp_low
     for c in range(3):
-        here = disp_ref[c, at : at + part, :]
-        after = disp_ref[c, at + 1 : at + part + 1, :]
+        here = channel(disp_ref, c, at, part)
+        after = channel(disp_ref, c, at + 1, part)
         shifted.append(
             lane_pick(jnp.concatenate([here, jnp.where(upper, here, after)], axis=0), index)
         )
@@ -237,10 +241,11 @@
 def field_rows(source, low, count, out_ref):
     for j in range(count):
         row = (low + j) % ROWS
-        for c in range(3):
-            out_ref[c, j : j + 1, :] = source[
-                c : c + 1, row * LANES : (row + 1) * LANES
-            ]
+        out_ref[4 * j : 4 * j + 3, :] = source[:, row * LANES : (row + 1) * LANES]
+
+
+def channel(ref, c, low, count):
+    return ref[pl.ds(4 * low + c, count, stride=4), :]
 
 
 EDGE = 8
@@ -299,10 +304,10 @@
 
 
 def dev_edge_kernel(*refs):
-    raw, kept, outs, scratches = refs[:10], refs[10:20], refs[20:24], refs[24:32]
-    sems = refs[32]
-    disp_in, veloc_in, jac_in, lam_in, mu_in, dens_in, conn_in, peer_in, grad_in, back_in = raw
-    disp, veloc, jac, lam, mu, dens, conn, peer, grad, back = kept
+    raw, kept, outs, scratches = refs[:11], refs[11:22], refs[22:26], refs[26:34]
+    sems = refs[34]
+    disp_in, veloc_in, jac_in, lam_in, mu_in, dens_in, conn_in, peer_in, grad_in, back_in = raw[:10]
+    disp, veloc, jac, lam, mu, dens, conn, peer, grad, back = kept[:10]
     low = 2 * (FIRST - EDGE)
     mine, lower, upper = pl.ds(low, 2 * WIDE), pl.ds(0, low), pl.ds(low + 2 * WIDE, ELEM - low - 2 * WIDE)
     steps = [
@@ -311,7 +316,7 @@
         [(jac_in.at[:, mine, :], jac.at[:, mine, :]), (grad_in, grad)]
         + [(x.at[mine, :], y.at[mine, :]) for x, y in ((lam_in, lam), (mu_in, mu), (dens_in, dens))]
         + [(back_in, back)],
-        [(veloc_in, veloc)]
+        [(veloc_in, veloc), (raw[10], kept[10])]
         + [(jac_in.at[:, part, :], jac.at[:, part, :]) for part in (upper, lower)]
         + [
             (x.at[part, :], y.at[part, :])
@@ -334,7 +339,7 @@
         for copy in copies[step]:
             copy.wait()
 
-    edge_part("dev", ready, (disp,) + tuple(kept[2:]), outs, scratches)
+    edge_part("dev", ready, (disp,) + tuple(kept[2:10]), outs, scratches)
     ready(3)
 
 
@@ -343,7 +348,7 @@
 
 
 def inner_kernel(
-    slots_ref,
+    slots_in,
     slot_row_ref,
     disp_in,
     veloc_in,
@@ -360,6 +365,7 @@
     base_ref,
     fixed_ref,
     index_out,
+    collect_ref,
     spread_ref,
     peer_index_ref,
     value_ref,
@@ -367,55 +373,28 @@
     place_ref,
     turned_ref,
     disp_ref,
+    veloc_rows_ref,
     peer_rows_ref,
     total_ref,
     spread_wide_ref,
+    slots_ref,
+    slots_sem,
 ):
+    slots_copy = pltpu.make_async_copy(slots_in, slots_ref, slots_sem)
+    slots_copy.start()
     field_rows(disp_in, 0, FIRST + 1, disp_ref)
-    field_rows(veloc_in, 0, ROWS, veloc_ref)
     index_rows(conn_ref, 0, ELEM, index_ref)
     value_rows((jac_ref, lam_ref, mu_ref, dens_ref), 0, ELEM, value_ref)
     value_ref[:, ELEM:, :] = jnp.zeros_like(value_ref[:, ELEM:, :])
-    for s in range(FCAP):
-        e = slots_ref[s]
-        for a in range(5):
-            fixed_ref[a, s : s + 1, :] = value_ref[a, pl.ds(e, 1), :]
-        index_out[0, s : s + 1, :] = index_ref[pl.ds(e, 1), :]
-    tail = ELEM // 2 - LANES
     place_ref[0:LANES, :] = inverse_rows(index_ref[0:LANES, :], turned_ref, NODES, LANES - 1)
-    both = jnp.concatenate(
-        [
-            index_ref[LANES : LANES + tail, :],
-            index_out[0],
-            jnp.zeros((LANES - tail - FCAP, LANES), jnp.int32),
-        ],
-        axis=0,
-    )
-    found = inverse_rows(both, turned_ref, NODES, LANES - 1)
-    place_ref[LANES : LANES + tail, :] = found[0:tail]
-    index_out[1] = found[tail : tail + FCAP]
-    for half in range(2):
-        peer_maps(peer_ref, 2 * half, peer_rows_ref.at[pl.ds(half * HALF, HALF), :])
-    peer_rows_ref[SHARED:, :] = jnp.zeros((LANES - SHARED, LANES), jnp.int32)
-    peer_index_ref[0] = peer_rows_ref[0:SHARED, :]
-    peer_index_ref[1] = inverse_rows(peer_rows_ref[...], turned_ref, LANES, 0)[0:SHARED]
-    rows = lax.broadcasted_iota(jnp.int32, (ROWS, FCAP), 0)
-    slot_row = slot_row_ref[...]
-    second = lax.shift_right_logical(slot_row + 1, 1)
-    second = jnp.where(second == ROWS, 0, second)
-    spread_wide_ref[...] = jnp.zeros_like(spread_wide_ref)
-    spread_wide_ref[:, 0:FCAP] = jnp.where(
-        lax.shift_right_logical(slot_row, 1) == rows, 1.0, 0.0
-    )
-    spread_wide_ref[:, LANES : LANES + FCAP] = jnp.where(second == rows, 1.0, 0.0)
-    spread_ref[...] = spread_wide_ref[...].astype(jnp.bfloat16)
     total_ref[...] = jnp.zeros_like(total_ref)
     for c in range(4):
         total_ref[c, 0:1, :] = spill_in[c, 0:1, :]
-    for low_row in (0, HALF):
+
+    def add_rows(low_row):
         row_forces(
             low_row,
-            HALF,
+            FIRST,
             disp_ref,
             0,
             value_ref,
@@ -427,6 +406,49 @@
             total_ref,
             0,
         )
+
+    field_rows(veloc_in, 0, ROWS, veloc_rows_ref)
+    for c in range(3):
+        veloc_ref[c] = channel(veloc_rows_ref, c, 0, ROWS)
+    for half in range(2):
+        peer_maps(peer_ref, 2 * half, peer_rows_ref.at[pl.ds(half * HALF, HALF), :])
+    peer_rows_ref[SHARED:, :] = jnp.zeros((LANES - SHARED, LANES), jnp.int32)
+    peer_index_ref[0] = peer_rows_ref[0:SHARED, :]
+    peer_index_ref[1] = inverse_rows(peer_rows_ref[...], turned_ref, LANES, 0)[0:SHARED]
+    slots_copy.wait()
+    for s in range(FCAP):
+        e = slots_ref[s]
+        for a in range(5):
+            fixed_ref[a, s : s + 1, :] = value_ref[a, pl.ds(e, 1), :]
+        index_out[0, s : s + 1, :] = index_ref[pl.ds(e, 1), :]
+    tail = ELEM // 2 - LANES
+    both = jnp.concatenate(
+        [
+            index_ref[LANES : LANES + tail, :],
+            index_out[0],
+            jnp.zeros((LANES - tail - FCAP, LANES), jnp.int32),
+        ],
+        axis=0,
+    )
+    found = inverse_rows(both, turned_ref, NODES, LANES - 1)
+    place_ref[LANES : LANES + tail, :] = found[0:tail]
+    index_out[1] = found[tail : tail + FCAP]
+    rows = lax.broadcasted_iota(jnp.int32, (ROWS, FCAP), 0)
+    slot_row = slot_row_ref[...]
+    second = lax.shift_right_logical(slot_row + 1, 1)
+    second = jnp.where(second == ROWS, 0, second)
+    spread_wide_ref[...] = jnp.zeros_like(spread_wide_ref)
+    spread_wide_ref[0:ROWS, 0:FCAP] = jnp.where(
+        lax.shift_right_logical(slot_row, 1) == rows, 1.0, 0.0
+    )
+    spread_wide_ref[0:ROWS, LANES : LANES + FCAP] = jnp.where(second == rows, 1.0, 0.0)
+    spread_ref[...] = spread_wide_ref[0:ROWS, :].astype(jnp.bfloat16)
+    for half in range(2):
+        turned = spread_wide_ref[:, half * LANES : (half + 1) * LANES].T
+        collect_ref[half * FCAP : (half + 1) * FCAP, :] = turned[:FCAP, :ROWS].astype(
+            jnp.bfloat16
+        )
+    add_rows(0)
     for c in range(4):
         base_ref[c] = total_ref[c, 0:FIRST, :]
 
@@ -447,7 +469,6 @@
 
 def middle_kernel(
     opening,
-    slots_ref,
     moved_ref,
     veloc_ref,
     inner_ref,
@@ -457,6 +478,7 @@
     inverse_ref,
     fixed_ref,
     index_ref,
+    collect_ref,
     spread_ref,
     peer_index_ref,
     got0,
@@ -471,9 +493,9 @@
     *rest,
 ):
     if opening:
-        inverse_out, sends0, sends1, sends2, sends3, window_ref, staged_ref = rest
+        inverse_out, sends0, sends1, sends2, sends3, staged_ref = rest
     else:
-        sends0, sends1, sends2, sends3, window_ref, staged_ref = rest
+        sends0, sends1, sends2, sends3, staged_ref = rest
     placed = received_rows(
         (got0, got1, got2, got3), 4 if opening else 3, peer_index_ref, staged_ref
     )
@@ -485,19 +507,18 @@
     else:
         inverse_mass = inverse_ref[...]
     base = [whole_base(c, inner_ref, dev_ref, region_ref) for c in range(3)]
+    moved = []
     for c in range(3):
         local = base[c] if opening else summed_ref[c]
         force = jnp.concatenate([local[:FIRST], local[FIRST:] + placed[c]], axis=0)
         v = veloc_ref[c] - STEP * (inverse_mass * force)
-        moved = STEP * v if opening else moved_ref[c, 0:ROWS, :] + STEP * v
-        moved_out[c, 0:ROWS, :] = moved
-        moved_out[c, ROWS:PAD_ROWS, :] = jnp.broadcast_to(moved[0:1], (PAD_ROWS - ROWS, LANES))
+        moved.append(STEP * v if opening else moved_ref[c] + STEP * v)
+        moved_out[c] = moved[c]
         veloc_out[c] = v
     fine = fine_local(
-        moved_out,
-        slots_ref,
-        window_ref,
+        moved,
         [fixed_ref[a] for a in range(5)] + [index_ref[a] for a in range(2)],
+        collect_ref[...],
         spread_ref[...],
         grad_ref[...],
         back_ref[...],
@@ -520,18 +541,17 @@
     part = pl.ds(low, count)
     for c in range(3):
         v = veloc_ref[c, part, :] - STEP * (inverse_ref[part, :] * force[c])
-        rows_ref[0, c] = moved_ref[c, part, :] + STEP * v
-        rows_ref[1, c] = v
+        rows_ref[0, pl.ds(c, count, stride=4), :] = moved_ref[c, part, :] + STEP * v
+        rows_ref[1, pl.ds(c, count, stride=4), :] = v
     copies = []
     for which in (1, 0):
         for j in range(count):
             cols = slice(j * LANES, (j + 1) * LANES)
             whole = slice((low + j) * LANES, (low + j + 1) * LANES)
-            for c in range(3):
-                row = rows_ref[which, c, j : j + 1, :]
-                if which == 0:
-                    row = disp_in[c : c + 1, whole] + row
-                lines_ref[which, c : c + 1, cols] = row
+            row = rows_ref[which, 4 * j : 4 * j + 3, :]
+            if which == 0:
+                row = disp_in[:, whole] + row
+            lines_ref[which, :, cols] = row
         copy = pltpu.make_async_copy(
             lines_ref.at[which],
             outs[which].at[:, pl.ds(low * LANES, count * LANES)],
@@ -596,7 +616,7 @@
 def swap_all(sends, axis):
     return [
         lax.ppermute(sent, axis, swap_pairs(lax.axis_size(axis), colour))
-        for colour, sent in enumerate(sends)
+        for colour, sent in zip((1, 0), sends)
     ]
 
 
@@ -624,10 +644,8 @@
 ):
     grad_np, back_np = slope_operands()
     grad, back = jnp.asarray(grad_np), jnp.asarray(back_np)
-    scalar = pl.BlockSpec(memory_space=pltpu.SMEM)
     vector = pl.BlockSpec(memory_space=pltpu.VMEM)
     field = shape((3, ROWS, LANES))
-    padded = shape((3, PAD_ROWS, LANES))
     elements = (
         jnp.transpose(jacobian, (0, 2, 1)),
         lame_lambda.T,
@@ -641,29 +659,30 @@
 
     got, bases = [], []
     raw = pl.BlockSpec(memory_space=pltpu.HBM)
-    arguments = (disp_start, veloc_start, *elements, peer_nodes, grad, back)
+    slot_row = fine_slots.reshape(1, FCAP)
+    arguments = (disp_start, veloc_start, *elements, peer_nodes, grad, back, slot_row)
     edge_outs = [shape((4, HALF, LANES)), shape((4, 8, LANES))] + sends(4, 2)
     edge_scratch = [
         scratch(6, LANES, LANES),
         scratch(LANES, LANES, kind=jnp.int32),
         scratch(LANES, LANES, kind=jnp.int32),
         scratch(LANES, LANES),
-        scratch(3, WIDE + 8, LANES),
+        scratch(4 * (WIDE + 8), LANES),
         scratch(HALF, LANES, kind=jnp.int32),
         scratch(4, HALF, LANES),
         scratch(4, WIDE + 8, LANES),
     ]
     outs = pl.pallas_call(
         dev_edge_kernel,
-        in_specs=[raw] * 10,
+        in_specs=[raw] * 11,
         out_shape=[shape(x.shape, x.dtype) for x in arguments] + edge_outs,
-        out_specs=[vector] * 14,
-        scratch_shapes=edge_scratch + [pltpu.SemaphoreType.DMA((20,))],
+        out_specs=[vector] * 15,
+        scratch_shapes=edge_scratch + [pltpu.SemaphoreType.DMA((21,))],
         compiler_params=PARAMS,
         name="edge_dev",
     )(*[pltpu.with_memory_space_constraint(x, pltpu.HBM) for x in arguments])
-    disp_near, veloc_near, *near = outs[:10]
-    base, order, send0, send1 = outs[10:]
+    disp_near, veloc_near, *near, slots_near = outs[:11]
+    base, order, send0, send1 = outs[11:]
     bases.append(base)
     got += swap_all((send0, send1), "dev")
     base, spill, send0, send1 = pl.pallas_call(
@@ -677,33 +696,37 @@
     )(disp_near, *near, order)
     bases.append(base)
     got += swap_all((send0, send1), "region")
-    veloc, inner, fixed, index, spread, peer_index = pl.pallas_call(
+    veloc, inner, fixed, index, collect, spread, peer_index = pl.pallas_call(
         inner_kernel,
-        in_specs=[scalar] + [vector] * 12,
+        in_specs=[raw] + [vector] * 12,
         out_shape=[
             field,
             shape((4, FIRST, LANES)),
             shape((5, FCAP, LANES)),
             shape((2, FCAP, LANES), jnp.int32),
+            shape((2 * FCAP, ROWS), jnp.bfloat16),
             shape((ROWS, 2 * LANES), jnp.bfloat16),
             shape((2, SHARED, LANES), jnp.int32),
         ],
-        out_specs=[vector] * 6,
+        out_specs=[vector] * 7,
         scratch_shapes=[
             scratch(6, ELEM + 8, LANES),
             scratch(ELEM + 8, LANES, kind=jnp.int32),
             scratch(ELEM // 2, LANES, kind=jnp.int32),
             scratch(LANES, LANES),
-            scratch(3, FIRST + 8, LANES),
+            scratch(4 * (FIRST + 8), LANES),
+            scratch(4 * ROWS, LANES),
             scratch(LANES, LANES, kind=jnp.int32),
             scratch(4, FIRST + 8, LANES),
-            scratch(ROWS, 2 * LANES),
+            scratch(2 * LANES, 2 * LANES),
+            pltpu.SMEM((FCAP,), jnp.int32),
+            pltpu.SemaphoreType.DMA(()),
         ],
         compiler_params=PARAMS,
         name="inner",
     )(
-        fine_slots,
-        fine_slots.reshape(1, FCAP),
+        pltpu.with_memory_space_constraint(fine_slots, pltpu.HBM),
+        slots_near,
         disp_near,
         veloc_near,
         *near[:6],
@@ -716,17 +739,13 @@
         extra = [shape((ROWS, LANES))] if opening else []
         outs = pl.pallas_call(
             functools.partial(middle_kernel, opening),
-            in_specs=[scalar] + [vector] * 17,
-            out_shape=[padded, field, field] + extra + sends(3, 4),
+            in_specs=[vector] * 18,
+            out_shape=[field, field, field] + extra + sends(3, 4),
             out_specs=[vector] * (7 + len(extra)),
-            scratch_shapes=[
-                scratch(3, FCAP, LANES),
-                scratch(4, HALF, LANES),
-            ],
+            scratch_shapes=[scratch(4, HALF, LANES)],
             compiler_params=PARAMS,
             name="middle",
         )(
-            fine_slots,
             moved,
             veloc,
             inner,
@@ -735,6 +754,7 @@
             inverse_mass,
             fixed,
             index,
+            collect,
             spread,
             peer_index,
             *got,
@@ -747,7 +767,7 @@
         got = swap_all(outs[-4:-2], "dev") + swap_all(outs[-2:], "region")
     state = (disp_near, moved, veloc, summed, inverse_mass)
     last_scratch = [
-        scratch(2, 3, FIRST, LANES),
+        scratch(2, 4 * FIRST, LANES),
         scratch(2, 3, FIRST * LANES),
         pltpu.SemaphoreType.DMA((2,)),
     ]

time: 64.7 us -> 61.3 us (0.947); the launches traced: 64.6 us -> 60.2 us
  Pallas kernels: 15.1 us -> 11.8 us
  starting transfers between devices: 32.8 us -> 29.9 us
  waiting for transfers between devices: 15 us -> 17.7 us
  local copies, waits for them, and re-layouts: 0.66 us -> 0.01 us
    pallas_call x5, Pallas kernels: 11.9 us -> 8.92 us  [the longest x3 4.03 us: body(): pl.pallas_call(functools.partial(middle_kernel, opening), in_specs=[vecto...]
    ppermute x16, starting transfers between devices: 32.8 us -> 29.9 us  [swap_all(): lax.ppermute(sent, axis, swap_pairs(lax.axis_size(axis), colour))]
    ppermute x16, waiting for transfers between devices: 15 us -> 17.7 us  [swap_all(): lax.ppermute(sent, axis, swap_pairs(lax.axis_size(axis), colour))]
    unnamed x6 -> x4, local copies, waits for them, and re-layouts: 0.66 us -> 0.01 us
  transfers between devices with their start and end apart: 16 -> 16, of which waited for: 3 -> 5; matrix products, arithmetic and copies ran while one was open for 0% -> 0% of each run, Pallas kernels for 8% -> 7%
where the time goes in v3:
time: 61.3 us; the launch traced here: 60.2 us
  starting transfers between devices  29.9 us (49%)
  waiting for transfers between devices  17.7 us (29%)
  Pallas kernels  11.8 us (19%)
  between operations  0.87 us (1%)
    ppermute x16, starting transfers between devices, swap_all(): lax.ppermute(sent, axis, swap_pairs(lax.axis_size(axis), colour))  29.9 us
    ppermute x16, waiting for transfers between devices, swap_all(): lax.ppermute(sent, axis, swap_pairs(lax.axis_size(axis), colour))  17.7 us
    pallas_call x3, Pallas kernels, body(): pl.pallas_call(functools.partial(middle_kernel, opening), in_specs=[vecto...  4.03 us
    pallas_call x1, Pallas kernels, body(): pl.pallas_call(inner_kernel, in_specs=[raw] + [vector] * 12, out_shape=[f...  2.52 us
    pallas_call x1, Pallas kernels, body(): pl.pallas_call(dev_edge_kernel, in_specs=[raw] * 11, out_shape=[shape(x.s...  2.36 us
  transfers between devices with their start and end apart: 16, of which 5 were waited for; matrix products, arithmetic and copies ran while one was open for 0% of the time, Pallas kernels for 7%

profile of v3, /device:TPU:0, one launch (start us, length us, event | category | flops | bytes accessed | tf_op | source)
XLA Modules:
  0.0 60.2 jit_solution(17139675684908179136)
XLA Ops:
  0.6 2.4 %edge_dev.1 = (f32[3,20480]{1,0:T(4,128)S(1)}, f32[3,20480]{1,0:T(4,128)S(1)}, f32[3,320,125]{2,1,0:T(8,128)S(1)}, f32[320,125]{1,0:T(8,128)S(1)}, f32[320,125]{...) custom-call(f32[3,20480]{1,0:T(4,128)} %refs_0_.1, ...), custom_call_target="tpu_custom_call" | custom-call | tf_op jit(solution)/shard_map/edge_dev/pallas_call | solution.py:675
  3.0 9.6 %collective-permute-start = (f32[80,128]{1,0:T(8,128)S(1)}, f32[80,128]{1,0:T(8,128)S(1)}, u32[]{:S(2)}, u32[]{:S(2)}) collective-permute-start(f32[80,128]{1,0:T(8,128)S(1)} %get-tuple-element.74), channel_id=1, source_target_pairs={{1,2},{2,1},{3,4},{4,3},{5,6},{6,5},{7,8},{8,7},{9,10},{10,9},{11,... | collective-permute-start | bytes 122888 | tf_op jit(solution)/shard_map/ppermute | solution.py:618
  12.6 0.0 collective-permute-start.1
  12.6 1.1 %edge_region.1 = (f32[4,40,128]{2,1,0:T(8,128)S(1)}, f32[4,8,128]{2,1,0:T(8,128)S(1)}, f32[80,128]{1,0:T(8,128)S(1)}, f32[80,128]{1,0:T(8,128)S(1)}) custom-call(f32[3,20480]{1,0:T(4,128)S(1)} %get-tuple-element.52.refs_0_.disp_in, f32[3,320,125]{2,1,0:T(8,128)S(1)} %get-tuple-element.55.refs_1_.jac_ref, f32[320,125]{1,0:T(8,128)S(1)} %get-tuple-element.56.refs_2_.lam_ref, ...), custom_call_target="tpu_custom_call" | custom-call | tf_op jit(solution)/shard_map/edge_region/pallas_call | solution.py:688
  13.7 2.0 %collective-permute-start.2 = (f32[80,128]{1,0:T(8,128)S(1)}, f32[80,128]{1,0:T(8,128)S(1)}, u32[]{:S(2)}, u32[]{:S(2)}) collective-permute-start(f32[80,128]{1,0:T(8,128)S(1)} %get-tuple-element.76), channel_id=1, source_target_pairs={{64,128},{128,64},{192,0},{0,192},{65,129},{129,65},{193,1},{1,193... | collective-permute-start | bytes 122888 | tf_op jit(solution)/shard_map/ppermute | solution.py:618
  15.7 0.1 collective-permute-start.3
  15.8 2.5 %inner.1 = (f32[3,160,128]{2,1,0:T(8,128)S(1)}, f32[4,80,128]{2,1,0:T(8,128)S(1)}, f32[5,80,128]{2,1,0:T(8,128)S(1)}, s32[2,80,128]{2,1,0:T(8,128)S(1)}, bf16[16...) custom-call(s32[80]{0:T(128)} %slots_in.1, ...), custom_call_target="tpu_custom_call" | custom-call | tf_op jit(solution)/shard_map/inner/pallas_call | solution.py:699
  18.4 0.0 collective-permute-done.got0
  18.4 0.0 collective-permute-done.1.got1
  18.4 1.6 %collective-permute-done.2.got2 = f32[80,128]{1,0:T(8,128)S(1)} collective-permute-done((f32[80,128]{1,0:T(8,128)S(1)}, f32[80,128]{1,0:T(8,128)S(1)}, u32[]{:S(2)}, u32[]{:S(2)}) %collective-permute-start.2) | collective-permute-done | bytes 40992 | tf_op jit(solution)/shard_map/ppermute | solution.py:618
  20.0 0.3 collective-permute-done.3.got3
  20.3 1.4 %middle.3 = (f32[3,160,128]{2,1,0:T(8,128)S(1)}, f32[3,160,128]{2,1,0:T(8,128)S(1)}, f32[3,160,128]{2,1,0:T(8,128)S(1)}, f32[160,128]{1,0:T(8,128)S(1)}, f32[60,...) custom-call(s32[2,80,128]{2,1,0:T(8,128)S(1)} %get-tuple-element.65.moved_ref.summed_ref., ...), custom_call_target="tpu_custom_call" | custom-call | tf_op jit(solution)/shard_map/middle/pallas_call | solution.py:740
  21.7 4.0 %collective-permute-start.4 = (f32[60,128]{1,0:T(8,128)S(1)}, f32[60,128]{1,0:T(8,128)S(1)}, u32[]{:S(2)}, u32[]{:S(2)}) collective-permute-start(f32[60,128]{1,0:T(8,128)S(1)} %get-tuple-element.82), channel_id=1, source_target_pairs={{1,2},{2,1},{3,4},{4,3},{5,6},{6,5},{7,8},{8,7},{9,10},{10,9},{11,... | collective-permute-start | bytes 92168 | tf_op jit(solution)/shard_map/ppermute | solution.py:618
  25.7 0.0 collective-permute-start.5
  25.7 1.9 %collective-permute-start.6 = (f32[60,128]{1,0:T(8,128)S(1)}, f32[60,128]{1,0:T(8,128)S(1)}, u32[]{:S(2)}, u32[]{:S(2)}) collective-permute-start(f32[60,128]{1,0:T(8,128)S(1)} %get-tuple-element.84), channel_id=1, source_target_pairs={{64,128},{128,64},{192,0},{0,192},{65,129},{129,65},{193,1},{1,193... | collective-permute-start | bytes 92168 | tf_op jit(solution)/shard_map/ppermute | solution.py:618
  27.6 0.1 collective-permute-start.7
  27.7 5.5 %collective-permute-done.4.got0 = f32[60,128]{1,0:T(8,128)S(1)} collective-permute-done((f32[60,128]{1,0:T(8,128)S(1)}, f32[60,128]{1,0:T(8,128)S(1)}, u32[]{:S(2)}, u32[]{:S(2)}) %collective-permute-start.4) | collective-permute-done | bytes 30752 | tf_op jit(solution)/shard_map/ppermute | solution.py:618
  33.2 0.0 collective-permute-done.5.got1
  33.2 0.0 collective-permute-done.6.got2
  33.2 1.3 %middle.4 = (f32[3,160,128]{2,1,0:T(8,128)S(1)}, f32[3,160,128]{2,1,0:T(8,128)S(1)}, f32[3,160,128]{2,1,0:T(8,128)S(1)}, f32[60,128]{1,0:T(8,128)S(1)}, f32[60,1...) custom-call(f32[3,160,128]{2,1,0:T(8,128)S(1)} %get-tuple-element.78.moved_ref, ...), custom_call_target="tpu_custom_call" | custom-call | tf_op jit(solution)/shard_map/middle/pallas_call | solution.py:740
  34.6 4.0 %collective-permute-start.8 = (f32[60,128]{1,0:T(8,128)S(1)}, f32[60,128]{1,0:T(8,128)S(1)}, u32[]{:S(2)}, u32[]{:S(2)}) collective-permute-start(f32[60,128]{1,0:T(8,128)S(1)} %get-tuple-element.89), channel_id=1, source_target_pairs={{1,2},{2,1},{3,4},{4,3},{5,6},{6,5},{7,8},{8,7},{9,10},{10,9},{11,... | collective-permute-start | bytes 92168 | tf_op jit(solution)/shard_map/ppermute | solution.py:618
  38.6 0.0 collective-permute-start.9
  38.6 1.9 %collective-permute-start.10 = (f32[60,128]{1,0:T(8,128)S(1)}, f32[60,128]{1,0:T(8,128)S(1)}, u32[]{:S(2)}, u32[]{:S(2)}) collective-permute-start(f32[60,128]{1,0:T(8,128)S(1)} %get-tuple-element.91), channel_id=1, source_target_pairs={{64,128},{128,64},{192,0},{0,192},{65,129},{129,65},{193,1},{1,193... | collective-permute-start | bytes 92168 | tf_op jit(solution)/shard_map/ppermute | solution.py:618
  40.5 0.1 collective-permute-start.11
  40.6 5.5 %collective-permute-done.8.got0 = f32[60,128]{1,0:T(8,128)S(1)} collective-permute-done((f32[60,128]{1,0:T(8,128)S(1)}, f32[60,128]{1,0:T(8,128)S(1)}, u32[]{:S(2)}, u32[]{:S(2)}) %collective-permute-start.8) | collective-permute-done | bytes 30752 | tf_op jit(solution)/shard_map/ppermute | solution.py:618
  46.1 1.3 %middle.5 = (f32[3,160,128]{2,1,0:T(8,128)S(1)}, f32[3,160,128]{2,1,0:T(8,128)S(1)}, f32[3,160,128]{2,1,0:T(8,128)S(1)}, f32[60,128]{1,0:T(8,128)S(1)}, f32[60,1...) custom-call(f32[3,160,128]{2,1,0:T(8,128)S(1)} %get-tuple-element.86.moved_ref, ...), custom_call_target="tpu_custom_call" | custom-call | tf_op jit(solution)/shard_map/middle/pallas_call | solution.py:740
  47.5 4.1 %collective-permute-start.12 = (f32[60,128]{1,0:T(8,128)S(1)}, f32[60,128]{1,0:T(8,128)S(1)}, u32[]{:S(2)}, u32[]{:S(2)}) collective-permute-start(f32[60,128]{1,0:T(8,128)S(1)} %get-tuple-element.96), channel_id=1, source_target_pairs={{1,2},{2,1},{3,4},{4,3},{5,6},{6,5},{7,8},{8,7},{9,10},{10,9},{11,... | collective-permute-start | bytes 92168 | tf_op jit(solution)/shard_map/ppermute | solution.py:618
  51.5 1.9 %collective-permute-start.14 = (f32[60,128]{1,0:T(8,128)S(1)}, f32[60,128]{1,0:T(8,128)S(1)}, u32[]{:S(2)}, u32[]{:S(2)}) collective-permute-start(f32[60,128]{1,0:T(8,128)S(1)} %get-tuple-element.98), channel_id=1, source_target_pairs={{64,128},{128,64},{192,0},{0,192},{65,129},{129,65},{193,1},{1,193... | collective-permute-start | bytes 92168 | tf_op jit(solution)/shard_map/ppermute | solution.py:618
  53.5 0.1 collective-permute-start.15
  53.5 0.8 %last_inner.1 = (f32[3,20480]{1,0:T(4,128)}, f32[3,20480]{1,0:T(4,128)}) custom-call(f32[3,20480]{1,0:T(4,128)S(1)} %get-tuple-element.52.refs_0_.disp_in, f32[3,160,128]{2,1,0:T(8,128)S(1)} %get-tuple-element.93.moved_ref, f32[3,160,128]{2,1,0:T(8,128)S(1)} %get-tuple-element.94.veloc_ref, f32[3,160,128]{2,1,0:T(8,128)S(1)} %get-tuple-element.95.summed_ref, ...), custom_call_target="tpu_custom_call" | custom-call | tf_op jit(solution)/shard_map/last_inner/pallas_call | solution.py:774
  54.3 4.7 %collective-permute-done.12.got0 = f32[60,128]{1,0:T(8,128)S(1)} collective-permute-done((f32[60,128]{1,0:T(8,128)S(1)}, f32[60,128]{1,0:T(8,128)S(1)}, u32[]{:S(2)}, u32[]{:S(2)}) %collective-permute-start.12) | collective-permute-done | bytes 30752 | tf_op jit(solution)/shard_map/ppermute | solution.py:618
  59.1 1.0 %last_edge.1 = (f32[3,20480]{1,0:T(4,128)}, f32[3,20480]{1,0:T(4,128)}) custom-call(f32[3,20480]{1,0:T(4,128)S(1)} %get-tuple-element.52.refs_0_.disp_in, f32[3,160,128]{2,1,0:T(8,128)S(1)} %get-tuple-element.93.moved_ref, f32[3,160,128]{2,1,0:T(8,128)S(1)} %get-tuple-element.94.veloc_ref, ...), custom_call_target="tpu_custom_call", output_to_operand_aliasing={{0}: (10, {}), {1}: (11, {})} | custom-call | tf_op jit(solution)/shard_map/last_edge/pallas_call | solution.py:783
  (12 shorter events, 0.0 us)
Async XLA Ops:
  3.0 15.4 %collective-permute-start = (f32[80,128]{1,0:T(8,128)S(1)}, f32[80,128]{1,0:T(8,128)S(1)}, u32[]{:S(2)}, u32[]{:S(2)}) collective-permute-start(f32[80,128]{1,0:T(8,128)S(1)} %get-tuple-element.74), channel_id=1, source_target_pairs={{1,2},{2,1},{3,4},{4,3},{5,6},{6,5},{7,8},{8,7},{9,10},{10,9},{11,... | collective-permute-start | bytes 122888 | tf_op jit(solution)/shard_map/ppermute | solution.py:618
  12.6 5.8 %collective-permute-start.1 = (f32[80,128]{1,0:T(8,128)S(1)}, f32[80,128]{1,0:T(8,128)S(1)}, u32[]{:S(2)}, u32[]{:S(2)}) collective-permute-start(f32[80,128]{1,0:T(8,128)S(1)} %get-tuple-element.75), channel_id=1, source_target_pairs={{0,1},{1,0},{2,3},{3,2},{4,5},{5,4},{6,7},{7,6},{8,9},{9,8},{10,11... | collective-permute-start | bytes 122888 | tf_op jit(solution)/shard_map/ppermute | solution.py:618
  13.7 6.2 %collective-permute-start.2 = (f32[80,128]{1,0:T(8,128)S(1)}, f32[80,128]{1,0:T(8,128)S(1)}, u32[]{:S(2)}, u32[]{:S(2)}) collective-permute-start(f32[80,128]{1,0:T(8,128)S(1)} %get-tuple-element.76), channel_id=1, source_target_pairs={{64,128},{128,64},{192,0},{0,192},{65,129},{129,65},{193,1},{1,193... | collective-permute-start | bytes 122888 | tf_op jit(solution)/shard_map/ppermute | solution.py:618
  15.7 4.6 %collective-permute-start.3 = (f32[80,128]{1,0:T(8,128)S(1)}, f32[80,128]{1,0:T(8,128)S(1)}, u32[]{:S(2)}, u32[]{:S(2)}) collective-permute-start(f32[80,128]{1,0:T(8,128)S(1)} %get-tuple-element.77), channel_id=1, source_target_pairs={{0,64},{64,0},{128,192},{192,128},{1,65},{65,1},{129,193},{193,129... | collective-permute-start | bytes 122888 | tf_op jit(solution)/shard_map/ppermute | solution.py:618
  15.8 4.5 %copy-start = (bf16[384,384]{1,0:T(8,128)(2,1)S(1)}, bf16[384,384]{1,0:T(8,128)(2,1)}, u32[]{:S(2)}) copy-start(bf16[384,384]{1,0:T(8,128)(2,1)} %constant.4.clone.refs_8_.grad_ref) | copy-start | bytes 884740
  15.8 4.5 %copy-start.1 = (bf16[384,256]{1,0:T(8,128)(2,1)S(1)}, bf16[384,256]{1,0:T(8,128)(2,1)}, u32[]{:S(2)}) copy-start(bf16[384,256]{1,0:T(8,128)(2,1)} %constant.5.clone.refs_9_.back_ref) | copy-start | bytes 589828
  21.7 11.6 %collective-permute-start.4 = (f32[60,128]{1,0:T(8,128)S(1)}, f32[60,128]{1,0:T(8,128)S(1)}, u32[]{:S(2)}, u32[]{:S(2)}) collective-permute-start(f32[60,128]{1,0:T(8,128)S(1)} %get-tuple-element.82), channel_id=1, source_target_pairs={{1,2},{2,1},{3,4},{4,3},{5,6},{6,5},{7,8},{8,7},{9,10},{10,9},{11,... | collective-permute-start | bytes 92168 | tf_op jit(solution)/shard_map/ppermute | solution.py:618
  25.7 7.6 %collective-permute-start.5 = (f32[60,128]{1,0:T(8,128)S(1)}, f32[60,128]{1,0:T(8,128)S(1)}, u32[]{:S(2)}, u32[]{:S(2)}) collective-permute-start(f32[60,128]{1,0:T(8,128)S(1)} %get-tuple-element.83), channel_id=1, source_target_pairs={{0,1},{1,0},{2,3},{3,2},{4,5},{5,4},{6,7},{7,6},{8,9},{9,8},{10,11... | collective-permute-start | bytes 92168 | tf_op jit(solution)/shard_map/ppermute | solution.py:618
  25.7 7.6 %collective-permute-start.6 = (f32[60,128]{1,0:T(8,128)S(1)}, f32[60,128]{1,0:T(8,128)S(1)}, u32[]{:S(2)}, u32[]{:S(2)}) collective-permute-start(f32[60,128]{1,0:T(8,128)S(1)} %get-tuple-element.84), channel_id=1, source_target_pairs={{64,128},{128,64},{192,0},{0,192},{65,129},{129,65},{193,1},{1,193... | collective-permute-start | bytes 92168 | tf_op jit(solution)/shard_map/ppermute | solution.py:618
  27.6 5.6 %collective-permute-start.7 = (f32[60,128]{1,0:T(8,128)S(1)}, f32[60,128]{1,0:T(8,128)S(1)}, u32[]{:S(2)}, u32[]{:S(2)}) collective-permute-start(f32[60,128]{1,0:T(8,128)S(1)} %get-tuple-element.85), channel_id=1, source_target_pairs={{0,64},{64,0},{128,192},{192,128},{1,65},{65,1},{129,193},{193,129... | collective-permute-start | bytes 92168 | tf_op jit(solution)/shard_map/ppermute | solution.py:618
  34.6 11.6 %collective-permute-start.8 = (f32[60,128]{1,0:T(8,128)S(1)}, f32[60,128]{1,0:T(8,128)S(1)}, u32[]{:S(2)}, u32[]{:S(2)}) collective-permute-start(f32[60,128]{1,0:T(8,128)S(1)} %get-tuple-element.89), channel_id=1, source_target_pairs={{1,2},{2,1},{3,4},{4,3},{5,6},{6,5},{7,8},{8,7},{9,10},{10,9},{11,... | collective-permute-start | bytes 92168 | tf_op jit(solution)/shard_map/ppermute | solution.py:618
  38.6 7.5 %collective-permute-start.9 = (f32[60,128]{1,0:T(8,128)S(1)}, f32[60,128]{1,0:T(8,128)S(1)}, u32[]{:S(2)}, u32[]{:S(2)}) collective-permute-start(f32[60,128]{1,0:T(8,128)S(1)} %get-tuple-element.90), channel_id=1, source_target_pairs={{0,1},{1,0},{2,3},{3,2},{4,5},{5,4},{6,7},{7,6},{8,9},{9,8},{10,11... | collective-permute-start | bytes 92168 | tf_op jit(solution)/shard_map/ppermute | solution.py:618
  38.6 7.5 %collective-permute-start.10 = (f32[60,128]{1,0:T(8,128)S(1)}, f32[60,128]{1,0:T(8,128)S(1)}, u32[]{:S(2)}, u32[]{:S(2)}) collective-permute-start(f32[60,128]{1,0:T(8,128)S(1)} %get-tuple-element.91), channel_id=1, source_target_pairs={{64,128},{128,64},{192,0},{0,192},{65,129},{129,65},{193,1},{1,193... | collective-permute-start | bytes 92168 | tf_op jit(solution)/shard_map/ppermute | solution.py:618
  40.5 5.6 %collective-permute-start.11 = (f32[60,128]{1,0:T(8,128)S(1)}, f32[60,128]{1,0:T(8,128)S(1)}, u32[]{:S(2)}, u32[]{:S(2)}) collective-permute-start(f32[60,128]{1,0:T(8,128)S(1)} %get-tuple-element.92), channel_id=1, source_target_pairs={{0,64},{64,0},{128,192},{192,128},{1,65},{65,1},{129,193},{193,129... | collective-permute-start | bytes 92168 | tf_op jit(solution)/shard_map/ppermute | solution.py:618
  47.5 11.6 %collective-permute-start.12 = (f32[60,128]{1,0:T(8,128)S(1)}, f32[60,128]{1,0:T(8,128)S(1)}, u32[]{:S(2)}, u32[]{:S(2)}) collective-permute-start(f32[60,128]{1,0:T(8,128)S(1)} %get-tuple-element.96), channel_id=1, source_target_pairs={{1,2},{2,1},{3,4},{4,3},{5,6},{6,5},{7,8},{8,7},{9,10},{10,9},{11,... | collective-permute-start | bytes 92168 | tf_op jit(solution)/shard_map/ppermute | solution.py:618
  51.5 7.5 %collective-permute-start.13 = (f32[60,128]{1,0:T(8,128)S(1)}, f32[60,128]{1,0:T(8,128)S(1)}, u32[]{:S(2)}, u32[]{:S(2)}) collective-permute-start(f32[60,128]{1,0:T(8,128)S(1)} %get-tuple-element.97), channel_id=1, source_target_pairs={{0,1},{1,0},{2,3},{3,2},{4,5},{5,4},{6,7},{7,6},{8,9},{9,8},{10,11... | collective-permute-start | bytes 92168 | tf_op jit(solution)/shard_map/ppermute | solution.py:618
  51.5 7.5 %collective-permute-start.14 = (f32[60,128]{1,0:T(8,128)S(1)}, f32[60,128]{1,0:T(8,128)S(1)}, u32[]{:S(2)}, u32[]{:S(2)}) collective-permute-start(f32[60,128]{1,0:T(8,128)S(1)} %get-tuple-element.98), channel_id=1, source_target_pairs={{64,128},{128,64},{192,0},{0,192},{65,129},{129,65},{193,1},{1,193... | collective-permute-start | bytes 92168 | tf_op jit(solution)/shard_map/ppermute | solution.py:618
  53.5 5.6 %collective-permute-start.15 = (f32[60,128]{1,0:T(8,128)S(1)}, f32[60,128]{1,0:T(8,128)S(1)}, u32[]{:S(2)}, u32[]{:S(2)}) collective-permute-start(f32[60,128]{1,0:T(8,128)S(1)} %get-tuple-element.99), channel_id=1, source_target_pairs={{0,64},{64,0},{128,192},{192,128},{1,65},{65,1},{129,193},{193,129... | collective-permute-start | bytes 92168 | tf_op jit(solution)/shard_map/ppermute | solution.py:618

commit v4 on v3

--- a/solution.py
+++ b/solution.py
@@ -160,7 +160,7 @@
 
 def send_pair(shared, picks, odd, staged_ref, outs):
     for c, values in enumerate(shared):
-        staged_ref[c] = lane_pick(values, picks)
+        staged_ref[c, 0:HALF, :] = lane_pick(values, picks)
     for c in range(len(shared)):
         part = [staged_ref[c, GROUPS * p : GROUPS * (p + 1), :] for p in range(2)]
         put = pl.ds(c * GROUPS, GROUPS)
@@ -173,7 +173,7 @@
         got = [a[c * GROUPS : (c + 1) * GROUPS, :] for a in arrived]
         staged_ref[c, 0:GROUPS, :] = jnp.where(odd, got[1][...], got[0][...])
         staged_ref[c, GROUPS : 2 * GROUPS, :] = jnp.where(odd, got[0][...], got[1][...])
-    return [lane_pick(staged_ref[c], places) for c in range(channels)]
+    return [lane_pick(staged_ref[c, 0:HALF, :], places) for c in range(channels)]
 
 
 def odd_place(axis):
@@ -655,7 +655,7 @@
     )
 
     def sends(channels, count):
-        return [shape((channels * GROUPS, LANES))] * count
+        return [shape((-(-channels * GROUPS // 8) * 8, LANES))] * count
 
     got, bases = [], []
     raw = pl.BlockSpec(memory_space=pltpu.HBM)
@@ -669,7 +669,7 @@
         scratch(LANES, LANES),
         scratch(4 * (WIDE + 8), LANES),
         scratch(HALF, LANES, kind=jnp.int32),
-        scratch(4, HALF, LANES),
+        scratch(4, HALF + 8, LANES),
         scratch(4, WIDE + 8, LANES),
     ]
     outs = pl.pallas_call(
@@ -712,10 +712,10 @@
         scratch_shapes=[
             scratch(6, ELEM + 8, LANES),
             scratch(ELEM + 8, LANES, kind=jnp.int32),
-            scratch(ELEM // 2, LANES, kind=jnp.int32),
+            scratch(ELEM // 2 + 8, LANES, kind=jnp.int32),
             scratch(LANES, LANES),
             scratch(4 * (FIRST + 8), LANES),
-            scratch(4 * ROWS, LANES),
+            scratch(4 * ROWS + 8, LANES),
             scratch(LANES, LANES, kind=jnp.int32),
             scratch(4, FIRST + 8, LANES),
             scratch(2 * LANES, 2 * LANES),
@@ -742,7 +742,7 @@
             in_specs=[vector] * 18,
             out_shape=[field, field, field] + extra + sends(3, 4),
             out_specs=[vector] * (7 + len(extra)),
-            scratch_shapes=[scratch(4, HALF, LANES)],
+            scratch_shapes=[scratch(4, HALF + 8, LANES)],
             compiler_params=PARAMS,
             name="middle",
         )(
@@ -767,7 +767,7 @@
         got = swap_all(outs[-4:-2], "dev") + swap_all(outs[-2:], "region")
     state = (disp_near, moved, veloc, summed, inverse_mass)
     last_scratch = [
-        scratch(2, 4 * FIRST, LANES),
+        scratch(2, 4 * FIRST + 8, LANES),
         scratch(2, 3, FIRST * LANES),
         pltpu.SemaphoreType.DMA((2,)),
     ]
@@ -785,7 +785,7 @@
         in_specs=[vector] * 10 + [raw] * 2,
         out_shape=[shape((3, NLOC)), shape((3, NLOC))],
         out_specs=[raw] * 2,
-        scratch_shapes=[scratch(4, HALF, LANES)] + last_scratch,
+        scratch_shapes=[scratch(4, HALF + 8, LANES)] + last_scratch,
         input_output_aliases={10: 0, 11: 1},
         compiler_params=PARAMS,
         name="last_edge",

time: 61.3 us -> 61.4 us (level)
  no operation moved by 1% of the time
where the time goes in v4:
time: 61.4 us; the launch traced here: 60.2 us
  starting transfers between devices  29.9 us (49%)
  waiting for transfers between devices  17.6 us (29%)
  Pallas kernels  11.8 us (19%)
  between operations  0.87 us (1%)
    ppermute x16, starting transfers between devices, swap_all(): lax.ppermute(sent, axis, swap_pairs(lax.axis_size(axis), colour))  29.9 us
    ppermute x16, waiting for transfers between devices, swap_all(): lax.ppermute(sent, axis, swap_pairs(lax.axis_size(axis), colour))  17.6 us
    pallas_call x3, Pallas kernels, body(): pl.pallas_call(functools.partial(middle_kernel, opening), in_specs=[vecto...  4.03 us
    pallas_call x1, Pallas kernels, body(): pl.pallas_call(inner_kernel, in_specs=[raw] + [vector] * 12, out_shape=[f...  2.52 us
    pallas_call x1, Pallas kernels, body(): pl.pallas_call(dev_edge_kernel, in_specs=[raw] * 11, out_shape=[shape(x.s...  2.36 us
  transfers between devices with their start and end apart: 16, of which 5 were waited for; matrix products, arithmetic and copies ran while one was open for 0% of the time, Pallas kernels for 7%

profile of v4, /device:TPU:0, one launch (start us, length us, event | category | flops | bytes accessed | tf_op | source)
XLA Modules:
  0.0 60.2 jit_solution(11429613403355412107)
XLA Ops:
  0.6 2.4 %edge_dev.1 = (f32[3,20480]{1,0:T(4,128)S(1)}, f32[3,20480]{1,0:T(4,128)S(1)}, f32[3,320,125]{2,1,0:T(8,128)S(1)}, f32[320,125]{1,0:T(8,128)S(1)}, f32[320,125]{...) custom-call(f32[3,20480]{1,0:T(4,128)} %refs_0_.1, ...), custom_call_target="tpu_custom_call" | custom-call | tf_op jit(solution)/shard_map/edge_dev/pallas_call | solution.py:675
  3.0 9.6 %collective-permute-start = (f32[80,128]{1,0:T(8,128)S(1)}, f32[80,128]{1,0:T(8,128)S(1)}, u32[]{:S(2)}, u32[]{:S(2)}) collective-permute-start(f32[80,128]{1,0:T(8,128)S(1)} %get-tuple-element.74), channel_id=1, source_target_pairs={{1,2},{2,1},{3,4},{4,3},{5,6},{6,5},{7,8},{8,7},{9,10},{10,9},{11,... | collective-permute-start | bytes 122888 | tf_op jit(solution)/shard_map/ppermute | solution.py:618
  12.6 0.0 collective-permute-start.1
  12.6 1.1 %edge_region.1 = (f32[4,40,128]{2,1,0:T(8,128)S(1)}, f32[4,8,128]{2,1,0:T(8,128)S(1)}, f32[80,128]{1,0:T(8,128)S(1)}, f32[80,128]{1,0:T(8,128)S(1)}) custom-call(f32[3,20480]{1,0:T(4,128)S(1)} %get-tuple-element.52.refs_0_.disp_in, f32[3,320,125]{2,1,0:T(8,128)S(1)} %get-tuple-element.55.refs_1_.jac_ref, f32[320,125]{1,0:T(8,128)S(1)} %get-tuple-element.56.refs_2_.lam_ref, ...), custom_call_target="tpu_custom_call" | custom-call | tf_op jit(solution)/shard_map/edge_region/pallas_call | solution.py:688
  13.7 2.0 %collective-permute-start.2 = (f32[80,128]{1,0:T(8,128)S(1)}, f32[80,128]{1,0:T(8,128)S(1)}, u32[]{:S(2)}, u32[]{:S(2)}) collective-permute-start(f32[80,128]{1,0:T(8,128)S(1)} %get-tuple-element.76), channel_id=1, source_target_pairs={{64,128},{128,64},{192,0},{0,192},{65,129},{129,65},{193,1},{1,193... | collective-permute-start | bytes 122888 | tf_op jit(solution)/shard_map/ppermute | solution.py:618
  15.7 0.1 collective-permute-start.3
  15.8 2.5 %inner.1 = (f32[3,160,128]{2,1,0:T(8,128)S(1)}, f32[4,80,128]{2,1,0:T(8,128)S(1)}, f32[5,80,128]{2,1,0:T(8,128)S(1)}, s32[2,80,128]{2,1,0:T(8,128)S(1)}, bf16[16...) custom-call(s32[80]{0:T(128)} %slots_in.1, ...), custom_call_target="tpu_custom_call" | custom-call | tf_op jit(solution)/shard_map/inner/pallas_call | solution.py:699
  18.4 0.0 collective-permute-done.got0
  18.4 1.6 %collective-permute-done.2.got2 = f32[80,128]{1,0:T(8,128)S(1)} collective-permute-done((f32[80,128]{1,0:T(8,128)S(1)}, f32[80,128]{1,0:T(8,128)S(1)}, u32[]{:S(2)}, u32[]{:S(2)}) %collective-permute-start.2) | collective-permute-done | bytes 40992 | tf_op jit(solution)/shard_map/ppermute | solution.py:618
  20.0 0.3 collective-permute-done.3.got3
  20.3 1.4 %middle.3 = (f32[3,160,128]{2,1,0:T(8,128)S(1)}, f32[3,160,128]{2,1,0:T(8,128)S(1)}, f32[3,160,128]{2,1,0:T(8,128)S(1)}, f32[160,128]{1,0:T(8,128)S(1)}, f32[64,...) custom-call(s32[2,80,128]{2,1,0:T(8,128)S(1)} %get-tuple-element.65.moved_ref.summed_ref., ...), custom_call_target="tpu_custom_call" | custom-call | tf_op jit(solution)/shard_map/middle/pallas_call | solution.py:740
  21.7 4.0 %collective-permute-start.4 = (f32[64,128]{1,0:T(8,128)S(1)}, f32[64,128]{1,0:T(8,128)S(1)}, u32[]{:S(2)}, u32[]{:S(2)}) collective-permute-start(f32[64,128]{1,0:T(8,128)S(1)} %get-tuple-element.82), channel_id=1, source_target_pairs={{1,2},{2,1},{3,4},{4,3},{5,6},{6,5},{7,8},{8,7},{9,10},{10,9},{11,... | collective-permute-start | bytes 98312 | tf_op jit(solution)/shard_map/ppermute | solution.py:618
  25.7 1.9 %collective-permute-start.6 = (f32[64,128]{1,0:T(8,128)S(1)}, f32[64,128]{1,0:T(8,128)S(1)}, u32[]{:S(2)}, u32[]{:S(2)}) collective-permute-start(f32[64,128]{1,0:T(8,128)S(1)} %get-tuple-element.84), channel_id=1, source_target_pairs={{64,128},{128,64},{192,0},{0,192},{65,129},{129,65},{193,1},{1,193... | collective-permute-start | bytes 98312 | tf_op jit(solution)/shard_map/ppermute | solution.py:618
  27.6 0.1 collective-permute-start.7
  27.7 5.5 %collective-permute-done.4.got0 = f32[64,128]{1,0:T(8,128)S(1)} collective-permute-done((f32[64,128]{1,0:T(8,128)S(1)}, f32[64,128]{1,0:T(8,128)S(1)}, u32[]{:S(2)}, u32[]{:S(2)}) %collective-permute-start.4) | collective-permute-done | bytes 32800 | tf_op jit(solution)/shard_map/ppermute | solution.py:618
  33.2 0.0 collective-permute-done.7.got3
  33.2 1.3 %middle.4 = (f32[3,160,128]{2,1,0:T(8,128)S(1)}, f32[3,160,128]{2,1,0:T(8,128)S(1)}, f32[3,160,128]{2,1,0:T(8,128)S(1)}, f32[64,128]{1,0:T(8,128)S(1)}, f32[64,1...) custom-call(f32[3,160,128]{2,1,0:T(8,128)S(1)} %get-tuple-element.78.moved_ref, ...), custom_call_target="tpu_custom_call" | custom-call | tf_op jit(solution)/shard_map/middle/pallas_call | solution.py:740
  34.6 4.0 %collective-permute-start.8 = (f32[64,128]{1,0:T(8,128)S(1)}, f32[64,128]{1,0:T(8,128)S(1)}, u32[]{:S(2)}, u32[]{:S(2)}) collective-permute-start(f32[64,128]{1,0:T(8,128)S(1)} %get-tuple-element.89), channel_id=1, source_target_pairs={{1,2},{2,1},{3,4},{4,3},{5,6},{6,5},{7,8},{8,7},{9,10},{10,9},{11,... | collective-permute-start | bytes 98312 | tf_op jit(solution)/shard_map/ppermute | solution.py:618
  38.6 0.0 collective-permute-start.9
  38.6 1.9 %collective-permute-start.10 = (f32[64,128]{1,0:T(8,128)S(1)}, f32[64,128]{1,0:T(8,128)S(1)}, u32[]{:S(2)}, u32[]{:S(2)}) collective-permute-start(f32[64,128]{1,0:T(8,128)S(1)} %get-tuple-element.91), channel_id=1, source_target_pairs={{64,128},{128,64},{192,0},{0,192},{65,129},{129,65},{193,1},{1,193... | collective-permute-start | bytes 98312 | tf_op jit(solution)/shard_map/ppermute | solution.py:618
  40.5 0.1 collective-permute-start.11
  40.6 5.5 %collective-permute-done.8.got0 = f32[64,128]{1,0:T(8,128)S(1)} collective-permute-done((f32[64,128]{1,0:T(8,128)S(1)}, f32[64,128]{1,0:T(8,128)S(1)}, u32[]{:S(2)}, u32[]{:S(2)}) %collective-permute-start.8) | collective-permute-done | bytes 32800 | tf_op jit(solution)/shard_map/ppermute | solution.py:618
  46.1 0.0 collective-permute-done.9.got1
  46.1 0.0 collective-permute-done.10.got2
  46.1 0.0 collective-permute-done.11.got3
  46.1 1.3 %middle.5 = (f32[3,160,128]{2,1,0:T(8,128)S(1)}, f32[3,160,128]{2,1,0:T(8,128)S(1)}, f32[3,160,128]{2,1,0:T(8,128)S(1)}, f32[64,128]{1,0:T(8,128)S(1)}, f32[64,1...) custom-call(f32[3,160,128]{2,1,0:T(8,128)S(1)} %get-tuple-element.86.moved_ref, ...), custom_call_target="tpu_custom_call" | custom-call | tf_op jit(solution)/shard_map/middle/pallas_call | solution.py:740
  47.5 4.0 %collective-permute-start.12 = (f32[64,128]{1,0:T(8,128)S(1)}, f32[64,128]{1,0:T(8,128)S(1)}, u32[]{:S(2)}, u32[]{:S(2)}) collective-permute-start(f32[64,128]{1,0:T(8,128)S(1)} %get-tuple-element.96), channel_id=1, source_target_pairs={{1,2},{2,1},{3,4},{4,3},{5,6},{6,5},{7,8},{8,7},{9,10},{10,9},{11,... | collective-permute-start | bytes 98312 | tf_op jit(solution)/shard_map/ppermute | solution.py:618
  51.5 1.9 %collective-permute-start.14 = (f32[64,128]{1,0:T(8,128)S(1)}, f32[64,128]{1,0:T(8,128)S(1)}, u32[]{:S(2)}, u32[]{:S(2)}) collective-permute-start(f32[64,128]{1,0:T(8,128)S(1)} %get-tuple-element.98), channel_id=1, source_target_pairs={{64,128},{128,64},{192,0},{0,192},{65,129},{129,65},{193,1},{1,193... | collective-permute-start | bytes 98312 | tf_op jit(solution)/shard_map/ppermute | solution.py:618
  53.5 0.1 collective-permute-start.15
  53.5 0.8 %last_inner.1 = (f32[3,20480]{1,0:T(4,128)}, f32[3,20480]{1,0:T(4,128)}) custom-call(f32[3,20480]{1,0:T(4,128)S(1)} %get-tuple-element.52.refs_0_.disp_in, f32[3,160,128]{2,1,0:T(8,128)S(1)} %get-tuple-element.93.moved_ref, f32[3,160,128]{2,1,0:T(8,128)S(1)} %get-tuple-element.94.veloc_ref, f32[3,160,128]{2,1,0:T(8,128)S(1)} %get-tuple-element.95.summed_ref, ...), custom_call_target="tpu_custom_call" | custom-call | tf_op jit(solution)/shard_map/last_inner/pallas_call | solution.py:774
  54.4 4.7 %collective-permute-done.12.got0 = f32[64,128]{1,0:T(8,128)S(1)} collective-permute-done((f32[64,128]{1,0:T(8,128)S(1)}, f32[64,128]{1,0:T(8,128)S(1)}, u32[]{:S(2)}, u32[]{:S(2)}) %collective-permute-start.12) | collective-permute-done | bytes 32800 | tf_op jit(solution)/shard_map/ppermute | solution.py:618
  59.1 1.0 %last_edge.1 = (f32[3,20480]{1,0:T(4,128)}, f32[3,20480]{1,0:T(4,128)}) custom-call(f32[3,20480]{1,0:T(4,128)S(1)} %get-tuple-element.52.refs_0_.disp_in, f32[3,160,128]{2,1,0:T(8,128)S(1)} %get-tuple-element.93.moved_ref, f32[3,160,128]{2,1,0:T(8,128)S(1)} %get-tuple-element.94.veloc_ref, ...), custom_call_target="tpu_custom_call", output_to_operand_aliasing={{0}: (10, {}), {1}: (11, {})} | custom-call | tf_op jit(solution)/shard_map/last_edge/pallas_call | solution.py:783
  (12 shorter events, 0.0 us)
Async XLA Ops:
  3.0 15.4 %collective-permute-start = (f32[80,128]{1,0:T(8,128)S(1)}, f32[80,128]{1,0:T(8,128)S(1)}, u32[]{:S(2)}, u32[]{:S(2)}) collective-permute-start(f32[80,128]{1,0:T(8,128)S(1)} %get-tuple-element.74), channel_id=1, source_target_pairs={{1,2},{2,1},{3,4},{4,3},{5,6},{6,5},{7,8},{8,7},{9,10},{10,9},{11,... | collective-permute-start | bytes 122888 | tf_op jit(solution)/shard_map/ppermute | solution.py:618
  12.6 5.8 %collective-permute-start.1 = (f32[80,128]{1,0:T(8,128)S(1)}, f32[80,128]{1,0:T(8,128)S(1)}, u32[]{:S(2)}, u32[]{:S(2)}) collective-permute-start(f32[80,128]{1,0:T(8,128)S(1)} %get-tuple-element.75), channel_id=1, source_target_pairs={{0,1},{1,0},{2,3},{3,2},{4,5},{5,4},{6,7},{7,6},{8,9},{9,8},{10,11... | collective-permute-start | bytes 122888 | tf_op jit(solution)/shard_map/ppermute | solution.py:618
  13.7 6.3 %collective-permute-start.2 = (f32[80,128]{1,0:T(8,128)S(1)}, f32[80,128]{1,0:T(8,128)S(1)}, u32[]{:S(2)}, u32[]{:S(2)}) collective-permute-start(f32[80,128]{1,0:T(8,128)S(1)} %get-tuple-element.76), channel_id=1, source_target_pairs={{64,128},{128,64},{192,0},{0,192},{65,129},{129,65},{193,1},{1,193... | collective-permute-start | bytes 122888 | tf_op jit(solution)/shard_map/ppermute | solution.py:618
  15.7 4.6 %collective-permute-start.3 = (f32[80,128]{1,0:T(8,128)S(1)}, f32[80,128]{1,0:T(8,128)S(1)}, u32[]{:S(2)}, u32[]{:S(2)}) collective-permute-start(f32[80,128]{1,0:T(8,128)S(1)} %get-tuple-element.77), channel_id=1, source_target_pairs={{0,64},{64,0},{128,192},{192,128},{1,65},{65,1},{129,193},{193,129... | collective-permute-start | bytes 122888 | tf_op jit(solution)/shard_map/ppermute | solution.py:618
  15.8 4.5 %copy-start = (bf16[384,384]{1,0:T(8,128)(2,1)S(1)}, bf16[384,384]{1,0:T(8,128)(2,1)}, u32[]{:S(2)}) copy-start(bf16[384,384]{1,0:T(8,128)(2,1)} %constant.4.clone.refs_8_.grad_ref) | copy-start | bytes 884740
  15.8 4.5 %copy-start.1 = (bf16[384,256]{1,0:T(8,128)(2,1)S(1)}, bf16[384,256]{1,0:T(8,128)(2,1)}, u32[]{:S(2)}) copy-start(bf16[384,256]{1,0:T(8,128)(2,1)} %constant.5.clone.refs_9_.back_ref) | copy-start | bytes 589828
  21.7 11.6 %collective-permute-start.4 = (f32[64,128]{1,0:T(8,128)S(1)}, f32[64,128]{1,0:T(8,128)S(1)}, u32[]{:S(2)}, u32[]{:S(2)}) collective-permute-start(f32[64,128]{1,0:T(8,128)S(1)} %get-tuple-element.82), channel_id=1, source_target_pairs={{1,2},{2,1},{3,4},{4,3},{5,6},{6,5},{7,8},{8,7},{9,10},{10,9},{11,... | collective-permute-start | bytes 98312 | tf_op jit(solution)/shard_map/ppermute | solution.py:618
  25.7 7.6 %collective-permute-start.5 = (f32[64,128]{1,0:T(8,128)S(1)}, f32[64,128]{1,0:T(8,128)S(1)}, u32[]{:S(2)}, u32[]{:S(2)}) collective-permute-start(f32[64,128]{1,0:T(8,128)S(1)} %get-tuple-element.83), channel_id=1, source_target_pairs={{0,1},{1,0},{2,3},{3,2},{4,5},{5,4},{6,7},{7,6},{8,9},{9,8},{10,11... | collective-permute-start | bytes 98312 | tf_op jit(solution)/shard_map/ppermute | solution.py:618
  25.7 7.6 %collective-permute-start.6 = (f32[64,128]{1,0:T(8,128)S(1)}, f32[64,128]{1,0:T(8,128)S(1)}, u32[]{:S(2)}, u32[]{:S(2)}) collective-permute-start(f32[64,128]{1,0:T(8,128)S(1)} %get-tuple-element.84), channel_id=1, source_target_pairs={{64,128},{128,64},{192,0},{0,192},{65,129},{129,65},{193,1},{1,193... | collective-permute-start | bytes 98312 | tf_op jit(solution)/shard_map/ppermute | solution.py:618
  27.6 5.6 %collective-permute-start.7 = (f32[64,128]{1,0:T(8,128)S(1)}, f32[64,128]{1,0:T(8,128)S(1)}, u32[]{:S(2)}, u32[]{:S(2)}) collective-permute-start(f32[64,128]{1,0:T(8,128)S(1)} %get-tuple-element.85), channel_id=1, source_target_pairs={{0,64},{64,0},{128,192},{192,128},{1,65},{65,1},{129,193},{193,129... | collective-permute-start | bytes 98312 | tf_op jit(solution)/shard_map/ppermute | solution.py:618
  34.6 11.6 %collective-permute-start.8 = (f32[64,128]{1,0:T(8,128)S(1)}, f32[64,128]{1,0:T(8,128)S(1)}, u32[]{:S(2)}, u32[]{:S(2)}) collective-permute-start(f32[64,128]{1,0:T(8,128)S(1)} %get-tuple-element.89), channel_id=1, source_target_pairs={{1,2},{2,1},{3,4},{4,3},{5,6},{6,5},{7,8},{8,7},{9,10},{10,9},{11,... | collective-permute-start | bytes 98312 | tf_op jit(solution)/shard_map/ppermute | solution.py:618
  38.6 7.5 %collective-permute-start.9 = (f32[64,128]{1,0:T(8,128)S(1)}, f32[64,128]{1,0:T(8,128)S(1)}, u32[]{:S(2)}, u32[]{:S(2)}) collective-permute-start(f32[64,128]{1,0:T(8,128)S(1)} %get-tuple-element.90), channel_id=1, source_target_pairs={{0,1},{1,0},{2,3},{3,2},{4,5},{5,4},{6,7},{7,6},{8,9},{9,8},{10,11... | collective-permute-start | bytes 98312 | tf_op jit(solution)/shard_map/ppermute | solution.py:618
  38.6 7.5 %collective-permute-start.10 = (f32[64,128]{1,0:T(8,128)S(1)}, f32[64,128]{1,0:T(8,128)S(1)}, u32[]{:S(2)}, u32[]{:S(2)}) collective-permute-start(f32[64,128]{1,0:T(8,128)S(1)} %get-tuple-element.91), channel_id=1, source_target_pairs={{64,128},{128,64},{192,0},{0,192},{65,129},{129,65},{193,1},{1,193... | collective-permute-start | bytes 98312 | tf_op jit(solution)/shard_map/ppermute | solution.py:618
  40.5 5.6 %collective-permute-start.11 = (f32[64,128]{1,0:T(8,128)S(1)}, f32[64,128]{1,0:T(8,128)S(1)}, u32[]{:S(2)}, u32[]{:S(2)}) collective-permute-start(f32[64,128]{1,0:T(8,128)S(1)} %get-tuple-element.92), channel_id=1, source_target_pairs={{0,64},{64,0},{128,192},{192,128},{1,65},{65,1},{129,193},{193,129... | collective-permute-start | bytes 98312 | tf_op jit(solution)/shard_map/ppermute | solution.py:618
  47.5 11.6 %collective-permute-start.12 = (f32[64,128]{1,0:T(8,128)S(1)}, f32[64,128]{1,0:T(8,128)S(1)}, u32[]{:S(2)}, u32[]{:S(2)}) collective-permute-start(f32[64,128]{1,0:T(8,128)S(1)} %get-tuple-element.96), channel_id=1, source_target_pairs={{1,2},{2,1},{3,4},{4,3},{5,6},{6,5},{7,8},{8,7},{9,10},{10,9},{11,... | collective-permute-start | bytes 98312 | tf_op jit(solution)/shard_map/ppermute | solution.py:618
  51.5 7.5 %collective-permute-start.13 = (f32[64,128]{1,0:T(8,128)S(1)}, f32[64,128]{1,0:T(8,128)S(1)}, u32[]{:S(2)}, u32[]{:S(2)}) collective-permute-start(f32[64,128]{1,0:T(8,128)S(1)} %get-tuple-element.97), channel_id=1, source_target_pairs={{0,1},{1,0},{2,3},{3,2},{4,5},{5,4},{6,7},{7,6},{8,9},{9,8},{10,11... | collective-permute-start | bytes 98312 | tf_op jit(solution)/shard_map/ppermute | solution.py:618
  51.5 7.5 %collective-permute-start.14 = (f32[64,128]{1,0:T(8,128)S(1)}, f32[64,128]{1,0:T(8,128)S(1)}, u32[]{:S(2)}, u32[]{:S(2)}) collective-permute-start(f32[64,128]{1,0:T(8,128)S(1)} %get-tuple-element.98), channel_id=1, source_target_pairs={{64,128},{128,64},{192,0},{0,192},{65,129},{129,65},{193,1},{1,193... | collective-permute-start | bytes 98312 | tf_op jit(solution)/shard_map/ppermute | solution.py:618
  53.5 5.6 %collective-permute-start.15 = (f32[64,128]{1,0:T(8,128)S(1)}, f32[64,128]{1,0:T(8,128)S(1)}, u32[]{:S(2)}, u32[]{:S(2)}) collective-permute-start(f32[64,128]{1,0:T(8,128)S(1)} %get-tuple-element.99), channel_id=1, source_target_pairs={{0,64},{64,0},{128,192},{192,128},{1,65},{65,1},{129,193},{193,129... | collective-permute-start | bytes 98312 | tf_op jit(solution)/shard_map/ppermute | solution.py:618

commit v5 on v4

--- a/solution.py
+++ b/solution.py
@@ -310,13 +310,16 @@
     disp, veloc, jac, lam, mu, dens, conn, peer, grad, back = kept[:10]
     low = 2 * (FIRST - EDGE)
     mine, lower, upper = pl.ds(low, 2 * WIDE), pl.ds(0, low), pl.ds(low + 2 * WIDE, ELEM - low - 2 * WIDE)
+    start, stop = (FIRST - EDGE) * LANES, (FIRST + HALF + 1) * LANES
+    strip, above, below = pl.ds(start, stop - start), pl.ds(stop, NLOC - stop), pl.ds(0, start)
     steps = [
         [(conn_in.at[mine, :], conn.at[mine, :])],
-        [(disp_in, disp), (peer_in, peer)],
+        [(disp_in.at[:, strip], disp.at[:, strip]), (peer_in, peer)],
         [(jac_in.at[:, mine, :], jac.at[:, mine, :]), (grad_in, grad)]
         + [(x.at[mine, :], y.at[mine, :]) for x, y in ((lam_in, lam), (mu_in, mu), (dens_in, dens))]
         + [(back_in, back)],
-        [(veloc_in, veloc), (raw[10], kept[10])]
+        [(disp_in.at[:, part], disp.at[:, part]) for part in (above, below)]
+        + [(veloc_in, veloc), (raw[10], kept[10])]
         + [(jac_in.at[:, part, :], jac.at[:, part, :]) for part in (upper, lower)]
         + [
             (x.at[part, :], y.at[part, :])
@@ -677,7 +680,7 @@
         in_specs=[raw] * 11,
         out_shape=[shape(x.shape, x.dtype) for x in arguments] + edge_outs,
         out_specs=[vector] * 15,
-        scratch_shapes=edge_scratch + [pltpu.SemaphoreType.DMA((21,))],
+        scratch_shapes=edge_scratch + [pltpu.SemaphoreType.DMA((23,))],
         compiler_params=PARAMS,
         name="edge_dev",
     )(*[pltpu.with_memory_space_constraint(x, pltpu.HBM) for x in arguments])

time: 61.4 us -> 61.3 us (level)
  no operation moved by 1% of the time
where the time goes in v5:
time: 61.3 us; the launch traced here: 60.2 us
  starting transfers between devices  29.9 us (49%)
  waiting for transfers between devices  17.6 us (29%)
  Pallas kernels  11.8 us (19%)
  between operations  0.87 us (1%)
    ppermute x16, starting transfers between devices, swap_all(): lax.ppermute(sent, axis, swap_pairs(lax.axis_size(axis), colour))  29.9 us
    ppermute x16, waiting for transfers between devices, swap_all(): lax.ppermute(sent, axis, swap_pairs(lax.axis_size(axis), colour))  17.6 us
    pallas_call x3, Pallas kernels, body(): pl.pallas_call(functools.partial(middle_kernel, opening), in_specs=[vecto...  4.02 us
    pallas_call x1, Pallas kernels, body(): pl.pallas_call(inner_kernel, in_specs=[raw] + [vector] * 12, out_shape=[f...  2.52 us
    pallas_call x1, Pallas kernels, body(): pl.pallas_call(dev_edge_kernel, in_specs=[raw] * 11, out_shape=[shape(x.s...  2.38 us
  transfers between devices with their start and end apart: 16, of which 5 were waited for; matrix products, arithmetic and copies ran while one was open for 0% of the time, Pallas kernels for 7%

profile of v5, /device:TPU:0, one launch (start us, length us, event | category | flops | bytes accessed | tf_op | source)
XLA Modules:
  0.0 60.2 jit_solution(7772680337142355761)
XLA Ops:
  0.6 2.4 %edge_dev.1 = (f32[3,20480]{1,0:T(4,128)S(1)}, f32[3,20480]{1,0:T(4,128)S(1)}, f32[3,320,125]{2,1,0:T(8,128)S(1)}, f32[320,125]{1,0:T(8,128)S(1)}, f32[320,125]{...) custom-call(f32[3,20480]{1,0:T(4,128)} %refs_0_.1, ...), custom_call_target="tpu_custom_call" | custom-call | tf_op jit(solution)/shard_map/edge_dev/pallas_call | solution.py:678
  3.0 9.6 %collective-permute-start = (f32[80,128]{1,0:T(8,128)S(1)}, f32[80,128]{1,0:T(8,128)S(1)}, u32[]{:S(2)}, u32[]{:S(2)}) collective-permute-start(f32[80,128]{1,0:T(8,128)S(1)} %get-tuple-element.74), channel_id=1, source_target_pairs={{1,2},{2,1},{3,4},{4,3},{5,6},{6,5},{7,8},{8,7},{9,10},{10,9},{11,... | collective-permute-start | bytes 122888 | tf_op jit(solution)/shard_map/ppermute | solution.py:621
  12.7 0.0 collective-permute-start.1
  12.7 1.1 %edge_region.1 = (f32[4,40,128]{2,1,0:T(8,128)S(1)}, f32[4,8,128]{2,1,0:T(8,128)S(1)}, f32[80,128]{1,0:T(8,128)S(1)}, f32[80,128]{1,0:T(8,128)S(1)}) custom-call(f32[3,20480]{1,0:T(4,128)S(1)} %get-tuple-element.52.refs_0_.disp_in, f32[3,320,125]{2,1,0:T(8,128)S(1)} %get-tuple-element.55.refs_1_.jac_ref, f32[320,125]{1,0:T(8,128)S(1)} %get-tuple-element.56.refs_2_.lam_ref, ...), custom_call_target="tpu_custom_call" | custom-call | tf_op jit(solution)/shard_map/edge_region/pallas_call | solution.py:691
  13.7 2.0 %collective-permute-start.2 = (f32[80,128]{1,0:T(8,128)S(1)}, f32[80,128]{1,0:T(8,128)S(1)}, u32[]{:S(2)}, u32[]{:S(2)}) collective-permute-start(f32[80,128]{1,0:T(8,128)S(1)} %get-tuple-element.76), channel_id=1, source_target_pairs={{64,128},{128,64},{192,0},{0,192},{65,129},{129,65},{193,1},{1,193... | collective-permute-start | bytes 122888 | tf_op jit(solution)/shard_map/ppermute | solution.py:621
  15.8 0.1 collective-permute-start.3
  15.9 2.5 %inner.1 = (f32[3,160,128]{2,1,0:T(8,128)S(1)}, f32[4,80,128]{2,1,0:T(8,128)S(1)}, f32[5,80,128]{2,1,0:T(8,128)S(1)}, s32[2,80,128]{2,1,0:T(8,128)S(1)}, bf16[16...) custom-call(s32[80]{0:T(128)} %slots_in.1, ...), custom_call_target="tpu_custom_call" | custom-call | tf_op jit(solution)/shard_map/inner/pallas_call | solution.py:702
  18.4 0.0 collective-permute-done.1.got1
  18.4 1.6 %collective-permute-done.2.got2 = f32[80,128]{1,0:T(8,128)S(1)} collective-permute-done((f32[80,128]{1,0:T(8,128)S(1)}, f32[80,128]{1,0:T(8,128)S(1)}, u32[]{:S(2)}, u32[]{:S(2)}) %collective-permute-start.2) | collective-permute-done | bytes 40992 | tf_op jit(solution)/shard_map/ppermute | solution.py:621
  20.0 0.3 collective-permute-done.3.got3
  20.3 1.3 %middle.3 = (f32[3,160,128]{2,1,0:T(8,128)S(1)}, f32[3,160,128]{2,1,0:T(8,128)S(1)}, f32[3,160,128]{2,1,0:T(8,128)S(1)}, f32[160,128]{1,0:T(8,128)S(1)}, f32[64,...) custom-call(s32[2,80,128]{2,1,0:T(8,128)S(1)} %get-tuple-element.65.moved_ref.summed_ref., ...), custom_call_target="tpu_custom_call" | custom-call | tf_op jit(solution)/shard_map/middle/pallas_call | solution.py:743
  21.7 4.0 %collective-permute-start.4 = (f32[64,128]{1,0:T(8,128)S(1)}, f32[64,128]{1,0:T(8,128)S(1)}, u32[]{:S(2)}, u32[]{:S(2)}) collective-permute-start(f32[64,128]{1,0:T(8,128)S(1)} %get-tuple-element.82), channel_id=1, source_target_pairs={{1,2},{2,1},{3,4},{4,3},{5,6},{6,5},{7,8},{8,7},{9,10},{10,9},{11,... | collective-permute-start | bytes 98312 | tf_op jit(solution)/shard_map/ppermute | solution.py:621
  25.7 0.0 collective-permute-start.5
  25.7 1.9 %collective-permute-start.6 = (f32[64,128]{1,0:T(8,128)S(1)}, f32[64,128]{1,0:T(8,128)S(1)}, u32[]{:S(2)}, u32[]{:S(2)}) collective-permute-start(f32[64,128]{1,0:T(8,128)S(1)} %get-tuple-element.84), channel_id=1, source_target_pairs={{64,128},{128,64},{192,0},{0,192},{65,129},{129,65},{193,1},{1,193... | collective-permute-start | bytes 98312 | tf_op jit(solution)/shard_map/ppermute | solution.py:621
  27.6 0.1 collective-permute-start.7
  27.7 5.5 %collective-permute-done.4.got0 = f32[64,128]{1,0:T(8,128)S(1)} collective-permute-done((f32[64,128]{1,0:T(8,128)S(1)}, f32[64,128]{1,0:T(8,128)S(1)}, u32[]{:S(2)}, u32[]{:S(2)}) %collective-permute-start.4) | collective-permute-done | bytes 32800 | tf_op jit(solution)/shard_map/ppermute | solution.py:621
  33.2 0.0 collective-permute-done.5.got1
  33.2 0.0 collective-permute-done.6.got2
  33.2 1.3 %middle.4 = (f32[3,160,128]{2,1,0:T(8,128)S(1)}, f32[3,160,128]{2,1,0:T(8,128)S(1)}, f32[3,160,128]{2,1,0:T(8,128)S(1)}, f32[64,128]{1,0:T(8,128)S(1)}, f32[64,1...) custom-call(f32[3,160,128]{2,1,0:T(8,128)S(1)} %get-tuple-element.78.moved_ref, ...), custom_call_target="tpu_custom_call" | custom-call | tf_op jit(solution)/shard_map/middle/pallas_call | solution.py:743
  34.6 4.0 %collective-permute-start.8 = (f32[64,128]{1,0:T(8,128)S(1)}, f32[64,128]{1,0:T(8,128)S(1)}, u32[]{:S(2)}, u32[]{:S(2)}) collective-permute-start(f32[64,128]{1,0:T(8,128)S(1)} %get-tuple-element.89), channel_id=1, source_target_pairs={{1,2},{2,1},{3,4},{4,3},{5,6},{6,5},{7,8},{8,7},{9,10},{10,9},{11,... | collective-permute-start | bytes 98312 | tf_op jit(solution)/shard_map/ppermute | solution.py:621
  38.6 1.9 %collective-permute-start.10 = (f32[64,128]{1,0:T(8,128)S(1)}, f32[64,128]{1,0:T(8,128)S(1)}, u32[]{:S(2)}, u32[]{:S(2)}) collective-permute-start(f32[64,128]{1,0:T(8,128)S(1)} %get-tuple-element.91), channel_id=1, source_target_pairs={{64,128},{128,64},{192,0},{0,192},{65,129},{129,65},{193,1},{1,193... | collective-permute-start | bytes 98312 | tf_op jit(solution)/shard_map/ppermute | solution.py:621
  40.5 0.1 collective-permute-start.11
  40.6 5.5 %collective-permute-done.8.got0 = f32[64,128]{1,0:T(8,128)S(1)} collective-permute-done((f32[64,128]{1,0:T(8,128)S(1)}, f32[64,128]{1,0:T(8,128)S(1)}, u32[]{:S(2)}, u32[]{:S(2)}) %collective-permute-start.8) | collective-permute-done | bytes 32800 | tf_op jit(solution)/shard_map/ppermute | solution.py:621
  46.1 0.0 collective-permute-done.10.got2
  46.1 0.0 collective-permute-done.11.got3
  46.2 1.3 %middle.5 = (f32[3,160,128]{2,1,0:T(8,128)S(1)}, f32[3,160,128]{2,1,0:T(8,128)S(1)}, f32[3,160,128]{2,1,0:T(8,128)S(1)}, f32[64,128]{1,0:T(8,128)S(1)}, f32[64,1...) custom-call(f32[3,160,128]{2,1,0:T(8,128)S(1)} %get-tuple-element.86.moved_ref, ...), custom_call_target="tpu_custom_call" | custom-call | tf_op jit(solution)/shard_map/middle/pallas_call | solution.py:743
  47.5 4.1 %collective-permute-start.12 = (f32[64,128]{1,0:T(8,128)S(1)}, f32[64,128]{1,0:T(8,128)S(1)}, u32[]{:S(2)}, u32[]{:S(2)}) collective-permute-start(f32[64,128]{1,0:T(8,128)S(1)} %get-tuple-element.96), channel_id=1, source_target_pairs={{1,2},{2,1},{3,4},{4,3},{5,6},{6,5},{7,8},{8,7},{9,10},{10,9},{11,... | collective-permute-start | bytes 98312 | tf_op jit(solution)/shard_map/ppermute | solution.py:621
  51.6 1.9 %collective-permute-start.14 = (f32[64,128]{1,0:T(8,128)S(1)}, f32[64,128]{1,0:T(8,128)S(1)}, u32[]{:S(2)}, u32[]{:S(2)}) collective-permute-start(f32[64,128]{1,0:T(8,128)S(1)} %get-tuple-element.98), channel_id=1, source_target_pairs={{64,128},{128,64},{192,0},{0,192},{65,129},{129,65},{193,1},{1,193... | collective-permute-start | bytes 98312 | tf_op jit(solution)/shard_map/ppermute | solution.py:621
  53.5 0.1 collective-permute-start.15
  53.6 0.8 %last_inner.1 = (f32[3,20480]{1,0:T(4,128)}, f32[3,20480]{1,0:T(4,128)}) custom-call(f32[3,20480]{1,0:T(4,128)S(1)} %get-tuple-element.52.refs_0_.disp_in, f32[3,160,128]{2,1,0:T(8,128)S(1)} %get-tuple-element.93.moved_ref, f32[3,160,128]{2,1,0:T(8,128)S(1)} %get-tuple-element.94.veloc_ref, f32[3,160,128]{2,1,0:T(8,128)S(1)} %get-tuple-element.95.summed_ref, ...), custom_call_target="tpu_custom_call" | custom-call | tf_op jit(solution)/shard_map/last_inner/pallas_call | solution.py:777
  54.4 4.7 %collective-permute-done.12.got0 = f32[64,128]{1,0:T(8,128)S(1)} collective-permute-done((f32[64,128]{1,0:T(8,128)S(1)}, f32[64,128]{1,0:T(8,128)S(1)}, u32[]{:S(2)}, u32[]{:S(2)}) %collective-permute-start.12) | collective-permute-done | bytes 32800 | tf_op jit(solution)/shard_map/ppermute | solution.py:621
  59.1 1.0 %last_edge.1 = (f32[3,20480]{1,0:T(4,128)}, f32[3,20480]{1,0:T(4,128)}) custom-call(f32[3,20480]{1,0:T(4,128)S(1)} %get-tuple-element.52.refs_0_.disp_in, f32[3,160,128]{2,1,0:T(8,128)S(1)} %get-tuple-element.93.moved_ref, f32[3,160,128]{2,1,0:T(8,128)S(1)} %get-tuple-element.94.veloc_ref, ...), custom_call_target="tpu_custom_call", output_to_operand_aliasing={{0}: (10, {}), {1}: (11, {})} | custom-call | tf_op jit(solution)/shard_map/last_edge/pallas_call | solution.py:786
  (12 shorter events, 0.0 us)
Async XLA Ops:
  3.0 15.4 %collective-permute-start = (f32[80,128]{1,0:T(8,128)S(1)}, f32[80,128]{1,0:T(8,128)S(1)}, u32[]{:S(2)}, u32[]{:S(2)}) collective-permute-start(f32[80,128]{1,0:T(8,128)S(1)} %get-tuple-element.74), channel_id=1, source_target_pairs={{1,2},{2,1},{3,4},{4,3},{5,6},{6,5},{7,8},{8,7},{9,10},{10,9},{11,... | collective-permute-start | bytes 122888 | tf_op jit(solution)/shard_map/ppermute | solution.py:621
  12.7 5.8 %collective-permute-start.1 = (f32[80,128]{1,0:T(8,128)S(1)}, f32[80,128]{1,0:T(8,128)S(1)}, u32[]{:S(2)}, u32[]{:S(2)}) collective-permute-start(f32[80,128]{1,0:T(8,128)S(1)} %get-tuple-element.75), channel_id=1, source_target_pairs={{0,1},{1,0},{2,3},{3,2},{4,5},{5,4},{6,7},{7,6},{8,9},{9,8},{10,11... | collective-permute-start | bytes 122888 | tf_op jit(solution)/shard_map/ppermute | solution.py:621
  13.7 6.2 %collective-permute-start.2 = (f32[80,128]{1,0:T(8,128)S(1)}, f32[80,128]{1,0:T(8,128)S(1)}, u32[]{:S(2)}, u32[]{:S(2)}) collective-permute-start(f32[80,128]{1,0:T(8,128)S(1)} %get-tuple-element.76), channel_id=1, source_target_pairs={{64,128},{128,64},{192,0},{0,192},{65,129},{129,65},{193,1},{1,193... | collective-permute-start | bytes 122888 | tf_op jit(solution)/shard_map/ppermute | solution.py:621
  15.8 4.6 %collective-permute-start.3 = (f32[80,128]{1,0:T(8,128)S(1)}, f32[80,128]{1,0:T(8,128)S(1)}, u32[]{:S(2)}, u32[]{:S(2)}) collective-permute-start(f32[80,128]{1,0:T(8,128)S(1)} %get-tuple-element.77), channel_id=1, source_target_pairs={{0,64},{64,0},{128,192},{192,128},{1,65},{65,1},{129,193},{193,129... | collective-permute-start | bytes 122888 | tf_op jit(solution)/shard_map/ppermute | solution.py:621
  15.9 4.5 %copy-start = (bf16[384,384]{1,0:T(8,128)(2,1)S(1)}, bf16[384,384]{1,0:T(8,128)(2,1)}, u32[]{:S(2)}) copy-start(bf16[384,384]{1,0:T(8,128)(2,1)} %constant.4.clone.refs_8_.grad_ref) | copy-start | bytes 884740
  15.9 4.5 %copy-start.1 = (bf16[384,256]{1,0:T(8,128)(2,1)S(1)}, bf16[384,256]{1,0:T(8,128)(2,1)}, u32[]{:S(2)}) copy-start(bf16[384,256]{1,0:T(8,128)(2,1)} %constant.5.clone.refs_9_.back_ref) | copy-start | bytes 589828
  21.7 11.6 %collective-permute-start.4 = (f32[64,128]{1,0:T(8,128)S(1)}, f32[64,128]{1,0:T(8,128)S(1)}, u32[]{:S(2)}, u32[]{:S(2)}) collective-permute-start(f32[64,128]{1,0:T(8,128)S(1)} %get-tuple-element.82), channel_id=1, source_target_pairs={{1,2},{2,1},{3,4},{4,3},{5,6},{6,5},{7,8},{8,7},{9,10},{10,9},{11,... | collective-permute-start | bytes 98312 | tf_op jit(solution)/shard_map/ppermute | solution.py:621
  25.7 7.5 %collective-permute-start.5 = (f32[64,128]{1,0:T(8,128)S(1)}, f32[64,128]{1,0:T(8,128)S(1)}, u32[]{:S(2)}, u32[]{:S(2)}) collective-permute-start(f32[64,128]{1,0:T(8,128)S(1)} %get-tuple-element.83), channel_id=1, source_target_pairs={{0,1},{1,0},{2,3},{3,2},{4,5},{5,4},{6,7},{7,6},{8,9},{9,8},{10,11... | collective-permute-start | bytes 98312 | tf_op jit(solution)/shard_map/ppermute | solution.py:621
  25.7 7.5 %collective-permute-start.6 = (f32[64,128]{1,0:T(8,128)S(1)}, f32[64,128]{1,0:T(8,128)S(1)}, u32[]{:S(2)}, u32[]{:S(2)}) collective-permute-start(f32[64,128]{1,0:T(8,128)S(1)} %get-tuple-element.84), channel_id=1, source_target_pairs={{64,128},{128,64},{192,0},{0,192},{65,129},{129,65},{193,1},{1,193... | collective-permute-start | bytes 98312 | tf_op jit(solution)/shard_map/ppermute | solution.py:621
  27.6 5.6 %collective-permute-start.7 = (f32[64,128]{1,0:T(8,128)S(1)}, f32[64,128]{1,0:T(8,128)S(1)}, u32[]{:S(2)}, u32[]{:S(2)}) collective-permute-start(f32[64,128]{1,0:T(8,128)S(1)} %get-tuple-element.85), channel_id=1, source_target_pairs={{0,64},{64,0},{128,192},{192,128},{1,65},{65,1},{129,193},{193,129... | collective-permute-start | bytes 98312 | tf_op jit(solution)/shard_map/ppermute | solution.py:621
  34.6 11.6 %collective-permute-start.8 = (f32[64,128]{1,0:T(8,128)S(1)}, f32[64,128]{1,0:T(8,128)S(1)}, u32[]{:S(2)}, u32[]{:S(2)}) collective-permute-start(f32[64,128]{1,0:T(8,128)S(1)} %get-tuple-element.89), channel_id=1, source_target_pairs={{1,2},{2,1},{3,4},{4,3},{5,6},{6,5},{7,8},{8,7},{9,10},{10,9},{11,... | collective-permute-start | bytes 98312 | tf_op jit(solution)/shard_map/ppermute | solution.py:621
  38.6 7.5 %collective-permute-start.9 = (f32[64,128]{1,0:T(8,128)S(1)}, f32[64,128]{1,0:T(8,128)S(1)}, u32[]{:S(2)}, u32[]{:S(2)}) collective-permute-start(f32[64,128]{1,0:T(8,128)S(1)} %get-tuple-element.90), channel_id=1, source_target_pairs={{0,1},{1,0},{2,3},{3,2},{4,5},{5,4},{6,7},{7,6},{8,9},{9,8},{10,11... | collective-permute-start | bytes 98312 | tf_op jit(solution)/shard_map/ppermute | solution.py:621
  38.6 7.5 %collective-permute-start.10 = (f32[64,128]{1,0:T(8,128)S(1)}, f32[64,128]{1,0:T(8,128)S(1)}, u32[]{:S(2)}, u32[]{:S(2)}) collective-permute-start(f32[64,128]{1,0:T(8,128)S(1)} %get-tuple-element.91), channel_id=1, source_target_pairs={{64,128},{128,64},{192,0},{0,192},{65,129},{129,65},{193,1},{1,193... | collective-permute-start | bytes 98312 | tf_op jit(solution)/shard_map/ppermute | solution.py:621
  40.5 5.6 %collective-permute-start.11 = (f32[64,128]{1,0:T(8,128)S(1)}, f32[64,128]{1,0:T(8,128)S(1)}, u32[]{:S(2)}, u32[]{:S(2)}) collective-permute-start(f32[64,128]{1,0:T(8,128)S(1)} %get-tuple-element.92), channel_id=1, source_target_pairs={{0,64},{64,0},{128,192},{192,128},{1,65},{65,1},{129,193},{193,129... | collective-permute-start | bytes 98312 | tf_op jit(solution)/shard_map/ppermute | solution.py:621
  47.5 11.6 %collective-permute-start.12 = (f32[64,128]{1,0:T(8,128)S(1)}, f32[64,128]{1,0:T(8,128)S(1)}, u32[]{:S(2)}, u32[]{:S(2)}) collective-permute-start(f32[64,128]{1,0:T(8,128)S(1)} %get-tuple-element.96), channel_id=1, source_target_pairs={{1,2},{2,1},{3,4},{4,3},{5,6},{6,5},{7,8},{8,7},{9,10},{10,9},{11,... | collective-permute-start | bytes 98312 | tf_op jit(solution)/shard_map/ppermute | solution.py:621
  51.5 7.5 %collective-permute-start.13 = (f32[64,128]{1,0:T(8,128)S(1)}, f32[64,128]{1,0:T(8,128)S(1)}, u32[]{:S(2)}, u32[]{:S(2)}) collective-permute-start(f32[64,128]{1,0:T(8,128)S(1)} %get-tuple-element.97), channel_id=1, source_target_pairs={{0,1},{1,0},{2,3},{3,2},{4,5},{5,4},{6,7},{7,6},{8,9},{9,8},{10,11... | collective-permute-start | bytes 98312 | tf_op jit(solution)/shard_map/ppermute | solution.py:621
  51.6 7.5 %collective-permute-start.14 = (f32[64,128]{1,0:T(8,128)S(1)}, f32[64,128]{1,0:T(8,128)S(1)}, u32[]{:S(2)}, u32[]{:S(2)}) collective-permute-start(f32[64,128]{1,0:T(8,128)S(1)} %get-tuple-element.98), channel_id=1, source_target_pairs={{64,128},{128,64},{192,0},{0,192},{65,129},{129,65},{193,1},{1,193... | collective-permute-start | bytes 98312 | tf_op jit(solution)/shard_map/ppermute | solution.py:621
  53.5 5.6 %collective-permute-start.15 = (f32[64,128]{1,0:T(8,128)S(1)}, f32[64,128]{1,0:T(8,128)S(1)}, u32[]{:S(2)}, u32[]{:S(2)}) collective-permute-start(f32[64,128]{1,0:T(8,128)S(1)} %get-tuple-element.99), channel_id=1, source_target_pairs={{0,64},{64,0},{128,192},{192,128},{1,65},{65,1},{129,193},{193,129... | collective-permute-start | bytes 98312 | tf_op jit(solution)/shard_map/ppermute | solution.py:621
